TPU v7x, 32 devices: a whole 2x2x4 slice. The times are simulated.
32 devices in a mesh: gx: 8 (over y, x, core), gy: 4 (over z).
Axes of the slice: x: 2, y: 2, z: 4, core: 2. Of those that a mesh axis runs over, the one named last changes fastest.
Arguments:
- test_vectors: float32 [5, 64, 4096], P(None, None, ('gx', 'gy')), may hold values from -1100 to 1100
- face_jacobians: float32 [4, 5, 5], replicated, may hold values from -2.4 to 2.4
- wave_speed: float32 [4096], P(('gx', 'gy')), may hold values from 0.5 to 2
- viscosity: float32 [4096], P(('gx', 'gy')), may hold values from 0.05 to 0.5
- inverse_volume: float32 [4096], P(('gx', 'gy')), may hold values from 0.5 to 2
- connectivity: int32 [4, 4096], P(None, ('gx', 'gy')), may hold values from 0 to 192, as said below
- send_rows: int32 [4, 512], P(None, ('gx', 'gy')), may hold values from 0 to 127, as said below
- cell_count: int32 [32], P(('gx', 'gy')), may hold values from 64 to 128, as said below
Outputs:
- basis_vectors: float32 [5, 64, 4096], P(None, None, ('gx', 'gy'))
- factor: float32 [64, 64], replicated
Inputs may be any that keep to these rules, and one draw needn't show every extreme that they name: `cell_count`: one partition holds exactly 128 live cells and one exactly 64. `send_rows`: entries of partition p's lists name its owned cells below cell_count[p]; list 0 goes to the partition one row lower, 1 one row higher, 2 one column lower, 3 one column higher; every slot is sent, used or not. `connectivity`: an entry below 128 is a live owned cell; 128 + b * 16 + s is slot s of ghost block b, used only where that neighbouring partition exists; 192 is the far field (zero perturbation). How many slots of a block are used varies by partition and direction.
All inputs are finite; a program needn't handle non-finite values.
Results may differ from a plain program's by a relative error of at most 0.0001.
Values sent between devices are 32-bit elements; how exact they have to be, the bound alone decides.
No kernel may reach another device: no remote copies, remote signals or barrier semaphores. Data moves between devices by JAX's collectives and lax.ppermute only.
A program may use at most 64 MiB of HBM per device.

v0:
```python
import jax
import jax.numpy as jnp
from jax import lax
from jax.sharding import PartitionSpec as P

time_step = 0.4


def padded(cells, sides, width):
    for axis, dim in sides:
        count = lax.axis_size(axis)
        ends = count - 1
        head = lax.slice_in_dim(cells, 0, width, axis=dim)
        tail = lax.slice_in_dim(cells, cells.shape[dim] - width, cells.shape[dim], axis=dim)
        cells = jnp.concatenate(
            [
                lax.ppermute(tail, axis, [(i, (i + 1) % count) for i in range(ends)]),
                cells,
                lax.ppermute(head, axis, [((i + 1) % count, i) for i in range(ends)]),
            ],
            axis=dim,
        )
    return cells


def cell_operator(extended, connect, face_jacobians, wave_speed, viscosity, inverse_volume):
    owned_cells = connect.shape[1]
    own_state = extended[:, :, :owned_cells]
    advection = jnp.zeros(own_state.shape, jnp.float32)
    diffusion = jnp.zeros(own_state.shape, jnp.float32)
    for face_index in range(4):
        neighbor = jnp.take(extended, connect[face_index], axis=2)
        advection = advection + jnp.einsum(
            "ij,jvc->ivc", face_jacobians[face_index], neighbor, precision=lax.Precision.HIGHEST
        )
        diffusion = diffusion + neighbor
    return inverse_volume * (
        -0.5 * wave_speed * advection + viscosity * (diffusion - 4.0 * own_state)
    )


def ghost_blocks(current, send_rows):
    outgoing = jnp.moveaxis(jnp.take(current, send_rows, axis=2), 2, 0)
    along_rows = padded(outgoing[0:2], (("gx", 0),), 1)
    along_cols = padded(outgoing[2:4], (("gy", 0),), 1)
    return [along_rows[0], along_rows[3], along_cols[0], along_cols[3]]


def shards(
    test_vectors,
    face_jacobians,
    wave_speed,
    viscosity,
    inverse_volume,
    connectivity,
    send_rows,
    cell_count,
):
    fields, vectors, owned_cells = test_vectors.shape
    speed_cells = wave_speed[None, None, :]
    visc_cells = viscosity[None, None, :]
    volume_cells = inverse_volume[None, None, :]
    zero_block = jnp.zeros((fields, vectors, 1), jnp.float32)

    def operate(state_now):
        incoming = ghost_blocks(state_now, send_rows)
        extended = jnp.concatenate([state_now] + incoming + [zero_block], axis=2)
        return cell_operator(
            extended, connectivity, face_jacobians, speed_cells, visc_cells, volume_cells
        )

    section_one = operate(test_vectors)
    section_two = operate(test_vectors + 0.5 * time_step * section_one)
    section_three = operate(test_vectors + 0.5 * time_step * section_two)
    section_four = operate(test_vectors + time_step * section_three)
    advanced = test_vectors + time_step / 6.0 * (
        section_one + 2.0 * section_two + 2.0 * section_three + section_four
    )
    live_mask = (jnp.arange(owned_cells, dtype=jnp.int32) < cell_count[0]).astype(jnp.float32)
    advanced = advanced * live_mask[None, None, :]
    gram_local = jnp.einsum("fic,fjc->ij", advanced, advanced, precision=lax.Precision.HIGHEST)
    gram_whole = lax.psum(lax.psum(gram_local, "gy"), "gx")
    total_cells = owned_cells * lax.axis_size("gx") * lax.axis_size("gy")
    gram_whole = gram_whole / float(fields * total_cells)
    lower_factor = jnp.linalg.cholesky(gram_whole)
    inverse_lower = jax.scipy.linalg.solve_triangular(
        lower_factor, jnp.eye(vectors, dtype=jnp.float32), lower=True
    )
    basis_out = jnp.einsum("ij,fjc->fic", inverse_lower, advanced, precision=lax.Precision.HIGHEST)
    return (basis_out, lower_factor.T)


def solution(mesh):
    placed = (
        P(None, None, ("gx", "gy")),
        P(),
        P(("gx", "gy")),
        P(("gx", "gy")),
        P(("gx", "gy")),
        P(None, ("gx", "gy")),
        P(None, ("gx", "gy")),
        P(("gx", "gy")),
    )
    return jax.shard_map(
        shards,
        mesh=mesh,
        in_specs=placed,
        out_specs=(P(None, None, ("gx", "gy")), P()),
        check_vma=False,
    )
```

profile of v0, /device:TPU:0, one launch (start us, length us, event | category | flops | bytes accessed | tf_op | source)
XLA Modules:
  0.0 170.4 jit_solution(6013791741072201686)
XLA Ops:
  3.5 2.4 %collective-permute-start = (f32[1,5,64,16]{2,1,3,0:T(8,128)S(1)}, f32[1,5,64,16]{2,1,3,0:T(8,128)S(1)}, u32[]{:S(2)}, u32[]{:S(2)}) collective-permute-start(f32[1,5,64,16]{2,1,3,0:T(8,128)S(1)} %get-tuple-element.35), channel_id=1, source_target_pairs={{0,4},{4,8},{8,12},{12,16},{16,20},{20,24},{24,28},{1,5},{5,9},{9,... | collective-permute-start | bytes 61448 | tf_op jit(solution)/shard_map/ppermute | solution.py:17
  5.8 1.3 collective-permute-start.1
  7.1 4.3 %collective-permute-start.2 = (f32[1,5,64,16]{2,1,3,0:T(8,128)S(1)}, f32[1,5,64,16]{2,1,3,0:T(8,128)S(1)}, u32[]{:S(2)}, u32[]{:S(2)}) collective-permute-start(f32[1,5,64,16]{2,1,3,0:T(8,128)S(1)} %get-tuple-element.33), channel_id=1, source_target_pairs={{0,1},{1,2},{2,3},{4,5},{5,6},{6,7},{8,9},{9,10},{10,11},{12,13},{... | collective-permute-start | bytes 61448 | tf_op jit(solution)/shard_map/ppermute | solution.py:17
  14.2 3.4 %collective-permute-done.3 = f32[1,5,64,16]{2,1,3,0:T(8,128)S(1)} collective-permute-done((f32[1,5,64,16]{2,1,3,0:T(8,128)S(1)}, f32[1,5,64,16]{2,1,3,0:T(8,128)S(1)}, u32[]{:S(2)}, u32[]{:S(2)}) %collective-permute-start.3) | collective-permute-done | bytes 20512 | tf_op jit(solution)/shard_map/ppermute | solution.py:19
  25.5 2.9 %collective-permute-start.4 = (f32[1,5,64,16]{3,1,2,0:T(8,128)S(1)}, f32[1,5,64,16]{3,1,2,0:T(8,128)S(1)}, u32[]{:S(2)}, u32[]{:S(2)}) collective-permute-start(f32[1,5,64,16]{3,1,2,0:T(8,128)S(1)} %get-tuple-element.31), channel_id=1, source_target_pairs={{0,4},{4,8},{8,12},{12,16},{16,20},{20,24},{24,28},{1,5},{5,9},{9,... | collective-permute-start | bytes 61448 | tf_op jit(solution)/shard_map/ppermute | solution.py:17
  29.7 3.5 %collective-permute-start.6 = (f32[1,5,64,16]{3,1,2,0:T(8,128)S(1)}, f32[1,5,64,16]{3,1,2,0:T(8,128)S(1)}, u32[]{:S(2)}, u32[]{:S(2)}) collective-permute-start(f32[1,5,64,16]{3,1,2,0:T(8,128)S(1)} %get-tuple-element.29), channel_id=1, source_target_pairs={{0,1},{1,2},{2,3},{4,5},{5,6},{6,7},{8,9},{9,10},{10,11},{12,13},{... | collective-permute-start | bytes 61448 | tf_op jit(solution)/shard_map/ppermute | solution.py:17
  34.5 2.5 %collective-permute-done.6 = f32[1,5,64,16]{3,1,2,0:T(8,128)S(1)} collective-permute-done((f32[1,5,64,16]{3,1,2,0:T(8,128)S(1)}, f32[1,5,64,16]{3,1,2,0:T(8,128)S(1)}, u32[]{:S(2)}, u32[]{:S(2)}) %collective-permute-start.6) | collective-permute-done | bytes 20512 | tf_op jit(solution)/shard_map/ppermute | solution.py:17
  37.0 4.6 %collective-permute-done.7 = f32[1,5,64,16]{3,1,2,0:T(8,128)S(1)} collective-permute-done((f32[1,5,64,16]{3,1,2,0:T(8,128)S(1)}, f32[1,5,64,16]{3,1,2,0:T(8,128)S(1)}, u32[]{:S(2)}, u32[]{:S(2)}) %collective-permute-start.7) | collective-permute-done | bytes 20512 | tf_op jit(solution)/shard_map/ppermute | solution.py:19
  42.5 1.6 gather_fusion.9
  44.1 1.6 gather_fusion.8
  45.6 1.6 gather_fusion.7
  48.0 1.3 copy.171
  54.1 4.3 %collective-permute-start.8 = (f32[1,5,64,16]{3,1,2,0:T(8,128)S(1)}, f32[1,5,64,16]{3,1,2,0:T(8,128)S(1)}, u32[]{:S(2)}, u32[]{:S(2)}) collective-permute-start(f32[1,5,64,16]{3,1,2,0:T(8,128)S(1)} %get-tuple-element.27), channel_id=1, source_target_pairs={{0,4},{4,8},{8,12},{12,16},{16,20},{20,24},{24,28},{1,5},{5,9},{9,... | collective-permute-start | bytes 61448 | tf_op jit(solution)/shard_map/ppermute | solution.py:17
  59.8 3.5 %collective-permute-start.10 = (f32[1,5,64,16]{3,1,2,0:T(8,128)S(1)}, f32[1,5,64,16]{3,1,2,0:T(8,128)S(1)}, u32[]{:S(2)}, u32[]{:S(2)}) collective-permute-start(f32[1,5,64,16]{3,1,2,0:T(8,128)S(1)} %get-tuple-element.25), channel_id=1, source_target_pairs={{0,1},{1,2},{2,3},{4,5},{5,6},{6,7},{8,9},{9,10},{10,11},{12,13},{... | collective-permute-start | bytes 61448 | tf_op jit(solution)/shard_map/ppermute | solution.py:17
  63.2 1.5 collective-permute-start.11
  67.1 4.4 %collective-permute-done.11 = f32[1,5,64,16]{3,1,2,0:T(8,128)S(1)} collective-permute-done((f32[1,5,64,16]{3,1,2,0:T(8,128)S(1)}, f32[1,5,64,16]{3,1,2,0:T(8,128)S(1)}, u32[]{:S(2)}, u32[]{:S(2)}) %collective-permute-start.11) | collective-permute-done | bytes 20512 | tf_op jit(solution)/shard_map/ppermute | solution.py:19
  72.3 1.6 gather_fusion.14
  73.9 1.6 gather_fusion.13
  75.5 1.6 gather_fusion.12
  77.8 1.3 copy.183
  84.0 6.3 %collective-permute-start.12 = (f32[1,5,64,16]{3,1,2,0:T(8,128)S(1)}, f32[1,5,64,16]{3,1,2,0:T(8,128)S(1)}, u32[]{:S(2)}, u32[]{:S(2)}) collective-permute-start(f32[1,5,64,16]{3,1,2,0:T(8,128)S(1)} %get-tuple-element.23), channel_id=1, source_target_pairs={{0,4},{4,8},{8,12},{12,16},{16,20},{20,24},{24,28},{1,5},{5,9},{9,... | collective-permute-start | bytes 61448 | tf_op jit(solution)/shard_map/ppermute | solution.py:17
  91.6 2.2 %collective-permute-start.14 = (f32[1,5,64,16]{3,1,2,0:T(8,128)S(1)}, f32[1,5,64,16]{3,1,2,0:T(8,128)S(1)}, u32[]{:S(2)}, u32[]{:S(2)}) collective-permute-start(f32[1,5,64,16]{3,1,2,0:T(8,128)S(1)} %get-tuple-element.21), channel_id=1, source_target_pairs={{0,1},{1,2},{2,3},{4,5},{5,6},{6,7},{8,9},{9,10},{10,11},{12,13},{... | collective-permute-start | bytes 61448 | tf_op jit(solution)/shard_map/ppermute | solution.py:17
  93.8 1.3 collective-permute-start.15
  95.1 2.2 %collective-permute-done.13 = f32[1,5,64,16]{3,1,2,0:T(8,128)S(1)} collective-permute-done((f32[1,5,64,16]{3,1,2,0:T(8,128)S(1)}, f32[1,5,64,16]{3,1,2,0:T(8,128)S(1)}, u32[]{:S(2)}, u32[]{:S(2)}) %collective-permute-start.13) | collective-permute-done | bytes 20512 | tf_op jit(solution)/shard_map/ppermute | solution.py:19
  97.7 4.4 %collective-permute-done.15 = f32[1,5,64,16]{3,1,2,0:T(8,128)S(1)} collective-permute-done((f32[1,5,64,16]{3,1,2,0:T(8,128)S(1)}, f32[1,5,64,16]{3,1,2,0:T(8,128)S(1)}, u32[]{:S(2)}, u32[]{:S(2)}) %collective-permute-start.15) | collective-permute-done | bytes 20512 | tf_op jit(solution)/shard_map/ppermute | solution.py:19
  102.8 1.4 concatenate.15
  104.6 1.6 gather_fusion.16
  107.7 1.6 gather_fusion.19
  114.3 15.9 %psum.14 = f32[64,64]{0,1:T(8,128)S(1)} all-reduce(f32[64,64]{0,1:T(8,128)S(1)} %convolution_bitcast_fusion.2), channel_id=1, replica_groups=mesh['gx'=8,'gy'=4] {'gy'}, use_global_device_ids=true, to_apply=%region_0.3 | all-reduce | flops 4096 | bytes 32768 | tf_op jit(solution)/shard_map/psum | solution.py:82
  130.2 26.1 %psum.15 = f32[64,64]{0,1:T(8,128)S(1)} all-reduce(f32[64,64]{0,1:T(8,128)S(1)} %psum.14), channel_id=1, replica_groups=mesh['gx'=8,'gy'=4] {'gx'}, use_global_device_ids=true, to_apply=%region_1.4 | all-reduce | flops 4096 | bytes 32768 | tf_op jit(solution)/shard_map/psum | solution.py:82
  156.4 5.8 %cholesky.17 = f32[64,64]{1,0:T(8,128)S(1)} custom-call(f32[64,64]{1,0:T(8,128)S(1)} %fusion.99), custom_call_target="Cholesky" | custom-call | tf_op jit(solution)/shard_map/jit(cholesky)/cholesky | solution.py:85
  163.6 4.9 %custom-call.7 = f32[1,64,64]{1,2,0:T(8,128)S(1)} custom-call(f32[1,64,64]{2,1,0:T(8,128)S(1)} %get-tuple-element.37), custom_call_target="InvertDiagBlocksLowerTriangular" | custom-call | tf_op jit(solution)/shard_map/jit(_solve_triangular)/triangular_solve | solution.py:86
  (124 shorter events, 44.0 us)
Async XLA Ops:
  0.6 0.8 copy-start.5
  3.5 10.7 %collective-permute-start = (f32[1,5,64,16]{2,1,3,0:T(8,128)S(1)}, f32[1,5,64,16]{2,1,3,0:T(8,128)S(1)}, u32[]{:S(2)}, u32[]{:S(2)}) collective-permute-start(f32[1,5,64,16]{2,1,3,0:T(8,128)S(1)} %get-tuple-element.35), channel_id=1, source_target_pairs={{0,4},{4,8},{8,12},{12,16},{16,20},{20,24},{24,28},{1,5},{5,9},{9,... | collective-permute-start | bytes 61448 | tf_op jit(solution)/shard_map/ppermute | solution.py:17
  5.8 8.3 %collective-permute-start.1 = (f32[1,5,64,16]{2,1,3,0:T(8,128)S(1)}, f32[1,5,64,16]{2,1,3,0:T(8,128)S(1)}, u32[]{:S(2)}, u32[]{:S(2)}) collective-permute-start(f32[1,5,64,16]{2,1,3,0:T(8,128)S(1)} %get-tuple-element.34), channel_id=1, source_target_pairs={{4,0},{8,4},{12,8},{16,12},{20,16},{24,20},{28,24},{5,1},{9,5},{13... | collective-permute-start | bytes 61448 | tf_op jit(solution)/shard_map/ppermute | solution.py:19
  7.1 7.1 %collective-permute-start.2 = (f32[1,5,64,16]{2,1,3,0:T(8,128)S(1)}, f32[1,5,64,16]{2,1,3,0:T(8,128)S(1)}, u32[]{:S(2)}, u32[]{:S(2)}) collective-permute-start(f32[1,5,64,16]{2,1,3,0:T(8,128)S(1)} %get-tuple-element.33), channel_id=1, source_target_pairs={{0,1},{1,2},{2,3},{4,5},{5,6},{6,7},{8,9},{9,10},{10,11},{12,13},{... | collective-permute-start | bytes 61448 | tf_op jit(solution)/shard_map/ppermute | solution.py:17
  11.4 1.4 copy-start.8
  11.5 6.2 %collective-permute-start.3 = (f32[1,5,64,16]{2,1,3,0:T(8,128)S(1)}, f32[1,5,64,16]{2,1,3,0:T(8,128)S(1)}, u32[]{:S(2)}, u32[]{:S(2)}) collective-permute-start(f32[1,5,64,16]{2,1,3,0:T(8,128)S(1)} %get-tuple-element.32), channel_id=1, source_target_pairs={{1,0},{2,1},{3,2},{5,4},{6,5},{7,6},{9,8},{10,9},{11,10},{13,12},{... | collective-permute-start | bytes 61448 | tf_op jit(solution)/shard_map/ppermute | solution.py:19
  12.8 0.7 copy-start.4
  13.5 0.7 copy-start.9
  22.4 0.9 copy-start
  22.8 0.7 copy-start.6
  22.8 0.7 copy-start.7
  25.5 9.0 %collective-permute-start.4 = (f32[1,5,64,16]{3,1,2,0:T(8,128)S(1)}, f32[1,5,64,16]{3,1,2,0:T(8,128)S(1)}, u32[]{:S(2)}, u32[]{:S(2)}) collective-permute-start(f32[1,5,64,16]{3,1,2,0:T(8,128)S(1)} %get-tuple-element.31), channel_id=1, source_target_pairs={{0,4},{4,8},{8,12},{12,16},{16,20},{20,24},{24,28},{1,5},{5,9},{9,... | collective-permute-start | bytes 61448 | tf_op jit(solution)/shard_map/ppermute | solution.py:17
  28.4 6.1 %collective-permute-start.5 = (f32[1,5,64,16]{3,1,2,0:T(8,128)S(1)}, f32[1,5,64,16]{3,1,2,0:T(8,128)S(1)}, u32[]{:S(2)}, u32[]{:S(2)}) collective-permute-start(f32[1,5,64,16]{3,1,2,0:T(8,128)S(1)} %get-tuple-element.30), channel_id=1, source_target_pairs={{4,0},{8,4},{12,8},{16,12},{20,16},{24,20},{28,24},{5,1},{9,5},{13... | collective-permute-start | bytes 61448 | tf_op jit(solution)/shard_map/ppermute | solution.py:19
  29.7 7.4 %collective-permute-start.6 = (f32[1,5,64,16]{3,1,2,0:T(8,128)S(1)}, f32[1,5,64,16]{3,1,2,0:T(8,128)S(1)}, u32[]{:S(2)}, u32[]{:S(2)}) collective-permute-start(f32[1,5,64,16]{3,1,2,0:T(8,128)S(1)} %get-tuple-element.29), channel_id=1, source_target_pairs={{0,1},{1,2},{2,3},{4,5},{5,6},{6,7},{8,9},{9,10},{10,11},{12,13},{... | collective-permute-start | bytes 61448 | tf_op jit(solution)/shard_map/ppermute | solution.py:17
  33.2 8.5 %collective-permute-start.7 = (f32[1,5,64,16]{3,1,2,0:T(8,128)S(1)}, f32[1,5,64,16]{3,1,2,0:T(8,128)S(1)}, u32[]{:S(2)}, u32[]{:S(2)}) collective-permute-start(f32[1,5,64,16]{3,1,2,0:T(8,128)S(1)} %get-tuple-element.28), channel_id=1, source_target_pairs={{1,0},{2,1},{3,2},{5,4},{6,5},{7,6},{9,8},{10,9},{11,10},{13,12},{... | collective-permute-start | bytes 61448 | tf_op jit(solution)/shard_map/ppermute | solution.py:19
  48.0 1.3 copy-start.1
  54.1 11.3 %collective-permute-start.8 = (f32[1,5,64,16]{3,1,2,0:T(8,128)S(1)}, f32[1,5,64,16]{3,1,2,0:T(8,128)S(1)}, u32[]{:S(2)}, u32[]{:S(2)}) collective-permute-start(f32[1,5,64,16]{3,1,2,0:T(8,128)S(1)} %get-tuple-element.27), channel_id=1, source_target_pairs={{0,4},{4,8},{8,12},{12,16},{16,20},{20,24},{24,28},{1,5},{5,9},{9,... | collective-permute-start | bytes 61448 | tf_op jit(solution)/shard_map/ppermute | solution.py:17
  58.5 8.1 %collective-permute-start.9 = (f32[1,5,64,16]{3,1,2,0:T(8,128)S(1)}, f32[1,5,64,16]{3,1,2,0:T(8,128)S(1)}, u32[]{:S(2)}, u32[]{:S(2)}) collective-permute-start(f32[1,5,64,16]{3,1,2,0:T(8,128)S(1)} %get-tuple-element.26), channel_id=1, source_target_pairs={{4,0},{8,4},{12,8},{16,12},{20,16},{24,20},{28,24},{5,1},{9,5},{13... | collective-permute-start | bytes 61448 | tf_op jit(solution)/shard_map/ppermute | solution.py:19
  59.8 7.4 %collective-permute-start.10 = (f32[1,5,64,16]{3,1,2,0:T(8,128)S(1)}, f32[1,5,64,16]{3,1,2,0:T(8,128)S(1)}, u32[]{:S(2)}, u32[]{:S(2)}) collective-permute-start(f32[1,5,64,16]{3,1,2,0:T(8,128)S(1)} %get-tuple-element.25), channel_id=1, source_target_pairs={{0,1},{1,2},{2,3},{4,5},{5,6},{6,7},{8,9},{9,10},{10,11},{12,13},{... | collective-permute-start | bytes 61448 | tf_op jit(solution)/shard_map/ppermute | solution.py:17
  63.2 8.3 %collective-permute-start.11 = (f32[1,5,64,16]{3,1,2,0:T(8,128)S(1)}, f32[1,5,64,16]{3,1,2,0:T(8,128)S(1)}, u32[]{:S(2)}, u32[]{:S(2)}) collective-permute-start(f32[1,5,64,16]{3,1,2,0:T(8,128)S(1)} %get-tuple-element.24), channel_id=1, source_target_pairs={{1,0},{2,1},{3,2},{5,4},{6,5},{7,6},{9,8},{10,9},{11,10},{13,12},{... | collective-permute-start | bytes 61448 | tf_op jit(solution)/shard_map/ppermute | solution.py:19
  77.8 1.3 copy-start.2
  84.0 11.2 %collective-permute-start.12 = (f32[1,5,64,16]{3,1,2,0:T(8,128)S(1)}, f32[1,5,64,16]{3,1,2,0:T(8,128)S(1)}, u32[]{:S(2)}, u32[]{:S(2)}) collective-permute-start(f32[1,5,64,16]{3,1,2,0:T(8,128)S(1)} %get-tuple-element.23), channel_id=1, source_target_pairs={{0,4},{4,8},{8,12},{12,16},{16,20},{20,24},{24,28},{1,5},{5,9},{9,... | collective-permute-start | bytes 61448 | tf_op jit(solution)/shard_map/ppermute | solution.py:17
  90.3 7.0 %collective-permute-start.13 = (f32[1,5,64,16]{3,1,2,0:T(8,128)S(1)}, f32[1,5,64,16]{3,1,2,0:T(8,128)S(1)}, u32[]{:S(2)}, u32[]{:S(2)}) collective-permute-start(f32[1,5,64,16]{3,1,2,0:T(8,128)S(1)} %get-tuple-element.22), channel_id=1, source_target_pairs={{4,0},{8,4},{12,8},{16,12},{20,16},{24,20},{28,24},{5,1},{9,5},{13... | collective-permute-start | bytes 61448 | tf_op jit(solution)/shard_map/ppermute | solution.py:19
  91.6 6.1 %collective-permute-start.14 = (f32[1,5,64,16]{3,1,2,0:T(8,128)S(1)}, f32[1,5,64,16]{3,1,2,0:T(8,128)S(1)}, u32[]{:S(2)}, u32[]{:S(2)}) collective-permute-start(f32[1,5,64,16]{3,1,2,0:T(8,128)S(1)} %get-tuple-element.21), channel_id=1, source_target_pairs={{0,1},{1,2},{2,3},{4,5},{5,6},{6,7},{8,9},{9,10},{10,11},{12,13},{... | collective-permute-start | bytes 61448 | tf_op jit(solution)/shard_map/ppermute | solution.py:17
  93.8 8.3 %collective-permute-start.15 = (f32[1,5,64,16]{3,1,2,0:T(8,128)S(1)}, f32[1,5,64,16]{3,1,2,0:T(8,128)S(1)}, u32[]{:S(2)}, u32[]{:S(2)}) collective-permute-start(f32[1,5,64,16]{3,1,2,0:T(8,128)S(1)} %get-tuple-element.20), channel_id=1, source_target_pairs={{1,0},{2,1},{3,2},{5,4},{6,5},{7,6},{9,8},{10,9},{11,10},{13,12},{... | collective-permute-start | bytes 61448 | tf_op jit(solution)/shard_map/ppermute | solution.py:19
  102.1 0.7 copy-start.3
where the time goes:
time: 171 us; the launch traced here: 170 us
  blocking collectives  42 us (25%)
  local copies, waits for them, and re-layouts  41.4 us (24%)
  starting transfers between devices  39.9 us (23%)
  waiting for transfers between devices  23.6 us (14%)
  other arithmetic  13.3 us (8%)
  matrix products  7.86 us (5%)
  between operations  2.17 us (1%)
    psum x2, blocking collectives, shards(): gram_whole = lax.psum(lax.psum(gram_local, 'gy'), 'gx')  42 us
    ppermute x8, starting transfers between devices, padded(): lax.ppermute(tail, axis, [(i, (i + 1) % count) for i in range(ends)])  29.4 us
    gather x32, local copies, waits for them, and re-layouts, cell_operator(): neighbor = jnp.take(extended, connect[face_index], axis=2)  28.4 us
    ppermute x8, waiting for transfers between devices, padded(): lax.ppermute(head, axis, [((i + 1) % count, i) for i in range(ends)])  20.2 us
    ppermute x8, starting transfers between devices, padded(): lax.ppermute(head, axis, [((i + 1) % count, i) for i in range(ends)])  10.5 us
    another operation x3, other arithmetic, shards(): lower_factor = jnp.linalg.cholesky(gram_whole)  6.52 us
    dot_general x16, matrix products, cell_operator(): jnp.einsum('ij,jvc->ivc', face_jacobians[face_index], neighbor, precision...  6.35 us
    another operation x1, other arithmetic, shards(): jax.scipy.linalg.solve_triangular(lower_factor, jnp.eye(vectors, dtype=jn...  4.9 us
  transfers between devices with their start and end apart: 16, of which 9 were waited for; matrix products, arithmetic and copies ran while one was open for 0% of the time, Pallas kernels for 0%

commit v1 on v0

v1 whole, which is shorter than its diff:
```python
import functools

import jax
import jax.numpy as jnp
from jax import lax
from jax.experimental import pallas as pl
from jax.experimental.pallas import tpu as pltpu
from jax.sharding import PartitionSpec as P

time_step = 0.4
lanes = 128
sublanes = 8
HIGHEST = lax.Precision.HIGHEST


def partner(index, count, odd):
    other = index + 1 if index % 2 == odd else index - 1
    return other if 0 <= other < count else None


def matchings(rows, cols):
    row_even, row_odd, col_even, col_odd = [], [], [], []
    for i in range(rows):
        for j in range(cols):
            here = i * cols + j
            row_even.append((here, (i ^ 1) * cols + j))
            col_even.append((here, i * cols + (j ^ 1)))
            up = partner(i, rows, 1)
            row_odd.append((here, (rows - 1 - i if up is None else up) * cols + j))
            across = partner(j, cols, 1)
            col_odd.append((here, (i ^ 1) * cols + j if across is None else i * cols + across))
    return row_even, row_odd, col_even, col_odd


def lane_take(values, index):
    return jnp.take_along_axis(values, index, axis=1, mode="promise_in_bounds")


def swapped(lists, row_swap, col_swap):
    first, second, third, fourth = lists
    return [
        jnp.where(row_swap, second, first),
        jnp.where(row_swap, first, second),
        jnp.where(col_swap, fourth, third),
        jnp.where(col_swap, third, fourth),
    ]


def lane_ids():
    return lax.broadcasted_iota(jnp.int32, (sublanes, lanes), 1)


def send_index(send_ref, flags_ref, slots):
    lane = lane_ids()
    index = jnp.zeros((sublanes, lanes), jnp.int32)
    for b in range(4):
        swap = flags_ref[b // 2]
        source = jnp.bitwise_xor(b, swap)
        for s in range(slots):
            index = jnp.where(lane == b * slots + s, send_ref[source, s], index)
    return index


def pack(states, base_index, out_refs, groups, slots):
    group = lane_ids() // slots
    fields = len(states[0])
    packed = [[None] * fields for _ in range(4)]
    for m in range(groups):
        index = pltpu.roll(base_index, m * slots, 1) if m else base_index
        for f in range(fields):
            taken = lane_take(states[m][f], index)
            for b in range(4):
                before = packed[b][f]
                packed[b][f] = (
                    taken
                    if before is None
                    else jnp.where(group == (m + b) % groups, taken, before)
                )
    for b in range(4):
        for f in range(fields):
            out_refs[b][f] = packed[b][f]


def pack_kernel(flags_ref, send_ref, q_ref, *out_refs):
    fields, vectors, _ = q_ref.shape
    slots = send_ref.shape[1]
    groups = lanes // slots
    base_index = send_index(send_ref, flags_ref, slots)
    states = [
        [q_ref[f, pl.ds(m * sublanes, sublanes), :] for f in range(fields)] for m in range(groups)
    ]
    pack(states, base_index, out_refs, groups, slots)


def stage_kernel(
    stage,
    flags_ref,
    send_ref,
    jac_ref,
    count_ref,
    conn_ref,
    speed_ref,
    visc_ref,
    volume_ref,
    q_ref,
    *refs,
):
    refs = list(refs)
    state_ref = q_ref if stage == 0 else refs.pop(0)
    acc_ref = q_ref if stage == 0 else refs.pop(0)
    recv_refs = [refs.pop(0) for _ in range(4)]
    fields, vectors, cells = q_ref.shape
    slots = send_ref.shape[1]
    groups = lanes // slots
    lane = lane_ids()
    group = lane // slots
    shape = (sublanes, lanes)

    weight = jnp.broadcast_to(volume_ref[...], shape)
    advect = -0.5 * jnp.broadcast_to(speed_ref[...], shape) * weight
    diffuse = jnp.broadcast_to(visc_ref[...], shape) * weight
    row_swap = flags_ref[0] * slots
    col_swap = flags_ref[1] * slots
    own_index, ghost_index, is_ghost = [], [], []
    for face in range(4):
        entry = jnp.broadcast_to(conn_ref[pl.ds(face, 1), :], shape)
        ghost = entry - cells
        ghost = jnp.where(
            ghost < 2 * slots,
            jnp.bitwise_xor(ghost, row_swap),
            jnp.where(ghost < 4 * slots, jnp.bitwise_xor(ghost, col_swap), ghost),
        )
        own_index.append(jnp.bitwise_and(entry, lanes - 1))
        ghost_index.append(ghost)
        is_ghost.append(entry >= cells)

    last = stage == 3
    kept_coef = time_step / 6.0 if stage in (0, 3) else time_step / 3.0
    next_coef = (0.5 * time_step, 0.5 * time_step, time_step, None)[stage]
    if last:
        live = lane < count_ref[0]
        advanced_ref, gram_ref, wide_ref = refs
    else:
        next_ref, next_acc_ref, *out_refs = refs
    states = []
    zero = jnp.zeros(shape, jnp.float32)
    for m in range(groups):
        rows = pl.ds(m * sublanes, sublanes)
        own = [state_ref[f, rows, :] for f in range(fields)]
        ghosts = []
        for f in range(fields):
            block = zero
            for b in range(4):
                block = jnp.where(group == (m + b) % groups, recv_refs[b][f], block)
            ghosts.append(block)
        advection = [None] * fields
        diffusion = [-4.0 * own[f] for f in range(fields)]
        for face in range(4):
            index = jnp.bitwise_and(ghost_index[face] + m * slots, lanes - 1)
            near = []
            for f in range(fields):
                near.append(
                    jnp.where(
                        is_ghost[face],
                        lane_take(ghosts[f], index),
                        lane_take(own[f], own_index[face]),
                    )
                )
                diffusion[f] = diffusion[f] + near[f]
            for i in range(fields):
                for j in range(fields):
                    term = jac_ref[face, i * fields + j] * near[j]
                    advection[i] = term if advection[i] is None else advection[i] + term
        following = []
        for f in range(fields):
            slope = advect * advection[f] + diffuse * diffusion[f]
            kept = acc_ref[f, rows, :] + kept_coef * slope
            if last:
                advanced_ref[f, rows, :] = jnp.where(live, kept, 0.0)
            else:
                next_acc_ref[f, rows, :] = kept
                after = q_ref[f, rows, :] + next_coef * slope
                next_ref[f, rows, :] = after
                following.append(after)
        states.append(following)
    if not last:
        pack(states, send_index(send_ref, flags_ref, slots), out_refs, groups, slots)
        return
    half = vectors // 2
    wide_ref[...] = jnp.zeros(wide_ref.shape, jnp.float32)
    total = None
    for f in range(fields):
        wide_ref[pl.ds(0, vectors), :] = advanced_ref[f]
        wide_ref[pl.ds(vectors, vectors), :] = jnp.zeros((vectors, lanes), jnp.float32)
        low = wide_ref[...]
        high = jnp.concatenate([low[vectors:], low[:vectors]], axis=0)
        for left, right in ((low[:half], low), (low[half:vectors], high)):
            part = lax.dot_general(
                left,
                right,
                (((1,), (1,)), ((), ())),
                precision=HIGHEST,
                preferred_element_type=jnp.float32,
            )
            total = part if total is None else total + part
    gram_ref[...] = total


def factor_kernel(scale, gram_ref, advanced_ref, basis_ref, factor_ref):
    fields, vectors, cells = advanced_ref.shape
    half = vectors // 2
    folded = gram_ref[...] * scale
    turned = pltpu.roll(folded, vectors, 1)
    work = jnp.concatenate([folded, turned], axis=0)
    row = lax.broadcasted_iota(jnp.int32, (vectors, lanes), 0)
    lane = lax.broadcasted_iota(jnp.int32, (vectors, lanes), 1)
    work = jnp.where(lane < vectors, work, jnp.where(lane == row + vectors, 1.0, 0.0))
    blocks = [work[b * sublanes : (b + 1) * sublanes] for b in range(vectors // sublanes)]
    sub = lax.broadcasted_iota(jnp.int32, (sublanes, lanes), 0)
    scales = []
    for b in range(len(blocks)):
        start = b * sublanes
        count = len(blocks) - b
        columns = [
            [
                jnp.broadcast_to(blocks[c][:, start + k : start + k + 1], (sublanes, lanes))
                for c in range(b, len(blocks))
            ]
            for k in range(sublanes)
        ]
        for k in range(sublanes):
            pivot = jnp.broadcast_to(columns[k][0][k : k + 1], (sublanes, lanes))
            scales.append(pivot)
            inverse = 1.0 / pivot
            row_k = jnp.broadcast_to(blocks[b][k : k + 1], (sublanes, lanes)) * inverse
            later = [
                jnp.broadcast_to(columns[n][0][k : k + 1], (sublanes, lanes)) * inverse
                for n in range(k + 1, sublanes)
            ]
            for c in range(count):
                ratio = columns[k][c]
                if c == 0:
                    ratio = jnp.where(sub > k, ratio, 0.0)
                blocks[b + c] = blocks[b + c] - ratio * row_k
                for n in range(k + 1, sublanes):
                    columns[n][c] = columns[n][c] - ratio * later[n - k - 1]
    for b in range(len(blocks)):
        pivots = scales[b * sublanes]
        for k in range(1, sublanes):
            pivots = jnp.where(sub == k, scales[b * sublanes + k], pivots)
        blocks[b] = blocks[b] * lax.rsqrt(pivots)
    done = jnp.concatenate(blocks, axis=0)
    factor_ref[...] = jnp.where(lane >= row, done, 0.0)[:, :vectors]
    inverse_lower = pltpu.roll(done, vectors, 1)[:, :vectors]
    for f in range(fields):
        basis_ref[f] = jnp.dot(
            inverse_lower,
            advanced_ref[f],
            precision=HIGHEST,
            preferred_element_type=jnp.float32,
        )


def summed(value, axes):
    for axis, size, pair_first in axes:
        bits = size.bit_length() - 1
        at = 0
        while at < bits:
            width = 1 if (pair_first and at == 0) else min(2, bits - at)
            parts = [value]
            for k in range(1, 1 << width):
                step = k << at
                parts.append(lax.ppermute(value, axis, [(i, i ^ step) for i in range(size)]))
            while len(parts) > 1:
                parts = [parts[i] + parts[i + 1] for i in range(0, len(parts), 2)]
            value = parts[0]
            at += width
    return value


def shards(
    mesh_shape,
    test_vectors,
    face_jacobians,
    wave_speed,
    viscosity,
    inverse_volume,
    connectivity,
    send_rows,
    cell_count,
):
    rows, cols = mesh_shape
    fields, vectors, cells = test_vectors.shape
    slots = send_rows.shape[1]
    assert cells == lanes and vectors * slots == sublanes * lanes and 2 * vectors == lanes
    vmem = pl.BlockSpec(memory_space=pltpu.VMEM)
    smem = pl.BlockSpec(memory_space=pltpu.SMEM)
    flags = jnp.stack(
        [1 - lax.axis_index("gx") % 2, 1 - lax.axis_index("gy") % 2]
    ).astype(jnp.int32)
    jacobians = face_jacobians.reshape(4, fields * fields)
    speed = wave_speed.reshape(1, cells)
    visc = viscosity.reshape(1, cells)
    volume = inverse_volume.reshape(1, cells)
    state = jax.ShapeDtypeStruct(test_vectors.shape, jnp.float32)
    block = jax.ShapeDtypeStruct((fields, sublanes, lanes), jnp.float32)
    params = pltpu.CompilerParams(vmem_limit_bytes=16 * 1024 * 1024)
    pairs = matchings(rows, cols)

    def exchange(sent):
        got = [None] * 4
        for which in (0, 3, 2, 1):
            got[which] = lax.ppermute(sent[which], ("gx", "gy"), pairs[which])
        return got

    sent = pl.pallas_call(
        pack_kernel,
        out_shape=[block] * 4,
        in_specs=[smem, smem, vmem],
        out_specs=[vmem] * 4,
        compiler_params=params,
        name="pack",
    )(flags, send_rows, test_vectors)
    held = []
    for stage in range(4):
        got = exchange(sent)
        last = stage == 3
        gram_shape = jax.ShapeDtypeStruct((vectors // 2, lanes), jnp.float32)
        result = pl.pallas_call(
            functools.partial(stage_kernel, stage),
            out_shape=[state, gram_shape] if last else [state, state] + [block] * 4,
            in_specs=[smem] * 4 + [vmem] * (5 + len(held) + 4),
            out_specs=[vmem] * (2 if last else 6),
            scratch_shapes=[pltpu.VMEM((2 * vectors, lanes), jnp.float32)] if last else [],
            compiler_params=params,
            name="stage",
        )(
            flags,
            send_rows,
            jacobians,
            cell_count,
            connectivity,
            speed,
            visc,
            volume,
            test_vectors,
            *held,
            *got,
        )
        held, sent = result[:2], result[2:]
    advanced, gram = held
    gram = summed(gram, (("gx", rows, True), ("gy", cols, False)))
    scale = 1.0 / float(fields * cells * rows * cols)
    return pl.pallas_call(
        functools.partial(factor_kernel, scale),
        out_shape=[state, jax.ShapeDtypeStruct((vectors, vectors), jnp.float32)],
        in_specs=[vmem] * 2,
        out_specs=[vmem] * 2,
        compiler_params=params,
        name="factor",
    )(gram, advanced)


def solution(mesh):
    placed = (
        P(None, None, ("gx", "gy")),
        P(),
        P(("gx", "gy")),
        P(("gx", "gy")),
        P(("gx", "gy")),
        P(None, ("gx", "gy")),
        P(None, ("gx", "gy")),
        P(("gx", "gy")),
    )
    return jax.shard_map(
        functools.partial(shards, (mesh.shape["gx"], mesh.shape["gy"])),
        mesh=mesh,
        in_specs=placed,
        out_specs=(P(None, None, ("gx", "gy")), P()),
        check_vma=False,
    )
```

time: 171 us -> 52.7 us (0.31)
  blocking collectives: 42 us -> 0 us
  local copies, waits for them, and re-layouts: 41.4 us -> 2.28 us
  starting transfers between devices: 39.9 us -> 23.7 us
  other arithmetic: 13.3 us -> 0.09 us
  Pallas kernels: 0 us -> 10.8 us
  waiting for transfers between devices: 23.6 us -> 14.2 us
  matrix products: 7.86 us -> 0 us
    psum x2 -> x0, blocking collectives: 42 us -> none  [shards(): gram_whole = lax.psum(lax.psum(gram_local, 'gy'), 'gx')]
    gather x39 -> x0, local copies, waits for them, and re-layouts: 32.2 us -> none  [the longest x32 28.4 us: cell_operator(): neighbor = jnp.take(extended, connect[face_index], axis=2)]
    ppermute x16 -> x23, starting transfers between devices: 39.9 us -> 23.7 us  [the longest x16 15.7 us: exchange(): got[which] = lax.ppermute(sent[which], ('gx', 'gy'), pairs[which])]
    another operation x4 -> x1, other arithmetic: 11.4 us -> 0.08 us  [shards(): jnp.stack([1 - lax.axis_index('gx') % 2, 1 - lax.axis_index('gy') % 2])]
    pallas_call x0 -> x6, Pallas kernels: none -> 10.8 us  [the longest x4 7.19 us: shards(): pl.pallas_call(functools.partial(stage_kernel, stage), out_shape=[state,...]
    ppermute x16 -> x23, waiting for transfers between devices: 23.6 us -> 14.2 us  [the longest x7 7.46 us: summed(): lax.ppermute(value, axis, [(i, i ^ step) for i in range(size)])]
    dot_general x18 -> x0, matrix products: 7.63 us -> none  [the longest x16 6.35 us: cell_operator(): jnp.einsum('ij,jvc->ivc', face_jacobians[face_index], neighbor, precision...]
    concatenate x7 -> x0, local copies, waits for them, and re-layouts: 3.51 us -> none  [operate(): extended = jnp.concatenate([state_now] + incoming + [zero_block], axis=2)]
  transfers between devices with their start and end apart: 16 -> 23, of which waited for: 9 -> 13; matrix products, arithmetic and copies ran while one was open for 0% -> 0% of each run, Pallas kernels for 0% -> 0%
where the time goes in v1:
time: 52.7 us; the launch traced here: 52.5 us
  starting transfers between devices  23.7 us (45%)
  waiting for transfers between devices  14.2 us (27%)
  Pallas kernels  10.8 us (20%)
  local copies, waits for them, and re-layouts  2.28 us (4%)
  between operations  1.44 us (3%)
    ppermute x16, starting transfers between devices, exchange(): got[which] = lax.ppermute(sent[which], ('gx', 'gy'), pairs[which])  15.7 us
    ppermute x7, starting transfers between devices, summed(): lax.ppermute(value, axis, [(i, i ^ step) for i in range(size)])  7.99 us
    ppermute x7, waiting for transfers between devices, summed(): lax.ppermute(value, axis, [(i, i ^ step) for i in range(size)])  7.46 us
    pallas_call x4, Pallas kernels, shards(): pl.pallas_call(functools.partial(stage_kernel, stage), out_shape=[state,...  7.19 us
    ppermute x16, waiting for transfers between devices, exchange(): got[which] = lax.ppermute(sent[which], ('gx', 'gy'), pairs[which])  6.72 us
    pallas_call x1, Pallas kernels, shards(): pl.pallas_call(functools.partial(factor_kernel, scale), out_shape=[state,...  2.82 us
    unnamed x17, local copies, waits for them, and re-layouts  2.2 us
  transfers between devices with their start and end apart: 23, of which 13 were waited for; matrix products, arithmetic and copies ran while one was open for 0% of the time, Pallas kernels for 0%

profile of v1, /device:TPU:0, one launch (start us, length us, event | category | flops | bytes accessed | tf_op | source)
XLA Modules:
  0.0 52.5 jit_solution(7913397759892361989)
XLA Ops:
  1.3 0.9 %copy-done = f32[5,64,128]{2,1,0:T(8,128)S(1)} copy-done((f32[5,64,128]{2,1,0:T(8,128)S(1)}, f32[5,64,128]{2,1,0:T(8,128)}, u32[]{:S(2)}) %copy-start) | copy-done | bytes 163864
  2.3 0.8 %pack.1 = (f32[5,8,128]{2,1,0:T(8,128)S(1)}, f32[5,8,128]{2,1,0:T(8,128)S(1)}, f32[5,8,128]{2,1,0:T(8,128)S(1)}, f32[5,8,128]{2,1,0:T(8,128)S(1)}) custom-call(s32[2]{0:T(128)S(1)} %pad_add_fusion.flags_ref, s32[4,16]{1,0:T(4,128)S(1)} %copy-done.2, f32[5,64,128]{2,1,0:T(8,128)S(1)} %copy-done), custom_call_target="tpu_custom_call" | custom-call | tf_op jit(solution)/shard_map/pack/pallas_call | solution.py:316
  3.6 3.6 %collective-permute-start.1 = (f32[5,8,128]{2,1,0:T(8,128)S(1)}, f32[5,8,128]{2,1,0:T(8,128)S(1)}, u32[]{:S(2)}, u32[]{:S(2)}) collective-permute-start(f32[5,8,128]{2,1,0:T(8,128)S(1)} %get-tuple-element.27), channel_id=1, source_target_pairs={{0,28},{1,29},{2,30},{3,31},{4,8},{5,9},{6,10},{7,11},{8,4},{9,5},... | collective-permute-start | bytes 61448 | tf_op jit(solution)/shard_map/ppermute | solution.py:313
  7.1 1.6 %collective-permute-start.2 = (f32[5,8,128]{2,1,0:T(8,128)S(1)}, f32[5,8,128]{2,1,0:T(8,128)S(1)}, u32[]{:S(2)}, u32[]{:S(2)}) collective-permute-start(f32[5,8,128]{2,1,0:T(8,128)S(1)} %get-tuple-element.28), channel_id=1, source_target_pairs={{0,1},{1,0},{2,3},{3,2},{4,5},{5,4},{6,7},{7,6},{8,9},{9,8},{10,11... | collective-permute-start | bytes 61448 | tf_op jit(solution)/shard_map/ppermute | solution.py:313
  9.5 1.4 %collective-permute-done.2.refs_2_ = f32[5,8,128]{2,1,0:T(8,128)S(1)} collective-permute-done((f32[5,8,128]{2,1,0:T(8,128)S(1)}, f32[5,8,128]{2,1,0:T(8,128)S(1)}, u32[]{:S(2)}, u32[]{:S(2)}) %collective-permute-start.2) | collective-permute-done | bytes 20512 | tf_op jit(solution)/shard_map/ppermute | solution.py:313
  11.0 0.6 %copy-done.3 = s32[4,128]{1,0:T(4,128)S(1)} copy-done((s32[4,128]{1,0:T(4,128)S(1)}, s32[4,128]{1,0:T(4,128)}, u32[]{:S(2)}) %copy-start.3) | copy-done | bytes 2072
  11.6 1.6 %stage.4 = (f32[5,64,128]{2,1,0:T(8,128)S(1)}, f32[5,64,128]{2,1,0:T(8,128)S(1)}, f32[5,8,128]{2,1,0:T(8,128)S(1)}, f32[5,8,128]{2,1,0:T(8,128)S(1)}, f32[5,8,12...) custom-call(s32[2]{0:T(128)S(1)} %pad_add_fusion.flags_ref, s32[4,16]{1,0:T(4,128)S(1)} %copy-done.2, ...), custom_call_target="tpu_custom_call" | custom-call | tf_op jit(solution)/shard_map/stage/pallas_call | solution.py:329
  13.9 2.7 %collective-permute-start.6 = (f32[5,8,128]{2,1,0:T(8,128)S(1)}, f32[5,8,128]{2,1,0:T(8,128)S(1)}, u32[]{:S(2)}, u32[]{:S(2)}) collective-permute-start(f32[5,8,128]{2,1,0:T(8,128)S(1)} %get-tuple-element.34), channel_id=1, source_target_pairs={{0,1},{1,0},{2,3},{3,2},{4,5},{5,4},{6,7},{7,6},{8,9},{9,8},{10,11... | collective-permute-start | bytes 61448 | tf_op jit(solution)/shard_map/ppermute | solution.py:313
  16.7 0.8 %collective-permute-done.5.refs_3_ = f32[5,8,128]{2,1,0:T(8,128)S(1)} collective-permute-done((f32[5,8,128]{2,1,0:T(8,128)S(1)}, f32[5,8,128]{2,1,0:T(8,128)S(1)}, u32[]{:S(2)}, u32[]{:S(2)}) %collective-permute-start.5) | collective-permute-done | bytes 20512 | tf_op jit(solution)/shard_map/ppermute | solution.py:313
  17.5 0.9 %collective-permute-done.6.refs_4_ = f32[5,8,128]{2,1,0:T(8,128)S(1)} collective-permute-done((f32[5,8,128]{2,1,0:T(8,128)S(1)}, f32[5,8,128]{2,1,0:T(8,128)S(1)}, u32[]{:S(2)}, u32[]{:S(2)}) %collective-permute-start.6) | collective-permute-done | bytes 20512 | tf_op jit(solution)/shard_map/ppermute | solution.py:313
  18.4 1.6 %stage.5 = (f32[5,64,128]{2,1,0:T(8,128)S(1)}, f32[5,64,128]{2,1,0:T(8,128)S(1)}, f32[5,8,128]{2,1,0:T(8,128)S(1)}, f32[5,8,128]{2,1,0:T(8,128)S(1)}, f32[5,8,12...) custom-call(s32[2]{0:T(128)S(1)} %pad_add_fusion.flags_ref, s32[4,16]{1,0:T(4,128)S(1)} %copy-done.2, ...), custom_call_target="tpu_custom_call" | custom-call | tf_op jit(solution)/shard_map/stage/pallas_call | solution.py:329
  20.1 1.5 %collective-permute-start.9 = (f32[5,8,128]{2,1,0:T(8,128)S(1)}, f32[5,8,128]{2,1,0:T(8,128)S(1)}, u32[]{:S(2)}, u32[]{:S(2)}) collective-permute-start(f32[5,8,128]{2,1,0:T(8,128)S(1)} %get-tuple-element.39), channel_id=1, source_target_pairs={{0,28},{1,29},{2,30},{3,31},{4,8},{5,9},{6,10},{7,11},{8,4},{9,5},... | collective-permute-start | bytes 61448 | tf_op jit(solution)/shard_map/ppermute | solution.py:313
  21.6 2.2 %collective-permute-start.10 = (f32[5,8,128]{2,1,0:T(8,128)S(1)}, f32[5,8,128]{2,1,0:T(8,128)S(1)}, u32[]{:S(2)}, u32[]{:S(2)}) collective-permute-start(f32[5,8,128]{2,1,0:T(8,128)S(1)} %get-tuple-element.40), channel_id=1, source_target_pairs={{0,1},{1,0},{2,3},{3,2},{4,5},{5,4},{6,7},{7,6},{8,9},{9,8},{10,11... | collective-permute-start | bytes 61448 | tf_op jit(solution)/shard_map/ppermute | solution.py:313
  24.3 1.3 %collective-permute-done.10.refs_4_ = f32[5,8,128]{2,1,0:T(8,128)S(1)} collective-permute-done((f32[5,8,128]{2,1,0:T(8,128)S(1)}, f32[5,8,128]{2,1,0:T(8,128)S(1)}, u32[]{:S(2)}, u32[]{:S(2)}) %collective-permute-start.10) | collective-permute-done | bytes 20512 | tf_op jit(solution)/shard_map/ppermute | solution.py:313
  25.6 1.6 %stage.6 = (f32[5,64,128]{2,1,0:T(8,128)S(1)}, f32[5,64,128]{2,1,0:T(8,128)S(1)}, f32[5,8,128]{2,1,0:T(8,128)S(1)}, f32[5,8,128]{2,1,0:T(8,128)S(1)}, f32[5,8,12...) custom-call(s32[2]{0:T(128)S(1)} %pad_add_fusion.flags_ref, s32[4,16]{1,0:T(4,128)S(1)} %copy-done.2, ...), custom_call_target="tpu_custom_call" | custom-call | tf_op jit(solution)/shard_map/stage/pallas_call | solution.py:329
  27.3 0.7 %collective-permute-start.13 = (f32[5,8,128]{2,1,0:T(8,128)S(1)}, f32[5,8,128]{2,1,0:T(8,128)S(1)}, u32[]{:S(2)}, u32[]{:S(2)}) collective-permute-start(f32[5,8,128]{2,1,0:T(8,128)S(1)} %get-tuple-element.45), channel_id=1, source_target_pairs={{0,28},{1,29},{2,30},{3,31},{4,8},{5,9},{6,10},{7,11},{8,4},{9,5},... | collective-permute-start | bytes 61448 | tf_op jit(solution)/shard_map/ppermute | solution.py:313
  27.9 2.1 %collective-permute-start.14 = (f32[5,8,128]{2,1,0:T(8,128)S(1)}, f32[5,8,128]{2,1,0:T(8,128)S(1)}, u32[]{:S(2)}, u32[]{:S(2)}) collective-permute-start(f32[5,8,128]{2,1,0:T(8,128)S(1)} %get-tuple-element.46), channel_id=1, source_target_pairs={{0,1},{1,0},{2,3},{3,2},{4,5},{5,4},{6,7},{7,6},{8,9},{9,8},{10,11... | collective-permute-start | bytes 61448 | tf_op jit(solution)/shard_map/ppermute | solution.py:313
  30.1 1.4 %collective-permute-done.13.refs_3_ = f32[5,8,128]{2,1,0:T(8,128)S(1)} collective-permute-done((f32[5,8,128]{2,1,0:T(8,128)S(1)}, f32[5,8,128]{2,1,0:T(8,128)S(1)}, u32[]{:S(2)}, u32[]{:S(2)}) %collective-permute-start.13) | collective-permute-done | bytes 20512 | tf_op jit(solution)/shard_map/ppermute | solution.py:313
  31.8 2.4 %stage.7 = (f32[5,64,128]{2,1,0:T(8,128)S(1)}, f32[32,128]{1,0:T(8,128)S(1)}) custom-call(s32[2]{0:T(128)S(1)} %pad_add_fusion.flags_ref, s32[4,16]{1,0:T(4,128)S(1)} %copy-done.2, f32[4,25]{1,0:T(4,128)S(1)} %reshape.16.jac_ref, s32[1]{0:T(128)S(6)} %copy.12.count_ref, s32[4,128]{1,0:T(4,128)S(1)} %copy-done.3, f32[1,128]{1,0:T(1,128)S(1)} %bitcast.8, ...), custom_call_target="tpu_custom_call" | custom-call | tf_op jit(solution)/shard_map/stage/pallas_call | solution.py:329
  34.3 1.2 %collective-permute-done.16 = f32[32,128]{1,0:T(8,128)S(1)} collective-permute-done((f32[32,128]{1,0:T(8,128)S(1)}, f32[32,128]{1,0:T(8,128)S(1)}, u32[]{:S(2)}, u32[]{:S(2)}) %collective-permute-start.16) | collective-permute-done | bytes 16416 | tf_op jit(solution)/shard_map/ppermute | solution.py:273
  35.4 2.2 %collective-permute-start.19 = (f32[32,128]{1,0:T(8,128)S(1)}, f32[32,128]{1,0:T(8,128)S(1)}, u32[]{:S(2)}, u32[]{:S(2)}) collective-permute-start(f32[32,128]{1,0:T(8,128)S(1)} %add.30), channel_id=1, source_target_pairs={{0,24},{4,28},{8,16},{12,20},{16,8},{20,12},{24,0},{28,4},{1,25},{... | collective-permute-start | bytes 49160 | tf_op jit(solution)/shard_map/ppermute | solution.py:273
  37.6 0.7 %collective-permute-start.18 = (f32[32,128]{1,0:T(8,128)S(1)}, f32[32,128]{1,0:T(8,128)S(1)}, u32[]{:S(2)}, u32[]{:S(2)}) collective-permute-start(f32[32,128]{1,0:T(8,128)S(1)} %add.30), channel_id=1, source_target_pairs={{0,16},{4,20},{8,24},{12,28},{16,0},{20,4},{24,8},{28,12},{1,17},{... | collective-permute-start | bytes 49160 | tf_op jit(solution)/shard_map/ppermute | solution.py:273
  38.3 0.6 %collective-permute-start.17 = (f32[32,128]{1,0:T(8,128)S(1)}, f32[32,128]{1,0:T(8,128)S(1)}, u32[]{:S(2)}, u32[]{:S(2)}) collective-permute-start(f32[32,128]{1,0:T(8,128)S(1)} %add.30), channel_id=1, source_target_pairs={{0,8},{4,12},{8,0},{12,4},{16,24},{20,28},{24,16},{28,20},{1,9},{5... | collective-permute-start | bytes 49160 | tf_op jit(solution)/shard_map/ppermute | solution.py:273
  38.9 1.1 %collective-permute-done.19 = f32[32,128]{1,0:T(8,128)S(1)} collective-permute-done((f32[32,128]{1,0:T(8,128)S(1)}, f32[32,128]{1,0:T(8,128)S(1)}, u32[]{:S(2)}, u32[]{:S(2)}) %collective-permute-start.19) | collective-permute-done | bytes 16416 | tf_op jit(solution)/shard_map/ppermute | solution.py:273
  40.1 1.3 %collective-permute-done.18 = f32[32,128]{1,0:T(8,128)S(1)} collective-permute-done((f32[32,128]{1,0:T(8,128)S(1)}, f32[32,128]{1,0:T(8,128)S(1)}, u32[]{:S(2)}, u32[]{:S(2)}) %collective-permute-start.18) | collective-permute-done | bytes 16416 | tf_op jit(solution)/shard_map/ppermute | solution.py:273
  41.3 0.7 %collective-permute-done.17 = f32[32,128]{1,0:T(8,128)S(1)} collective-permute-done((f32[32,128]{1,0:T(8,128)S(1)}, f32[32,128]{1,0:T(8,128)S(1)}, u32[]{:S(2)}, u32[]{:S(2)}) %collective-permute-start.17) | collective-permute-done | bytes 16416 | tf_op jit(solution)/shard_map/ppermute | solution.py:273
  42.0 3.0 %collective-permute-start.22 = (f32[32,128]{1,0:T(8,128)S(1)}, f32[32,128]{1,0:T(8,128)S(1)}, u32[]{:S(2)}, u32[]{:S(2)}) collective-permute-start(f32[32,128]{1,0:T(8,128)S(1)} %add_add_fusion.1), channel_id=1, source_target_pairs={{0,3},{1,2},{2,1},{3,0},{4,7},{5,6},{6,5},{7,4},{8,11},{9,10},{10,... | collective-permute-start | bytes 49160 | tf_op jit(solution)/shard_map/ppermute | solution.py:273
  45.0 0.7 %collective-permute-start.21 = (f32[32,128]{1,0:T(8,128)S(1)}, f32[32,128]{1,0:T(8,128)S(1)}, u32[]{:S(2)}, u32[]{:S(2)}) collective-permute-start(f32[32,128]{1,0:T(8,128)S(1)} %add_add_fusion.1), channel_id=1, source_target_pairs={{0,2},{1,3},{2,0},{3,1},{4,6},{5,7},{6,4},{7,5},{8,10},{9,11},{10,... | collective-permute-start | bytes 49160 | tf_op jit(solution)/shard_map/ppermute | solution.py:273
  45.8 0.7 %collective-permute-start.20 = (f32[32,128]{1,0:T(8,128)S(1)}, f32[32,128]{1,0:T(8,128)S(1)}, u32[]{:S(2)}, u32[]{:S(2)}) collective-permute-start(f32[32,128]{1,0:T(8,128)S(1)} %add_add_fusion.1), channel_id=1, source_target_pairs={{0,1},{1,0},{2,3},{3,2},{4,5},{5,4},{6,7},{7,6},{8,9},{9,8},{10,11... | collective-permute-start | bytes 49160 | tf_op jit(solution)/shard_map/ppermute | solution.py:273
  46.5 1.3 %collective-permute-done.22 = f32[32,128]{1,0:T(8,128)S(1)} collective-permute-done((f32[32,128]{1,0:T(8,128)S(1)}, f32[32,128]{1,0:T(8,128)S(1)}, u32[]{:S(2)}, u32[]{:S(2)}) %collective-permute-start.22) | collective-permute-done | bytes 16416 | tf_op jit(solution)/shard_map/ppermute | solution.py:273
  47.7 1.9 %collective-permute-done.21 = f32[32,128]{1,0:T(8,128)S(1)} collective-permute-done((f32[32,128]{1,0:T(8,128)S(1)}, f32[32,128]{1,0:T(8,128)S(1)}, u32[]{:S(2)}, u32[]{:S(2)}) %collective-permute-start.21) | collective-permute-done | bytes 16416 | tf_op jit(solution)/shard_map/ppermute | solution.py:273
  49.7 2.8 %factor.1 = (f32[5,64,128]{2,1,0:T(8,128)}, f32[64,64]{1,0:T(8,128)}) custom-call(f32[32,128]{1,0:T(8,128)S(1)} %add_add_fusion.gram_ref, f32[5,64,128]{2,1,0:T(8,128)S(1)} %get-tuple-element.49.advanced_ref), custom_call_target="tpu_custom_call" | custom-call | tf_op jit(solution)/shard_map/factor/pallas_call | solution.py:354
  (42 shorter events, 3.1 us)
Async XLA Ops:
  0.6 0.7 %copy-start.2 = (s32[4,16]{1,0:T(4,128)S(1)}, s32[4,16]{1,0:T(4,128)}, u32[]{:S(2)}) copy-start(s32[4,16]{1,0:T(4,128)} %send_ref.9) | copy-start | bytes 772
  1.3 0.9 %copy-start = (f32[5,64,128]{2,1,0:T(8,128)S(1)}, f32[5,64,128]{2,1,0:T(8,128)}, u32[]{:S(2)}) copy-start(f32[5,64,128]{2,1,0:T(8,128)} %q_ref.9) | copy-start | bytes 491524
  2.2 7.1 %copy-start.7 = (f32[4,5,5]{2,0,1:T(4,128)S(1)}, f32[4,5,5]{2,0,1:T(4,128)}, u32[]{:S(2)}) copy-start(f32[4,5,5]{2,0,1:T(4,128)} %param.9) | copy-start | bytes 1204
  2.2 8.7 %copy-start.1 = (f32[5,64,128]{2,1,0:T(8,128)S(1)}, f32[5,64,128]{2,1,0:T(8,128)}, u32[]{:S(2)}) copy-start(f32[5,64,128]{2,1,0:T(8,128)} %q_ref.9) | copy-start | bytes 491524
  3.1 6.4 %collective-permute-start = (f32[5,8,128]{2,1,0:T(8,128)S(1)}, f32[5,8,128]{2,1,0:T(8,128)S(1)}, u32[]{:S(2)}, u32[]{:S(2)}) collective-permute-start(f32[5,8,128]{2,1,0:T(8,128)S(1)} %get-tuple-element.26), channel_id=1, source_target_pairs={{0,4},{1,5},{2,6},{3,7},{4,0},{5,1},{6,2},{7,3},{8,12},{9,13},{10,... | collective-permute-start | bytes 61448 | tf_op jit(solution)/shard_map/ppermute | solution.py:313
  3.6 5.9 %collective-permute-start.1 = (f32[5,8,128]{2,1,0:T(8,128)S(1)}, f32[5,8,128]{2,1,0:T(8,128)S(1)}, u32[]{:S(2)}, u32[]{:S(2)}) collective-permute-start(f32[5,8,128]{2,1,0:T(8,128)S(1)} %get-tuple-element.27), channel_id=1, source_target_pairs={{0,28},{1,29},{2,30},{3,31},{4,8},{5,9},{6,10},{7,11},{8,4},{9,5},... | collective-permute-start | bytes 61448 | tf_op jit(solution)/shard_map/ppermute | solution.py:313
  7.1 3.8 %collective-permute-start.2 = (f32[5,8,128]{2,1,0:T(8,128)S(1)}, f32[5,8,128]{2,1,0:T(8,128)S(1)}, u32[]{:S(2)}, u32[]{:S(2)}) collective-permute-start(f32[5,8,128]{2,1,0:T(8,128)S(1)} %get-tuple-element.28), channel_id=1, source_target_pairs={{0,1},{1,0},{2,3},{3,2},{4,5},{5,4},{6,7},{7,6},{8,9},{9,8},{10,11... | collective-permute-start | bytes 61448 | tf_op jit(solution)/shard_map/ppermute | solution.py:313
  8.7 2.2 %collective-permute-start.3 = (f32[5,8,128]{2,1,0:T(8,128)S(1)}, f32[5,8,128]{2,1,0:T(8,128)S(1)}, u32[]{:S(2)}, u32[]{:S(2)}) collective-permute-start(f32[5,8,128]{2,1,0:T(8,128)S(1)} %get-tuple-element.29), channel_id=1, source_target_pairs={{0,4},{1,2},{2,1},{3,7},{4,0},{5,6},{6,5},{7,3},{8,12},{9,10},{10,... | collective-permute-start | bytes 61448 | tf_op jit(solution)/shard_map/ppermute | solution.py:313
  10.9 0.7 %copy-start.3 = (s32[4,128]{1,0:T(4,128)S(1)}, s32[4,128]{1,0:T(4,128)}, u32[]{:S(2)}) copy-start(s32[4,128]{1,0:T(4,128)} %conn_ref.7) | copy-start | bytes 6148
  10.9 0.7 %copy-start.4 = (f32[128]{0:T(128)S(1)}, f32[128]{0:T(128)}, u32[]{:S(2)}) copy-start(f32[128]{0:T(128)} %param.10) | copy-start | bytes 1540
  10.9 0.7 %copy-start.5 = (f32[128]{0:T(128)S(1)}, f32[128]{0:T(128)}, u32[]{:S(2)}) copy-start(f32[128]{0:T(128)} %param.11) | copy-start | bytes 1540
  10.9 0.7 %copy-start.6 = (f32[128]{0:T(128)S(1)}, f32[128]{0:T(128)}, u32[]{:S(2)}) copy-start(f32[128]{0:T(128)} %param.12) | copy-start | bytes 1540
  13.2 3.4 %collective-permute-start.4 = (f32[5,8,128]{2,1,0:T(8,128)S(1)}, f32[5,8,128]{2,1,0:T(8,128)S(1)}, u32[]{:S(2)}, u32[]{:S(2)}) collective-permute-start(f32[5,8,128]{2,1,0:T(8,128)S(1)} %get-tuple-element.32), channel_id=1, source_target_pairs={{0,4},{1,5},{2,6},{3,7},{4,0},{5,1},{6,2},{7,3},{8,12},{9,13},{10,... | collective-permute-start | bytes 61448 | tf_op jit(solution)/shard_map/ppermute | solution.py:313
  13.3 4.2 %collective-permute-start.5 = (f32[5,8,128]{2,1,0:T(8,128)S(1)}, f32[5,8,128]{2,1,0:T(8,128)S(1)}, u32[]{:S(2)}, u32[]{:S(2)}) collective-permute-start(f32[5,8,128]{2,1,0:T(8,128)S(1)} %get-tuple-element.33), channel_id=1, source_target_pairs={{0,28},{1,29},{2,30},{3,31},{4,8},{5,9},{6,10},{7,11},{8,4},{9,5},... | collective-permute-start | bytes 61448 | tf_op jit(solution)/shard_map/ppermute | solution.py:313
  13.9 4.5 %collective-permute-start.6 = (f32[5,8,128]{2,1,0:T(8,128)S(1)}, f32[5,8,128]{2,1,0:T(8,128)S(1)}, u32[]{:S(2)}, u32[]{:S(2)}) collective-permute-start(f32[5,8,128]{2,1,0:T(8,128)S(1)} %get-tuple-element.34), channel_id=1, source_target_pairs={{0,1},{1,0},{2,3},{3,2},{4,5},{5,4},{6,7},{7,6},{8,9},{9,8},{10,11... | collective-permute-start | bytes 61448 | tf_op jit(solution)/shard_map/ppermute | solution.py:313
  16.6 1.8 %collective-permute-start.7 = (f32[5,8,128]{2,1,0:T(8,128)S(1)}, f32[5,8,128]{2,1,0:T(8,128)S(1)}, u32[]{:S(2)}, u32[]{:S(2)}) collective-permute-start(f32[5,8,128]{2,1,0:T(8,128)S(1)} %get-tuple-element.35), channel_id=1, source_target_pairs={{0,4},{1,2},{2,1},{3,7},{4,0},{5,6},{6,5},{7,3},{8,12},{9,10},{10,... | collective-permute-start | bytes 61448 | tf_op jit(solution)/shard_map/ppermute | solution.py:313
  20.0 3.8 %collective-permute-start.8 = (f32[5,8,128]{2,1,0:T(8,128)S(1)}, f32[5,8,128]{2,1,0:T(8,128)S(1)}, u32[]{:S(2)}, u32[]{:S(2)}) collective-permute-start(f32[5,8,128]{2,1,0:T(8,128)S(1)} %get-tuple-element.38), channel_id=1, source_target_pairs={{0,4},{1,5},{2,6},{3,7},{4,0},{5,1},{6,2},{7,3},{8,12},{9,13},{10,... | collective-permute-start | bytes 61448 | tf_op jit(solution)/shard_map/ppermute | solution.py:313
  20.1 4.2 %collective-permute-start.9 = (f32[5,8,128]{2,1,0:T(8,128)S(1)}, f32[5,8,128]{2,1,0:T(8,128)S(1)}, u32[]{:S(2)}, u32[]{:S(2)}) collective-permute-start(f32[5,8,128]{2,1,0:T(8,128)S(1)} %get-tuple-element.39), channel_id=1, source_target_pairs={{0,28},{1,29},{2,30},{3,31},{4,8},{5,9},{6,10},{7,11},{8,4},{9,5},... | collective-permute-start | bytes 61448 | tf_op jit(solution)/shard_map/ppermute | solution.py:313
  21.6 3.9 %collective-permute-start.10 = (f32[5,8,128]{2,1,0:T(8,128)S(1)}, f32[5,8,128]{2,1,0:T(8,128)S(1)}, u32[]{:S(2)}, u32[]{:S(2)}) collective-permute-start(f32[5,8,128]{2,1,0:T(8,128)S(1)} %get-tuple-element.40), channel_id=1, source_target_pairs={{0,1},{1,0},{2,3},{3,2},{4,5},{5,4},{6,7},{7,6},{8,9},{9,8},{10,11... | collective-permute-start | bytes 61448 | tf_op jit(solution)/shard_map/ppermute | solution.py:313
  23.8 1.8 %collective-permute-start.11 = (f32[5,8,128]{2,1,0:T(8,128)S(1)}, f32[5,8,128]{2,1,0:T(8,128)S(1)}, u32[]{:S(2)}, u32[]{:S(2)}) collective-permute-start(f32[5,8,128]{2,1,0:T(8,128)S(1)} %get-tuple-element.41), channel_id=1, source_target_pairs={{0,4},{1,2},{2,1},{3,7},{4,0},{5,6},{6,5},{7,3},{8,12},{9,10},{10,... | collective-permute-start | bytes 61448 | tf_op jit(solution)/shard_map/ppermute | solution.py:313
  27.2 2.9 %collective-permute-start.12 = (f32[5,8,128]{2,1,0:T(8,128)S(1)}, f32[5,8,128]{2,1,0:T(8,128)S(1)}, u32[]{:S(2)}, u32[]{:S(2)}) collective-permute-start(f32[5,8,128]{2,1,0:T(8,128)S(1)} %get-tuple-element.44), channel_id=1, source_target_pairs={{0,4},{1,5},{2,6},{3,7},{4,0},{5,1},{6,2},{7,3},{8,12},{9,13},{10,... | collective-permute-start | bytes 61448 | tf_op jit(solution)/shard_map/ppermute | solution.py:313
  27.3 4.2 %collective-permute-start.13 = (f32[5,8,128]{2,1,0:T(8,128)S(1)}, f32[5,8,128]{2,1,0:T(8,128)S(1)}, u32[]{:S(2)}, u32[]{:S(2)}) collective-permute-start(f32[5,8,128]{2,1,0:T(8,128)S(1)} %get-tuple-element.45), channel_id=1, source_target_pairs={{0,28},{1,29},{2,30},{3,31},{4,8},{5,9},{6,10},{7,11},{8,4},{9,5},... | collective-permute-start | bytes 61448 | tf_op jit(solution)/shard_map/ppermute | solution.py:313
  27.9 3.9 %collective-permute-start.14 = (f32[5,8,128]{2,1,0:T(8,128)S(1)}, f32[5,8,128]{2,1,0:T(8,128)S(1)}, u32[]{:S(2)}, u32[]{:S(2)}) collective-permute-start(f32[5,8,128]{2,1,0:T(8,128)S(1)} %get-tuple-element.46), channel_id=1, source_target_pairs={{0,1},{1,0},{2,3},{3,2},{4,5},{5,4},{6,7},{7,6},{8,9},{9,8},{10,11... | collective-permute-start | bytes 61448 | tf_op jit(solution)/shard_map/ppermute | solution.py:313
  30.1 1.8 %collective-permute-start.15 = (f32[5,8,128]{2,1,0:T(8,128)S(1)}, f32[5,8,128]{2,1,0:T(8,128)S(1)}, u32[]{:S(2)}, u32[]{:S(2)}) collective-permute-start(f32[5,8,128]{2,1,0:T(8,128)S(1)} %get-tuple-element.47), channel_id=1, source_target_pairs={{0,4},{1,2},{2,1},{3,7},{4,0},{5,6},{6,5},{7,3},{8,12},{9,10},{10,... | collective-permute-start | bytes 61448 | tf_op jit(solution)/shard_map/ppermute | solution.py:313
  34.2 1.2 %collective-permute-start.16 = (f32[32,128]{1,0:T(8,128)S(1)}, f32[32,128]{1,0:T(8,128)S(1)}, u32[]{:S(2)}, u32[]{:S(2)}) collective-permute-start(f32[32,128]{1,0:T(8,128)S(1)} %get-tuple-element.48), channel_id=1, source_target_pairs={{0,4},{4,0},{8,12},{12,8},{16,20},{20,16},{24,28},{28,24},{1,5},{5... | collective-permute-start | bytes 49160 | tf_op jit(solution)/shard_map/ppermute | solution.py:273
  35.4 4.6 %collective-permute-start.19 = (f32[32,128]{1,0:T(8,128)S(1)}, f32[32,128]{1,0:T(8,128)S(1)}, u32[]{:S(2)}, u32[]{:S(2)}) collective-permute-start(f32[32,128]{1,0:T(8,128)S(1)} %add.30), channel_id=1, source_target_pairs={{0,24},{4,28},{8,16},{12,20},{16,8},{20,12},{24,0},{28,4},{1,25},{... | collective-permute-start | bytes 49160 | tf_op jit(solution)/shard_map/ppermute | solution.py:273
  37.6 3.7 %collective-permute-start.18 = (f32[32,128]{1,0:T(8,128)S(1)}, f32[32,128]{1,0:T(8,128)S(1)}, u32[]{:S(2)}, u32[]{:S(2)}) collective-permute-start(f32[32,128]{1,0:T(8,128)S(1)} %add.30), channel_id=1, source_target_pairs={{0,16},{4,20},{8,24},{12,28},{16,0},{20,4},{24,8},{28,12},{1,17},{... | collective-permute-start | bytes 49160 | tf_op jit(solution)/shard_map/ppermute | solution.py:273
  38.3 3.7 %collective-permute-start.17 = (f32[32,128]{1,0:T(8,128)S(1)}, f32[32,128]{1,0:T(8,128)S(1)}, u32[]{:S(2)}, u32[]{:S(2)}) collective-permute-start(f32[32,128]{1,0:T(8,128)S(1)} %add.30), channel_id=1, source_target_pairs={{0,8},{4,12},{8,0},{12,4},{16,24},{20,28},{24,16},{28,20},{1,9},{5... | collective-permute-start | bytes 49160 | tf_op jit(solution)/shard_map/ppermute | solution.py:273
  42.0 5.7 %collective-permute-start.22 = (f32[32,128]{1,0:T(8,128)S(1)}, f32[32,128]{1,0:T(8,128)S(1)}, u32[]{:S(2)}, u32[]{:S(2)}) collective-permute-start(f32[32,128]{1,0:T(8,128)S(1)} %add_add_fusion.1), channel_id=1, source_target_pairs={{0,3},{1,2},{2,1},{3,0},{4,7},{5,6},{6,5},{7,4},{8,11},{9,10},{10,... | collective-permute-start | bytes 49160 | tf_op jit(solution)/shard_map/ppermute | solution.py:273
  45.0 4.7 %collective-permute-start.21 = (f32[32,128]{1,0:T(8,128)S(1)}, f32[32,128]{1,0:T(8,128)S(1)}, u32[]{:S(2)}, u32[]{:S(2)}) collective-permute-start(f32[32,128]{1,0:T(8,128)S(1)} %add_add_fusion.1), channel_id=1, source_target_pairs={{0,2},{1,3},{2,0},{3,1},{4,6},{5,7},{6,4},{7,5},{8,10},{9,11},{10,... | collective-permute-start | bytes 49160 | tf_op jit(solution)/shard_map/ppermute | solution.py:273
  45.8 3.9 %collective-permute-start.20 = (f32[32,128]{1,0:T(8,128)S(1)}, f32[32,128]{1,0:T(8,128)S(1)}, u32[]{:S(2)}, u32[]{:S(2)}) collective-permute-start(f32[32,128]{1,0:T(8,128)S(1)} %add_add_fusion.1), channel_id=1, source_target_pairs={{0,1},{1,0},{2,3},{3,2},{4,5},{5,4},{6,7},{7,6},{8,9},{9,8},{10,11... | collective-permute-start | bytes 49160 | tf_op jit(solution)/shard_map/ppermute | solution.py:273

commit v2 on v1

v2 whole, which is shorter than its diff:
```python
import functools

import jax
import jax.numpy as jnp
from jax import lax
from jax.experimental import pallas as pl
from jax.experimental.pallas import tpu as pltpu
from jax.sharding import PartitionSpec as P

time_step = 0.4
lanes = 128
sublanes = 8
HIGHEST = lax.Precision.HIGHEST


def partner(index, count, odd):
    other = index + 1 if index % 2 == odd else index - 1
    return other if 0 <= other < count else None


def matchings(rows, cols):
    row_even, row_odd, col_even, col_odd = [], [], [], []
    for i in range(rows):
        for j in range(cols):
            here = i * cols + j
            row_even.append((here, (i ^ 1) * cols + j))
            col_even.append((here, i * cols + (j ^ 1)))
            up = partner(i, rows, 1)
            row_odd.append((here, (rows - 1 - i if up is None else up) * cols + j))
            across = partner(j, cols, 1)
            col_odd.append((here, (i ^ 1) * cols + j if across is None else i * cols + across))
    return row_even, row_odd, col_even, col_odd


def lane_take(values, index):
    return jnp.take_along_axis(values, index, axis=1, mode="promise_in_bounds")


def lane_ids():
    return lax.broadcasted_iota(jnp.int32, (sublanes, lanes), 1)


def pack(states, send_table_ref, out_refs, groups, slots):
    group = lane_ids() // slots
    fields = len(states[0])
    packed = [[None] * fields for _ in range(4)]
    for m in range(groups):
        index = send_table_ref[pl.ds(m * sublanes, sublanes), :]
        for f in range(fields):
            taken = lane_take(states[m][f], index)
            for b in range(4):
                before = packed[b][f]
                packed[b][f] = (
                    taken
                    if before is None
                    else jnp.where(group == (m + b) % groups, taken, before)
                )
    for b in range(4):
        for f in range(fields):
            out_refs[b][f] = packed[b][f]


def prepare_kernel(send_ref, q_ref, send_table_ref, *out_refs):
    fields, vectors, cells = q_ref.shape
    slots = send_ref.shape[1]
    groups = lanes // slots
    shape = (sublanes, lanes)
    row_even = lax.axis_index("gx") % 2 == 0
    col_even = lax.axis_index("gy") % 2 == 0
    sends = jnp.concatenate(
        [send_ref[...], jnp.zeros((4, lanes - slots), jnp.int32)], axis=1
    )
    spread = [jnp.broadcast_to(sends[b : b + 1], shape) for b in range(4)]
    ordered = [
        jnp.where(row_even, spread[1], spread[0]),
        jnp.where(row_even, spread[0], spread[1]),
        jnp.where(col_even, spread[3], spread[2]),
        jnp.where(col_even, spread[2], spread[3]),
    ]
    base = ordered[0]
    for b in range(1, 4):
        base = jnp.where(lane_ids() // slots == b, pltpu.roll(ordered[b], b * slots, 1), base)
    for m in range(groups):
        send_table_ref[pl.ds(m * sublanes, sublanes), :] = (
            pltpu.roll(base, m * slots, 1) if m else base
        )
    states = [
        [q_ref[f, pl.ds(m * sublanes, sublanes), :] for f in range(fields)] for m in range(groups)
    ]
    pack(states, send_table_ref, out_refs, groups, slots)


def tables_kernel(
    slots,
    count_ref,
    jac_ref,
    conn_ref,
    speed_ref,
    visc_ref,
    volume_ref,
    weight_ref,
    entry_ref,
    ghost_ref,
    splat_ref,
):
    cells = conn_ref.shape[1]
    fields = jac_ref.shape[1]
    shape = (sublanes, lanes)
    groups = lanes // slots
    row_swap = jnp.where(lax.axis_index("gx") % 2 == 0, slots, 0)
    col_swap = jnp.where(lax.axis_index("gy") % 2 == 0, slots, 0)
    volume = jnp.broadcast_to(volume_ref[...], shape)
    weight_ref[0] = -0.5 * jnp.broadcast_to(speed_ref[...], shape) * volume
    weight_ref[1] = jnp.broadcast_to(visc_ref[...], shape) * volume
    weight_ref[2] = jnp.where(lane_ids() < jnp.broadcast_to(count_ref[...], shape), 1.0, 0.0)
    for face in range(4):
        entry = jnp.broadcast_to(conn_ref[pl.ds(face, 1), :], shape)
        entry_ref[face] = entry
        ghost = entry - cells
        ghost = jnp.where(
            ghost < 2 * slots,
            jnp.bitwise_xor(ghost, row_swap),
            jnp.where(ghost < 4 * slots, jnp.bitwise_xor(ghost, col_swap), ghost),
        )
        for m in range(groups):
            ghost_ref[face, pl.ds(m * sublanes, sublanes), :] = jnp.bitwise_and(
                ghost + m * slots, lanes - 1
            )
        for j in range(fields):
            splat_ref[pl.ds((face * fields + j) * fields, fields), :] = jnp.broadcast_to(
                jac_ref[face, :, pl.ds(j, 1)], (fields, lanes)
            )


def stage_kernel(
    stage,
    chunk,
    weight_ref,
    entry_ref,
    ghost_ref,
    splat_ref,
    send_table_ref,
    q_ref,
    *refs,
):
    refs = list(refs)
    state_ref = q_ref if stage == 0 else refs.pop(0)
    acc_ref = q_ref if stage == 0 else refs.pop(0)
    recv_refs = [refs.pop(0) for _ in range(4)]
    fields, vectors, cells = q_ref.shape
    groups = vectors // sublanes
    slots = lanes // groups
    group = lane_ids() // slots

    def tall(value):
        return value if chunk == 1 else jnp.concatenate([value] * chunk, axis=0)

    advect = tall(weight_ref[0])
    diffuse = tall(weight_ref[1])
    last = stage == 3
    kept_coef = time_step / 6.0 if stage in (0, 3) else time_step / 3.0
    next_coef = (0.5 * time_step, 0.5 * time_step, time_step, None)[stage]
    if last:
        advanced_ref, gram_ref = refs
        live = tall(weight_ref[2]) > 0.5
    else:
        next_ref, next_acc_ref, *out_refs = refs
    states = []
    zero = jnp.zeros((sublanes, lanes), jnp.float32)
    for start in range(0, groups, chunk):
        rows = pl.ds(start * sublanes, chunk * sublanes)
        own = [state_ref[f, rows, :] for f in range(fields)]
        ghosts = []
        for f in range(fields):
            parts = []
            for m in range(start, start + chunk):
                block = zero
                for b in range(4):
                    block = jnp.where(group == (m + b) % groups, recv_refs[b][f], block)
                parts.append(block)
            ghosts.append(jnp.concatenate(parts, axis=0))
        advection = [None] * fields
        diffusion = [-4.0 * own[f] for f in range(fields)]
        for face in range(4):
            entry = tall(entry_ref[face])
            outside = entry >= cells
            inside_index = jnp.bitwise_and(entry, lanes - 1)
            outside_index = ghost_ref[face, rows, :]
            for j in range(fields):
                near = jnp.where(
                    outside,
                    lane_take(ghosts[j], outside_index),
                    lane_take(own[j], inside_index),
                )
                diffusion[j] = diffusion[j] + near
                for i in range(fields):
                    at = (face * fields + j) * fields + i
                    term = splat_ref[pl.ds(at, 1), :] * near
                    advection[i] = term if advection[i] is None else advection[i] + term
        following = []
        for f in range(fields):
            slope = advect * advection[f] + diffuse * diffusion[f]
            kept = acc_ref[f, rows, :] + kept_coef * slope
            if last:
                advanced_ref[f, rows, :] = jnp.where(live, kept, 0.0)
            else:
                next_acc_ref[f, rows, :] = kept
                after = q_ref[f, rows, :] + next_coef * slope
                next_ref[f, rows, :] = after
                following.append(after)
        if not last:
            for m in range(chunk):
                states.append([x[m * sublanes : (m + 1) * sublanes] for x in following])
    if not last:
        pack(states, send_table_ref, out_refs, groups, slots)
        return
    half = vectors // 2
    wide = jnp.concatenate([advanced_ref[f] for f in range(fields)], axis=1)
    gram = lax.dot_general(
        wide,
        jnp.concatenate([wide, jnp.zeros_like(wide)], axis=0),
        (((1,), (1,)), ((), ())),
        precision=HIGHEST,
        preferred_element_type=jnp.float32,
    )
    gram_ref[...] = gram[:half] + pltpu.roll(gram[half:], vectors, 1)


def factor_kernel(scale, gram_ref, advanced_ref, basis_ref, factor_ref):
    fields, vectors, cells = advanced_ref.shape
    half = vectors // 2
    folded = gram_ref[...] * scale
    turned = pltpu.roll(folded, vectors, 1)
    work = jnp.concatenate([folded, turned], axis=0)
    row = lax.broadcasted_iota(jnp.int32, (vectors, lanes), 0)
    lane = lax.broadcasted_iota(jnp.int32, (vectors, lanes), 1)
    work = jnp.where(lane < vectors, work, jnp.where(lane == row + vectors, 1.0, 0.0))
    blocks = [work[b * sublanes : (b + 1) * sublanes] for b in range(vectors // sublanes)]
    sub = lax.broadcasted_iota(jnp.int32, (sublanes, lanes), 0)
    scales = []
    for b in range(len(blocks)):
        start = b * sublanes
        count = len(blocks) - b
        columns = [
            [
                jnp.broadcast_to(blocks[c][:, start + k : start + k + 1], (sublanes, lanes))
                for c in range(b, len(blocks))
            ]
            for k in range(sublanes)
        ]
        for k in range(sublanes):
            pivot = jnp.broadcast_to(columns[k][0][k : k + 1], (sublanes, lanes))
            scales.append(pivot)
            inverse = 1.0 / pivot
            row_k = jnp.broadcast_to(blocks[b][k : k + 1], (sublanes, lanes)) * inverse
            later = [
                jnp.broadcast_to(columns[n][0][k : k + 1], (sublanes, lanes)) * inverse
                for n in range(k + 1, sublanes)
            ]
            for c in range(count):
                ratio = columns[k][c]
                if c == 0:
                    ratio = jnp.where(sub > k, ratio, 0.0)
                blocks[b + c] = blocks[b + c] - ratio * row_k
                for n in range(k + 1, sublanes):
                    columns[n][c] = columns[n][c] - ratio * later[n - k - 1]
    for b in range(len(blocks)):
        pivots = scales[b * sublanes]
        for k in range(1, sublanes):
            pivots = jnp.where(sub == k, scales[b * sublanes + k], pivots)
        blocks[b] = blocks[b] * lax.rsqrt(pivots)
    done = jnp.concatenate(blocks, axis=0)
    factor_ref[...] = jnp.where(lane >= row, done, 0.0)[:, :vectors]
    inverse_lower = pltpu.roll(done, vectors, 1)[:, :vectors]
    for f in range(fields):
        basis_ref[f] = jnp.dot(
            inverse_lower,
            advanced_ref[f],
            precision=HIGHEST,
            preferred_element_type=jnp.float32,
        )


def summed(value, rows, cols):
    steps = [(1, 0)]
    step = 2
    while step < rows:
        steps.append((step + 1, 0))
        step *= 2
    step = 1
    while step < cols:
        steps.append((1, step))
        step *= 2
    for across, along in steps:
        pairs = [
            (i * cols + j, (i ^ across) * cols + (j ^ along))
            for i in range(rows)
            for j in range(cols)
        ]
        value = value + lax.ppermute(value, ("gx", "gy"), pairs)
    return value


def shards(
    mesh_shape,
    test_vectors,
    face_jacobians,
    wave_speed,
    viscosity,
    inverse_volume,
    connectivity,
    send_rows,
    cell_count,
):
    rows, cols = mesh_shape
    fields, vectors, cells = test_vectors.shape
    slots = send_rows.shape[1]
    groups = vectors // sublanes
    assert cells == lanes and groups * slots == lanes and 2 * vectors == lanes
    vmem = pl.BlockSpec(memory_space=pltpu.VMEM)
    speed = wave_speed.reshape(1, cells)
    visc = viscosity.reshape(1, cells)
    volume = inverse_volume.reshape(1, cells)
    state = jax.ShapeDtypeStruct(test_vectors.shape, jnp.float32)
    block = jax.ShapeDtypeStruct((fields, sublanes, lanes), jnp.float32)
    tables = [
        jax.ShapeDtypeStruct((3, sublanes, lanes), jnp.float32),
        jax.ShapeDtypeStruct((4, sublanes, lanes), jnp.int32),
        jax.ShapeDtypeStruct((4, vectors, lanes), jnp.int32),
        jax.ShapeDtypeStruct((4 * fields * fields, lanes), jnp.float32),
    ]
    params = pltpu.CompilerParams(vmem_limit_bytes=16 * 1024 * 1024)
    pairs = matchings(rows, cols)

    def exchange(sent):
        got = [None] * 4
        for which in (0, 3, 2, 1):
            got[which] = lax.ppermute(sent[which], ("gx", "gy"), pairs[which])
        return got

    send_table, *sent = pl.pallas_call(
        prepare_kernel,
        out_shape=[jax.ShapeDtypeStruct((vectors, lanes), jnp.int32)] + [block] * 4,
        in_specs=[vmem] * 2,
        out_specs=[vmem] * 5,
        compiler_params=params,
        name="prepare",
    )(send_rows, test_vectors)
    tables = pl.pallas_call(
        functools.partial(tables_kernel, slots),
        out_shape=tables,
        in_specs=[vmem] * 6,
        out_specs=[vmem] * 4,
        compiler_params=params,
        name="tables",
    )(cell_count.reshape(1, 1), face_jacobians, connectivity, speed, visc, volume)
    held = []
    for stage in range(4):
        got = exchange(sent)
        last = stage == 3
        gram_shape = jax.ShapeDtypeStruct((vectors // 2, lanes), jnp.float32)
        result = pl.pallas_call(
            functools.partial(stage_kernel, stage, 1),
            out_shape=[state, gram_shape] if last else [state, state] + [block] * 4,
            in_specs=[vmem] * (6 + len(held) + 4),
            out_specs=[vmem] * (2 if last else 6),
            compiler_params=params,
            name="stage",
        )(*tables, send_table, test_vectors, *held, *got)
        held, sent = result[:2], result[2:]
    advanced, gram = held
    gram = summed(gram, rows, cols)
    scale = 1.0 / float(fields * cells * rows * cols)
    return pl.pallas_call(
        functools.partial(factor_kernel, scale),
        out_shape=[state, jax.ShapeDtypeStruct((vectors, vectors), jnp.float32)],
        in_specs=[vmem] * 2,
        out_specs=[vmem] * 2,
        compiler_params=params,
        name="factor",
    )(gram, advanced)


def solution(mesh):
    placed = (
        P(None, None, ("gx", "gy")),
        P(),
        P(("gx", "gy")),
        P(("gx", "gy")),
        P(("gx", "gy")),
        P(None, ("gx", "gy")),
        P(None, ("gx", "gy")),
        P(("gx", "gy")),
    )
    return jax.shard_map(
        functools.partial(shards, (mesh.shape["gx"], mesh.shape["gy"])),
        mesh=mesh,
        in_specs=placed,
        out_specs=(P(None, None, ("gx", "gy")), P()),
        check_vma=False,
    )
```

time: 52.7 us -> 48.1 us (0.913)
  Pallas kernels: 10.8 us -> 7.14 us
  starting transfers between devices: 23.7 us -> 22.8 us
    pallas_call x5 -> x6, Pallas kernels: 7.99 us -> 4.32 us  [the longest x4 3.95 us: shards(): pl.pallas_call(functools.partial(stage_kernel, stage, 1), out_shape=[stat...]
    ppermute x7 -> x5, starting transfers between devices: 7.99 us -> 7.15 us  [summed(): value = value + lax.ppermute(value, ('gx', 'gy'), pairs)]
    ppermute x7 -> x5, waiting for transfers between devices: 7.46 us -> 8.22 us  [summed(): value = value + lax.ppermute(value, ('gx', 'gy'), pairs)]
    ppermute x16, waiting for transfers between devices: 6.72 us -> 5.99 us  [exchange(): got[which] = lax.ppermute(sent[which], ('gx', 'gy'), pairs[which])]
  transfers between devices with their start and end apart: 23 -> 21, of which waited for: 13 -> 12; matrix products, arithmetic and copies ran while one was open for 0% -> 0% of each run, Pallas kernels for 0% -> 0%
where the time goes in v2:
time: 48.1 us; the launch traced here: 47.9 us
  starting transfers between devices  22.8 us (47%)
  waiting for transfers between devices  14.2 us (30%)
  Pallas kernels  7.14 us (15%)
  local copies, waits for them, and re-layouts  2.27 us (5%)
  between operations  1.42 us (3%)
    ppermute x16, starting transfers between devices, exchange(): got[which] = lax.ppermute(sent[which], ('gx', 'gy'), pairs[which])  15.7 us
    ppermute x5, waiting for transfers between devices, summed(): value = value + lax.ppermute(value, ('gx', 'gy'), pairs)  8.22 us
    ppermute x5, starting transfers between devices, summed(): value = value + lax.ppermute(value, ('gx', 'gy'), pairs)  7.15 us
    ppermute x16, waiting for transfers between devices, exchange(): got[which] = lax.ppermute(sent[which], ('gx', 'gy'), pairs[which])  5.99 us
    pallas_call x4, Pallas kernels, shards(): pl.pallas_call(functools.partial(stage_kernel, stage, 1), out_shape=[stat...  3.95 us
    pallas_call x1, Pallas kernels, shards(): pl.pallas_call(functools.partial(factor_kernel, scale), out_shape=[state,...  2.82 us
    unnamed x17, local copies, waits for them, and re-layouts  2.27 us
  transfers between devices with their start and end apart: 21, of which 12 were waited for; matrix products, arithmetic and copies ran while one was open for 0% of the time, Pallas kernels for 0%

profile of v2, /device:TPU:0, one launch (start us, length us, event | category | flops | bytes accessed | tf_op | source)
XLA Modules:
  0.0 47.9 jit_solution(6390935673406421533)
XLA Ops:
  0.6 0.9 %copy-done = f32[5,64,128]{2,1,0:T(8,128)S(1)} copy-done((f32[5,64,128]{2,1,0:T(8,128)S(1)}, f32[5,64,128]{2,1,0:T(8,128)}, u32[]{:S(2)}) %copy-start) | copy-done | bytes 163864
  1.5 0.7 %copy-done.3 = s32[4,16]{1,0:T(4,128)S(1)} copy-done((s32[4,16]{1,0:T(4,128)S(1)}, s32[4,16]{1,0:T(4,128)}, u32[]{:S(2)}) %copy-start.3) | copy-done | bytes 280
  2.5 0.5 %collective-permute-start = (f32[5,8,128]{2,1,0:T(8,128)S(1)}, f32[5,8,128]{2,1,0:T(8,128)S(1)}, u32[]{:S(2)}, u32[]{:S(2)}) collective-permute-start(f32[5,8,128]{2,1,0:T(8,128)S(1)} %get-tuple-element.36), channel_id=1, source_target_pairs={{0,4},{1,5},{2,6},{3,7},{4,0},{5,1},{6,2},{7,3},{8,12},{9,13},{10,... | collective-permute-start | bytes 61448 | tf_op jit(solution)/shard_map/ppermute | solution.py:338
  3.0 3.6 %collective-permute-start.1 = (f32[5,8,128]{2,1,0:T(8,128)S(1)}, f32[5,8,128]{2,1,0:T(8,128)S(1)}, u32[]{:S(2)}, u32[]{:S(2)}) collective-permute-start(f32[5,8,128]{2,1,0:T(8,128)S(1)} %get-tuple-element.37), channel_id=1, source_target_pairs={{0,28},{1,29},{2,30},{3,31},{4,8},{5,9},{6,10},{7,11},{8,4},{9,5},... | collective-permute-start | bytes 61448 | tf_op jit(solution)/shard_map/ppermute | solution.py:338
  6.6 1.6 %collective-permute-start.2 = (f32[5,8,128]{2,1,0:T(8,128)S(1)}, f32[5,8,128]{2,1,0:T(8,128)S(1)}, u32[]{:S(2)}, u32[]{:S(2)}) collective-permute-start(f32[5,8,128]{2,1,0:T(8,128)S(1)} %get-tuple-element.38), channel_id=1, source_target_pairs={{0,1},{1,0},{2,3},{3,2},{4,5},{5,4},{6,7},{7,6},{8,9},{9,8},{10,11... | collective-permute-start | bytes 61448 | tf_op jit(solution)/shard_map/ppermute | solution.py:338
  8.9 0.6 %copy-done.2 = s32[4,128]{1,0:T(4,128)S(1)} copy-done((s32[4,128]{1,0:T(4,128)S(1)}, s32[4,128]{1,0:T(4,128)}, u32[]{:S(2)}) %copy-start.2) | copy-done | bytes 2072
  9.7 0.7 %collective-permute-done.2.refs_2_ = f32[5,8,128]{2,1,0:T(8,128)S(1)} collective-permute-done((f32[5,8,128]{2,1,0:T(8,128)S(1)}, f32[5,8,128]{2,1,0:T(8,128)S(1)}, u32[]{:S(2)}, u32[]{:S(2)}) %collective-permute-start.2) | collective-permute-done | bytes 20512 | tf_op jit(solution)/shard_map/ppermute | solution.py:338
  10.4 0.9 %stage.4 = (f32[5,64,128]{2,1,0:T(8,128)S(1)}, f32[5,64,128]{2,1,0:T(8,128)S(1)}, f32[5,8,128]{2,1,0:T(8,128)S(1)}, f32[5,8,128]{2,1,0:T(8,128)S(1)}, f32[5,8,12...) custom-call(f32[3,8,128]{2,1,0:T(8,128)S(1)} %get-tuple-element.31.weight_ref, s32[4,8,128]{2,1,0:T(8,128)S(1)} %get-tuple-element.32.entry_ref, ...), custom_call_target="tpu_custom_call" | custom-call | tf_op jit(solution)/shard_map/stage/pallas_call | solution.py:362
  11.3 0.6 %collective-permute-start.5 = (f32[5,8,128]{2,1,0:T(8,128)S(1)}, f32[5,8,128]{2,1,0:T(8,128)S(1)}, u32[]{:S(2)}, u32[]{:S(2)}) collective-permute-start(f32[5,8,128]{2,1,0:T(8,128)S(1)} %get-tuple-element.43), channel_id=1, source_target_pairs={{0,28},{1,29},{2,30},{3,31},{4,8},{5,9},{6,10},{7,11},{8,4},{9,5},... | collective-permute-start | bytes 61448 | tf_op jit(solution)/shard_map/ppermute | solution.py:338
  12.0 2.7 %collective-permute-start.6 = (f32[5,8,128]{2,1,0:T(8,128)S(1)}, f32[5,8,128]{2,1,0:T(8,128)S(1)}, u32[]{:S(2)}, u32[]{:S(2)}) collective-permute-start(f32[5,8,128]{2,1,0:T(8,128)S(1)} %get-tuple-element.44), channel_id=1, source_target_pairs={{0,1},{1,0},{2,3},{3,2},{4,5},{5,4},{6,7},{7,6},{8,9},{9,8},{10,11... | collective-permute-start | bytes 61448 | tf_op jit(solution)/shard_map/ppermute | solution.py:338
  14.7 0.8 %collective-permute-done.5.refs_3_ = f32[5,8,128]{2,1,0:T(8,128)S(1)} collective-permute-done((f32[5,8,128]{2,1,0:T(8,128)S(1)}, f32[5,8,128]{2,1,0:T(8,128)S(1)}, u32[]{:S(2)}, u32[]{:S(2)}) %collective-permute-start.5) | collective-permute-done | bytes 20512 | tf_op jit(solution)/shard_map/ppermute | solution.py:338
  15.5 0.9 %collective-permute-done.6.refs_4_ = f32[5,8,128]{2,1,0:T(8,128)S(1)} collective-permute-done((f32[5,8,128]{2,1,0:T(8,128)S(1)}, f32[5,8,128]{2,1,0:T(8,128)S(1)}, u32[]{:S(2)}, u32[]{:S(2)}) %collective-permute-start.6) | collective-permute-done | bytes 20512 | tf_op jit(solution)/shard_map/ppermute | solution.py:338
  16.4 0.9 %stage.5 = (f32[5,64,128]{2,1,0:T(8,128)S(1)}, f32[5,64,128]{2,1,0:T(8,128)S(1)}, f32[5,8,128]{2,1,0:T(8,128)S(1)}, f32[5,8,128]{2,1,0:T(8,128)S(1)}, f32[5,8,12...) custom-call(f32[3,8,128]{2,1,0:T(8,128)S(1)} %get-tuple-element.31.weight_ref, s32[4,8,128]{2,1,0:T(8,128)S(1)} %get-tuple-element.32.entry_ref, ...), custom_call_target="tpu_custom_call" | custom-call | tf_op jit(solution)/shard_map/stage/pallas_call | solution.py:362
  17.4 1.5 %collective-permute-start.9 = (f32[5,8,128]{2,1,0:T(8,128)S(1)}, f32[5,8,128]{2,1,0:T(8,128)S(1)}, u32[]{:S(2)}, u32[]{:S(2)}) collective-permute-start(f32[5,8,128]{2,1,0:T(8,128)S(1)} %get-tuple-element.49), channel_id=1, source_target_pairs={{0,28},{1,29},{2,30},{3,31},{4,8},{5,9},{6,10},{7,11},{8,4},{9,5},... | collective-permute-start | bytes 61448 | tf_op jit(solution)/shard_map/ppermute | solution.py:338
  18.9 2.2 %collective-permute-start.10 = (f32[5,8,128]{2,1,0:T(8,128)S(1)}, f32[5,8,128]{2,1,0:T(8,128)S(1)}, u32[]{:S(2)}, u32[]{:S(2)}) collective-permute-start(f32[5,8,128]{2,1,0:T(8,128)S(1)} %get-tuple-element.50), channel_id=1, source_target_pairs={{0,1},{1,0},{2,3},{3,2},{4,5},{5,4},{6,7},{7,6},{8,9},{9,8},{10,11... | collective-permute-start | bytes 61448 | tf_op jit(solution)/shard_map/ppermute | solution.py:338
  21.1 0.5 %collective-permute-done.9.refs_3_ = f32[5,8,128]{2,1,0:T(8,128)S(1)} collective-permute-done((f32[5,8,128]{2,1,0:T(8,128)S(1)}, f32[5,8,128]{2,1,0:T(8,128)S(1)}, u32[]{:S(2)}, u32[]{:S(2)}) %collective-permute-start.9) | collective-permute-done | bytes 20512 | tf_op jit(solution)/shard_map/ppermute | solution.py:338
  21.6 1.3 %collective-permute-done.10.refs_4_ = f32[5,8,128]{2,1,0:T(8,128)S(1)} collective-permute-done((f32[5,8,128]{2,1,0:T(8,128)S(1)}, f32[5,8,128]{2,1,0:T(8,128)S(1)}, u32[]{:S(2)}, u32[]{:S(2)}) %collective-permute-start.10) | collective-permute-done | bytes 20512 | tf_op jit(solution)/shard_map/ppermute | solution.py:338
  22.9 0.9 %stage.6 = (f32[5,64,128]{2,1,0:T(8,128)S(1)}, f32[5,64,128]{2,1,0:T(8,128)S(1)}, f32[5,8,128]{2,1,0:T(8,128)S(1)}, f32[5,8,128]{2,1,0:T(8,128)S(1)}, f32[5,8,12...) custom-call(f32[3,8,128]{2,1,0:T(8,128)S(1)} %get-tuple-element.31.weight_ref, s32[4,8,128]{2,1,0:T(8,128)S(1)} %get-tuple-element.32.entry_ref, ...), custom_call_target="tpu_custom_call" | custom-call | tf_op jit(solution)/shard_map/stage/pallas_call | solution.py:362
  23.8 0.7 %collective-permute-start.13 = (f32[5,8,128]{2,1,0:T(8,128)S(1)}, f32[5,8,128]{2,1,0:T(8,128)S(1)}, u32[]{:S(2)}, u32[]{:S(2)}) collective-permute-start(f32[5,8,128]{2,1,0:T(8,128)S(1)} %get-tuple-element.55), channel_id=1, source_target_pairs={{0,28},{1,29},{2,30},{3,31},{4,8},{5,9},{6,10},{7,11},{8,4},{9,5},... | collective-permute-start | bytes 61448 | tf_op jit(solution)/shard_map/ppermute | solution.py:338
  24.5 2.1 %collective-permute-start.14 = (f32[5,8,128]{2,1,0:T(8,128)S(1)}, f32[5,8,128]{2,1,0:T(8,128)S(1)}, u32[]{:S(2)}, u32[]{:S(2)}) collective-permute-start(f32[5,8,128]{2,1,0:T(8,128)S(1)} %get-tuple-element.56), channel_id=1, source_target_pairs={{0,1},{1,0},{2,3},{3,2},{4,5},{5,4},{6,7},{7,6},{8,9},{9,8},{10,11... | collective-permute-start | bytes 61448 | tf_op jit(solution)/shard_map/ppermute | solution.py:338
  26.6 1.4 %collective-permute-done.13.refs_3_ = f32[5,8,128]{2,1,0:T(8,128)S(1)} collective-permute-done((f32[5,8,128]{2,1,0:T(8,128)S(1)}, f32[5,8,128]{2,1,0:T(8,128)S(1)}, u32[]{:S(2)}, u32[]{:S(2)}) %collective-permute-start.13) | collective-permute-done | bytes 20512 | tf_op jit(solution)/shard_map/ppermute | solution.py:338
  28.4 1.3 %stage.7 = (f32[5,64,128]{2,1,0:T(8,128)S(1)}, f32[32,128]{1,0:T(8,128)S(1)}) custom-call(f32[3,8,128]{2,1,0:T(8,128)S(1)} %get-tuple-element.31.weight_ref, s32[4,8,128]{2,1,0:T(8,128)S(1)} %get-tuple-element.32.entry_ref, s32[4,64,128]{2,1,0:T(8,128)S(1)} %get-tuple-element.33.ghost_ref, f32[100,128]{1,0:T(8,128)S(1)} %get-tuple-element.34.splat_ref, ...), custom_call_target="tpu_custom_call" | custom-call | tf_op jit(solution)/shard_map/stage/pallas_call | solution.py:362
  29.7 1.2 %collective-permute-done.16 = f32[32,128]{1,0:T(8,128)S(1)} collective-permute-done((f32[32,128]{1,0:T(8,128)S(1)}, f32[32,128]{1,0:T(8,128)S(1)}, u32[]{:S(2)}, u32[]{:S(2)}) %collective-permute-start.16) | collective-permute-done | bytes 16416 | tf_op jit(solution)/shard_map/ppermute | solution.py:300
  30.9 1.2 %collective-permute-start.17 = (f32[32,128]{1,0:T(8,128)S(1)}, f32[32,128]{1,0:T(8,128)S(1)}, u32[]{:S(2)}, u32[]{:S(2)}) collective-permute-start(f32[32,128]{1,0:T(8,128)S(1)} %add.15), channel_id=1, source_target_pairs={{0,12},{1,13},{2,14},{3,15},{4,8},{5,9},{6,10},{7,11},{8,4},{9,5},... | collective-permute-start | bytes 49160 | tf_op jit(solution)/shard_map/ppermute | solution.py:300
  32.0 2.0 %collective-permute-done.17 = f32[32,128]{1,0:T(8,128)S(1)} collective-permute-done((f32[32,128]{1,0:T(8,128)S(1)}, f32[32,128]{1,0:T(8,128)S(1)}, u32[]{:S(2)}, u32[]{:S(2)}) %collective-permute-start.17) | collective-permute-done | bytes 16416 | tf_op jit(solution)/shard_map/ppermute | solution.py:300
  34.0 1.0 %collective-permute-start.18 = (f32[32,128]{1,0:T(8,128)S(1)}, f32[32,128]{1,0:T(8,128)S(1)}, u32[]{:S(2)}, u32[]{:S(2)}) collective-permute-start(f32[32,128]{1,0:T(8,128)S(1)} %add.16), channel_id=1, source_target_pairs={{0,20},{1,21},{2,22},{3,23},{4,16},{5,17},{6,18},{7,19},{8,28},{9,... | collective-permute-start | bytes 49160 | tf_op jit(solution)/shard_map/ppermute | solution.py:300
  35.0 2.2 %collective-permute-done.18 = f32[32,128]{1,0:T(8,128)S(1)} collective-permute-done((f32[32,128]{1,0:T(8,128)S(1)}, f32[32,128]{1,0:T(8,128)S(1)}, u32[]{:S(2)}, u32[]{:S(2)}) %collective-permute-start.18) | collective-permute-done | bytes 16416 | tf_op jit(solution)/shard_map/ppermute | solution.py:300
  37.2 1.8 %collective-permute-start.19 = (f32[32,128]{1,0:T(8,128)S(1)}, f32[32,128]{1,0:T(8,128)S(1)}, u32[]{:S(2)}, u32[]{:S(2)}) collective-permute-start(f32[32,128]{1,0:T(8,128)S(1)} %add.17), channel_id=1, source_target_pairs={{0,5},{1,4},{2,7},{3,6},{4,1},{5,0},{6,3},{7,2},{8,13},{9,12},{10,... | collective-permute-start | bytes 49160 | tf_op jit(solution)/shard_map/ppermute | solution.py:300
  39.0 1.4 %collective-permute-done.19 = f32[32,128]{1,0:T(8,128)S(1)} collective-permute-done((f32[32,128]{1,0:T(8,128)S(1)}, f32[32,128]{1,0:T(8,128)S(1)}, u32[]{:S(2)}, u32[]{:S(2)}) %collective-permute-start.19) | collective-permute-done | bytes 16416 | tf_op jit(solution)/shard_map/ppermute | solution.py:300
  40.4 3.2 %collective-permute-start.20 = (f32[32,128]{1,0:T(8,128)S(1)}, f32[32,128]{1,0:T(8,128)S(1)}, u32[]{:S(2)}, u32[]{:S(2)}) collective-permute-start(f32[32,128]{1,0:T(8,128)S(1)} %add.18), channel_id=1, source_target_pairs={{0,6},{1,7},{2,4},{3,5},{4,2},{5,3},{6,0},{7,1},{8,14},{9,15},{10,... | collective-permute-start | bytes 49160 | tf_op jit(solution)/shard_map/ppermute | solution.py:300
  43.6 1.4 %collective-permute-done.20 = f32[32,128]{1,0:T(8,128)S(1)} collective-permute-done((f32[32,128]{1,0:T(8,128)S(1)}, f32[32,128]{1,0:T(8,128)S(1)}, u32[]{:S(2)}, u32[]{:S(2)}) %collective-permute-start.20) | collective-permute-done | bytes 16416 | tf_op jit(solution)/shard_map/ppermute | solution.py:300
  45.1 2.8 %factor.1 = (f32[5,64,128]{2,1,0:T(8,128)}, f32[64,64]{1,0:T(8,128)}) custom-call(f32[32,128]{1,0:T(8,128)S(1)} %add.19.gram_ref, f32[5,64,128]{2,1,0:T(8,128)S(1)} %get-tuple-element.59.advanced_ref), custom_call_target="tpu_custom_call" | custom-call | tf_op jit(solution)/shard_map/factor/pallas_call | solution.py:374
  (39 shorter events, 1.1 us)
Async XLA Ops:
  0.6 0.9 %copy-start = (f32[5,64,128]{2,1,0:T(8,128)S(1)}, f32[5,64,128]{2,1,0:T(8,128)}, u32[]{:S(2)}) copy-start(f32[5,64,128]{2,1,0:T(8,128)} %q_ref.9) | copy-start | bytes 491524
  1.5 0.7 %copy-start.3 = (s32[4,16]{1,0:T(4,128)S(1)}, s32[4,16]{1,0:T(4,128)}, u32[]{:S(2)}) copy-start(s32[4,16]{1,0:T(4,128)} %send_ref.1) | copy-start | bytes 772
  2.2 6.6 %copy-start.7 = (f32[4,5,5]{2,0,1:T(4,128)S(1)}, f32[4,5,5]{2,0,1:T(4,128)}, u32[]{:S(2)}) copy-start(f32[4,5,5]{2,0,1:T(4,128)} %param.9) | copy-start | bytes 1204
  2.2 8.1 %copy-start.1 = (f32[5,64,128]{2,1,0:T(8,128)S(1)}, f32[5,64,128]{2,1,0:T(8,128)}, u32[]{:S(2)}) copy-start(f32[5,64,128]{2,1,0:T(8,128)} %q_ref.9) | copy-start | bytes 491524
  2.5 7.1 %collective-permute-start = (f32[5,8,128]{2,1,0:T(8,128)S(1)}, f32[5,8,128]{2,1,0:T(8,128)S(1)}, u32[]{:S(2)}, u32[]{:S(2)}) collective-permute-start(f32[5,8,128]{2,1,0:T(8,128)S(1)} %get-tuple-element.36), channel_id=1, source_target_pairs={{0,4},{1,5},{2,6},{3,7},{4,0},{5,1},{6,2},{7,3},{8,12},{9,13},{10,... | collective-permute-start | bytes 61448 | tf_op jit(solution)/shard_map/ppermute | solution.py:338
  3.0 6.6 %collective-permute-start.1 = (f32[5,8,128]{2,1,0:T(8,128)S(1)}, f32[5,8,128]{2,1,0:T(8,128)S(1)}, u32[]{:S(2)}, u32[]{:S(2)}) collective-permute-start(f32[5,8,128]{2,1,0:T(8,128)S(1)} %get-tuple-element.37), channel_id=1, source_target_pairs={{0,28},{1,29},{2,30},{3,31},{4,8},{5,9},{6,10},{7,11},{8,4},{9,5},... | collective-permute-start | bytes 61448 | tf_op jit(solution)/shard_map/ppermute | solution.py:338
  6.6 3.8 %collective-permute-start.2 = (f32[5,8,128]{2,1,0:T(8,128)S(1)}, f32[5,8,128]{2,1,0:T(8,128)S(1)}, u32[]{:S(2)}, u32[]{:S(2)}) collective-permute-start(f32[5,8,128]{2,1,0:T(8,128)S(1)} %get-tuple-element.38), channel_id=1, source_target_pairs={{0,1},{1,0},{2,3},{3,2},{4,5},{5,4},{6,7},{7,6},{8,9},{9,8},{10,11... | collective-permute-start | bytes 61448 | tf_op jit(solution)/shard_map/ppermute | solution.py:338
  8.2 2.2 %collective-permute-start.3 = (f32[5,8,128]{2,1,0:T(8,128)S(1)}, f32[5,8,128]{2,1,0:T(8,128)S(1)}, u32[]{:S(2)}, u32[]{:S(2)}) collective-permute-start(f32[5,8,128]{2,1,0:T(8,128)S(1)} %get-tuple-element.39), channel_id=1, source_target_pairs={{0,4},{1,2},{2,1},{3,7},{4,0},{5,6},{6,5},{7,3},{8,12},{9,10},{10,... | collective-permute-start | bytes 61448 | tf_op jit(solution)/shard_map/ppermute | solution.py:338
  8.8 0.7 %copy-start.2 = (s32[4,128]{1,0:T(4,128)S(1)}, s32[4,128]{1,0:T(4,128)}, u32[]{:S(2)}) copy-start(s32[4,128]{1,0:T(4,128)} %conn_ref.1) | copy-start | bytes 6148
  8.9 0.7 %copy-start.4 = (f32[128]{0:T(128)S(1)}, f32[128]{0:T(128)}, u32[]{:S(2)}) copy-start(f32[128]{0:T(128)} %param.10) | copy-start | bytes 1540
  8.9 0.7 %copy-start.5 = (f32[128]{0:T(128)S(1)}, f32[128]{0:T(128)}, u32[]{:S(2)}) copy-start(f32[128]{0:T(128)} %param.11) | copy-start | bytes 1540
  8.9 0.7 %copy-start.6 = (f32[128]{0:T(128)S(1)}, f32[128]{0:T(128)}, u32[]{:S(2)}) copy-start(f32[128]{0:T(128)} %param.12) | copy-start | bytes 1540
  11.3 3.4 %collective-permute-start.4 = (f32[5,8,128]{2,1,0:T(8,128)S(1)}, f32[5,8,128]{2,1,0:T(8,128)S(1)}, u32[]{:S(2)}, u32[]{:S(2)}) collective-permute-start(f32[5,8,128]{2,1,0:T(8,128)S(1)} %get-tuple-element.42), channel_id=1, source_target_pairs={{0,4},{1,5},{2,6},{3,7},{4,0},{5,1},{6,2},{7,3},{8,12},{9,13},{10,... | collective-permute-start | bytes 61448 | tf_op jit(solution)/shard_map/ppermute | solution.py:338
  11.3 4.2 %collective-permute-start.5 = (f32[5,8,128]{2,1,0:T(8,128)S(1)}, f32[5,8,128]{2,1,0:T(8,128)S(1)}, u32[]{:S(2)}, u32[]{:S(2)}) collective-permute-start(f32[5,8,128]{2,1,0:T(8,128)S(1)} %get-tuple-element.43), channel_id=1, source_target_pairs={{0,28},{1,29},{2,30},{3,31},{4,8},{5,9},{6,10},{7,11},{8,4},{9,5},... | collective-permute-start | bytes 61448 | tf_op jit(solution)/shard_map/ppermute | solution.py:338
  12.0 4.5 %collective-permute-start.6 = (f32[5,8,128]{2,1,0:T(8,128)S(1)}, f32[5,8,128]{2,1,0:T(8,128)S(1)}, u32[]{:S(2)}, u32[]{:S(2)}) collective-permute-start(f32[5,8,128]{2,1,0:T(8,128)S(1)} %get-tuple-element.44), channel_id=1, source_target_pairs={{0,1},{1,0},{2,3},{3,2},{4,5},{5,4},{6,7},{7,6},{8,9},{9,8},{10,11... | collective-permute-start | bytes 61448 | tf_op jit(solution)/shard_map/ppermute | solution.py:338
  14.7 1.8 %collective-permute-start.7 = (f32[5,8,128]{2,1,0:T(8,128)S(1)}, f32[5,8,128]{2,1,0:T(8,128)S(1)}, u32[]{:S(2)}, u32[]{:S(2)}) collective-permute-start(f32[5,8,128]{2,1,0:T(8,128)S(1)} %get-tuple-element.45), channel_id=1, source_target_pairs={{0,4},{1,2},{2,1},{3,7},{4,0},{5,6},{6,5},{7,3},{8,12},{9,10},{10,... | collective-permute-start | bytes 61448 | tf_op jit(solution)/shard_map/ppermute | solution.py:338
  17.3 3.8 %collective-permute-start.8 = (f32[5,8,128]{2,1,0:T(8,128)S(1)}, f32[5,8,128]{2,1,0:T(8,128)S(1)}, u32[]{:S(2)}, u32[]{:S(2)}) collective-permute-start(f32[5,8,128]{2,1,0:T(8,128)S(1)} %get-tuple-element.48), channel_id=1, source_target_pairs={{0,4},{1,5},{2,6},{3,7},{4,0},{5,1},{6,2},{7,3},{8,12},{9,13},{10,... | collective-permute-start | bytes 61448 | tf_op jit(solution)/shard_map/ppermute | solution.py:338
  17.4 4.2 %collective-permute-start.9 = (f32[5,8,128]{2,1,0:T(8,128)S(1)}, f32[5,8,128]{2,1,0:T(8,128)S(1)}, u32[]{:S(2)}, u32[]{:S(2)}) collective-permute-start(f32[5,8,128]{2,1,0:T(8,128)S(1)} %get-tuple-element.49), channel_id=1, source_target_pairs={{0,28},{1,29},{2,30},{3,31},{4,8},{5,9},{6,10},{7,11},{8,4},{9,5},... | collective-permute-start | bytes 61448 | tf_op jit(solution)/shard_map/ppermute | solution.py:338
  18.9 3.9 %collective-permute-start.10 = (f32[5,8,128]{2,1,0:T(8,128)S(1)}, f32[5,8,128]{2,1,0:T(8,128)S(1)}, u32[]{:S(2)}, u32[]{:S(2)}) collective-permute-start(f32[5,8,128]{2,1,0:T(8,128)S(1)} %get-tuple-element.50), channel_id=1, source_target_pairs={{0,1},{1,0},{2,3},{3,2},{4,5},{5,4},{6,7},{7,6},{8,9},{9,8},{10,11... | collective-permute-start | bytes 61448 | tf_op jit(solution)/shard_map/ppermute | solution.py:338
  21.1 1.8 %collective-permute-start.11 = (f32[5,8,128]{2,1,0:T(8,128)S(1)}, f32[5,8,128]{2,1,0:T(8,128)S(1)}, u32[]{:S(2)}, u32[]{:S(2)}) collective-permute-start(f32[5,8,128]{2,1,0:T(8,128)S(1)} %get-tuple-element.51), channel_id=1, source_target_pairs={{0,4},{1,2},{2,1},{3,7},{4,0},{5,6},{6,5},{7,3},{8,12},{9,10},{10,... | collective-permute-start | bytes 61448 | tf_op jit(solution)/shard_map/ppermute | solution.py:338
  23.8 2.9 %collective-permute-start.12 = (f32[5,8,128]{2,1,0:T(8,128)S(1)}, f32[5,8,128]{2,1,0:T(8,128)S(1)}, u32[]{:S(2)}, u32[]{:S(2)}) collective-permute-start(f32[5,8,128]{2,1,0:T(8,128)S(1)} %get-tuple-element.54), channel_id=1, source_target_pairs={{0,4},{1,5},{2,6},{3,7},{4,0},{5,1},{6,2},{7,3},{8,12},{9,13},{10,... | collective-permute-start | bytes 61448 | tf_op jit(solution)/shard_map/ppermute | solution.py:338
  23.8 4.2 %collective-permute-start.13 = (f32[5,8,128]{2,1,0:T(8,128)S(1)}, f32[5,8,128]{2,1,0:T(8,128)S(1)}, u32[]{:S(2)}, u32[]{:S(2)}) collective-permute-start(f32[5,8,128]{2,1,0:T(8,128)S(1)} %get-tuple-element.55), channel_id=1, source_target_pairs={{0,28},{1,29},{2,30},{3,31},{4,8},{5,9},{6,10},{7,11},{8,4},{9,5},... | collective-permute-start | bytes 61448 | tf_op jit(solution)/shard_map/ppermute | solution.py:338
  24.5 3.9 %collective-permute-start.14 = (f32[5,8,128]{2,1,0:T(8,128)S(1)}, f32[5,8,128]{2,1,0:T(8,128)S(1)}, u32[]{:S(2)}, u32[]{:S(2)}) collective-permute-start(f32[5,8,128]{2,1,0:T(8,128)S(1)} %get-tuple-element.56), channel_id=1, source_target_pairs={{0,1},{1,0},{2,3},{3,2},{4,5},{5,4},{6,7},{7,6},{8,9},{9,8},{10,11... | collective-permute-start | bytes 61448 | tf_op jit(solution)/shard_map/ppermute | solution.py:338
  26.6 1.8 %collective-permute-start.15 = (f32[5,8,128]{2,1,0:T(8,128)S(1)}, f32[5,8,128]{2,1,0:T(8,128)S(1)}, u32[]{:S(2)}, u32[]{:S(2)}) collective-permute-start(f32[5,8,128]{2,1,0:T(8,128)S(1)} %get-tuple-element.57), channel_id=1, source_target_pairs={{0,4},{1,2},{2,1},{3,7},{4,0},{5,6},{6,5},{7,3},{8,12},{9,10},{10,... | collective-permute-start | bytes 61448 | tf_op jit(solution)/shard_map/ppermute | solution.py:338
  29.7 1.2 %collective-permute-start.16 = (f32[32,128]{1,0:T(8,128)S(1)}, f32[32,128]{1,0:T(8,128)S(1)}, u32[]{:S(2)}, u32[]{:S(2)}) collective-permute-start(f32[32,128]{1,0:T(8,128)S(1)} %get-tuple-element.58), channel_id=1, source_target_pairs={{0,4},{1,5},{2,6},{3,7},{4,0},{5,1},{6,2},{7,3},{8,12},{9,13},{10,... | collective-permute-start | bytes 49160 | tf_op jit(solution)/shard_map/ppermute | solution.py:300
  30.9 3.2 %collective-permute-start.17 = (f32[32,128]{1,0:T(8,128)S(1)}, f32[32,128]{1,0:T(8,128)S(1)}, u32[]{:S(2)}, u32[]{:S(2)}) collective-permute-start(f32[32,128]{1,0:T(8,128)S(1)} %add.15), channel_id=1, source_target_pairs={{0,12},{1,13},{2,14},{3,15},{4,8},{5,9},{6,10},{7,11},{8,4},{9,5},... | collective-permute-start | bytes 49160 | tf_op jit(solution)/shard_map/ppermute | solution.py:300
  34.0 3.2 %collective-permute-start.18 = (f32[32,128]{1,0:T(8,128)S(1)}, f32[32,128]{1,0:T(8,128)S(1)}, u32[]{:S(2)}, u32[]{:S(2)}) collective-permute-start(f32[32,128]{1,0:T(8,128)S(1)} %add.16), channel_id=1, source_target_pairs={{0,20},{1,21},{2,22},{3,23},{4,16},{5,17},{6,18},{7,19},{8,28},{9,... | collective-permute-start | bytes 49160 | tf_op jit(solution)/shard_map/ppermute | solution.py:300
  37.2 3.2 %collective-permute-start.19 = (f32[32,128]{1,0:T(8,128)S(1)}, f32[32,128]{1,0:T(8,128)S(1)}, u32[]{:S(2)}, u32[]{:S(2)}) collective-permute-start(f32[32,128]{1,0:T(8,128)S(1)} %add.17), channel_id=1, source_target_pairs={{0,5},{1,4},{2,7},{3,6},{4,1},{5,0},{6,3},{7,2},{8,13},{9,12},{10,... | collective-permute-start | bytes 49160 | tf_op jit(solution)/shard_map/ppermute | solution.py:300
  40.4 4.6 %collective-permute-start.20 = (f32[32,128]{1,0:T(8,128)S(1)}, f32[32,128]{1,0:T(8,128)S(1)}, u32[]{:S(2)}, u32[]{:S(2)}) collective-permute-start(f32[32,128]{1,0:T(8,128)S(1)} %add.18), channel_id=1, source_target_pairs={{0,6},{1,7},{2,4},{3,5},{4,2},{5,3},{6,0},{7,1},{8,14},{9,15},{10,... | collective-permute-start | bytes 49160 | tf_op jit(solution)/shard_map/ppermute | solution.py:300

commit v3 on v2

--- a/solution.py
+++ b/solution.py
@@ -40,8 +40,7 @@
     return lax.broadcasted_iota(jnp.int32, (sublanes, lanes), 1)
 
 
-def pack(states, send_table_ref, out_refs, groups, slots):
-    group = lane_ids() // slots
+def pack(states, group, send_table_ref, out_refs, groups):
     fields = len(states[0])
     packed = [[None] * fields for _ in range(4)]
     for m in range(groups):
@@ -60,11 +59,16 @@
             out_refs[b][f] = packed[b][f]
 
 
-def prepare_kernel(send_ref, q_ref, send_table_ref, *out_refs):
-    fields, vectors, cells = q_ref.shape
+def groups_kernel(slots, group_ref):
+    group_ref[...] = lane_ids() // slots
+
+
+def prepare_kernel(group_ref, q_ref, send_ref, send_table_ref, *out_refs):
+    fields, vectors, _ = q_ref.shape
     slots = send_ref.shape[1]
     groups = lanes // slots
     shape = (sublanes, lanes)
+    group = group_ref[...]
     row_even = lax.axis_index("gx") % 2 == 0
     col_even = lax.axis_index("gy") % 2 == 0
     sends = jnp.concatenate(
@@ -79,7 +83,7 @@
     ]
     base = ordered[0]
     for b in range(1, 4):
-        base = jnp.where(lane_ids() // slots == b, pltpu.roll(ordered[b], b * slots, 1), base)
+        base = jnp.where(group == b, pltpu.roll(ordered[b], b * slots, 1), base)
     for m in range(groups):
         send_table_ref[pl.ds(m * sublanes, sublanes), :] = (
             pltpu.roll(base, m * slots, 1) if m else base
@@ -87,7 +91,7 @@
     states = [
         [q_ref[f, pl.ds(m * sublanes, sublanes), :] for f in range(fields)] for m in range(groups)
     ]
-    pack(states, send_table_ref, out_refs, groups, slots)
+    pack(states, group, send_table_ref, out_refs, groups)
 
 
 def tables_kernel(
@@ -98,24 +102,29 @@
     speed_ref,
     visc_ref,
     volume_ref,
-    weight_ref,
-    entry_ref,
-    ghost_ref,
-    splat_ref,
+    centre_ref,
+    inside_ref,
+    outside_ref,
+    own_coef_ref,
+    ghost_coef_ref,
 ):
     cells = conn_ref.shape[1]
-    fields = jac_ref.shape[1]
+    fields = jac_ref.shape[0]
+    groups = lanes // slots
     shape = (sublanes, lanes)
-    groups = lanes // slots
     row_swap = jnp.where(lax.axis_index("gx") % 2 == 0, slots, 0)
     col_swap = jnp.where(lax.axis_index("gy") % 2 == 0, slots, 0)
     volume = jnp.broadcast_to(volume_ref[...], shape)
-    weight_ref[0] = -0.5 * jnp.broadcast_to(speed_ref[...], shape) * volume
-    weight_ref[1] = jnp.broadcast_to(visc_ref[...], shape) * volume
-    weight_ref[2] = jnp.where(lane_ids() < jnp.broadcast_to(count_ref[...], shape), 1.0, 0.0)
+    advect = -0.5 * jnp.broadcast_to(speed_ref[...], shape) * volume
+    diffuse = jnp.broadcast_to(visc_ref[...], shape) * volume
+    centre_ref[0] = -4.0 * diffuse
+    centre_ref[1] = jnp.where(lane_ids() < jnp.broadcast_to(count_ref[...], shape), 1.0, 0.0)
+    sub = lax.broadcasted_iota(jnp.int32, shape, 0)
     for face in range(4):
         entry = jnp.broadcast_to(conn_ref[pl.ds(face, 1), :], shape)
-        entry_ref[face] = entry
+        owned = entry < cells
+        far = entry >= cells + 4 * slots
+        inside_ref[face] = jnp.bitwise_and(entry, lanes - 1)
         ghost = entry - cells
         ghost = jnp.where(
             ghost < 2 * slots,
@@ -123,99 +132,86 @@
             jnp.where(ghost < 4 * slots, jnp.bitwise_xor(ghost, col_swap), ghost),
         )
         for m in range(groups):
-            ghost_ref[face, pl.ds(m * sublanes, sublanes), :] = jnp.bitwise_and(
+            outside_ref[face, pl.ds(m * sublanes, sublanes), :] = jnp.bitwise_and(
                 ghost + m * slots, lanes - 1
             )
         for j in range(fields):
-            splat_ref[pl.ds((face * fields + j) * fields, fields), :] = jnp.broadcast_to(
-                jac_ref[face, :, pl.ds(j, 1)], (fields, lanes)
-            )
-
-
-def stage_kernel(
-    stage,
-    chunk,
-    weight_ref,
-    entry_ref,
-    ghost_ref,
-    splat_ref,
-    send_table_ref,
-    q_ref,
-    *refs,
-):
+            rows = pl.ds((face * fields + j) * fields, fields)
+            jacobian = jnp.broadcast_to(jac_ref[:, face, pl.ds(j, 1)], (fields, lanes))
+            coef = jacobian * advect[:fields] + jnp.where(sub == j, diffuse, 0.0)[:fields]
+            own_coef_ref[rows, :] = jnp.where(owned[:fields], coef, 0.0)
+            ghost_coef_ref[rows, :] = jnp.where((owned | far)[:fields], 0.0, coef)
+
+
+def coefficients(stage):
+    kept = time_step / 6.0 if stage in (0, 3) else time_step / 3.0
+    return kept, (0.5 * time_step, 0.5 * time_step, time_step, None)[stage]
+
+
+def neighbours(near, coef_ref, totals, face):
+    fields = len(near)
+    for j in range(fields):
+        for i in range(fields):
+            at = (face * fields + j) * fields + i
+            term = coef_ref[pl.ds(at, 1), :] * near[j]
+            totals[i] = term if totals[i] is None else totals[i] + term
+
+
+def own_kernel(stage, centre_ref, inside_ref, coef_ref, q_ref, *refs):
     refs = list(refs)
     state_ref = q_ref if stage == 0 else refs.pop(0)
     acc_ref = q_ref if stage == 0 else refs.pop(0)
+    kept_coef, next_coef = coefficients(stage)
+    fields, vectors, _ = q_ref.shape
+    for start in range(0, vectors, sublanes):
+        rows = pl.ds(start, sublanes)
+        own = [state_ref[f, rows, :] for f in range(fields)]
+        totals = [centre_ref[0] * own[f] for f in range(fields)]
+        for face in range(4):
+            near = [lane_take(own[f], inside_ref[face]) for f in range(fields)]
+            neighbours(near, coef_ref, totals, face)
+        for f in range(fields):
+            refs[0][f, rows, :] = acc_ref[f, rows, :] + kept_coef * totals[f]
+            if next_coef is not None:
+                refs[1][f, rows, :] = q_ref[f, rows, :] + next_coef * totals[f]
+
+
+def ghost_kernel(stage, outside_ref, coef_ref, centre_ref, group_ref, send_table_ref, *refs):
+    refs = list(refs)
+    last = stage == 3
+    part_refs = [refs.pop(0) for _ in range(1 if last else 2)]
     recv_refs = [refs.pop(0) for _ in range(4)]
-    fields, vectors, cells = q_ref.shape
+    kept_coef, next_coef = coefficients(stage)
+    fields, vectors, cells = part_refs[0].shape
     groups = vectors // sublanes
-    slots = lanes // groups
-    group = lane_ids() // slots
-
-    def tall(value):
-        return value if chunk == 1 else jnp.concatenate([value] * chunk, axis=0)
-
-    advect = tall(weight_ref[0])
-    diffuse = tall(weight_ref[1])
-    last = stage == 3
-    kept_coef = time_step / 6.0 if stage in (0, 3) else time_step / 3.0
-    next_coef = (0.5 * time_step, 0.5 * time_step, time_step, None)[stage]
-    if last:
-        advanced_ref, gram_ref = refs
-        live = tall(weight_ref[2]) > 0.5
-    else:
-        next_ref, next_acc_ref, *out_refs = refs
+    group = group_ref[...]
     states = []
-    zero = jnp.zeros((sublanes, lanes), jnp.float32)
-    for start in range(0, groups, chunk):
-        rows = pl.ds(start * sublanes, chunk * sublanes)
-        own = [state_ref[f, rows, :] for f in range(fields)]
+    for m in range(groups):
+        rows = pl.ds(m * sublanes, sublanes)
         ghosts = []
         for f in range(fields):
-            parts = []
-            for m in range(start, start + chunk):
-                block = zero
-                for b in range(4):
-                    block = jnp.where(group == (m + b) % groups, recv_refs[b][f], block)
-                parts.append(block)
-            ghosts.append(jnp.concatenate(parts, axis=0))
-        advection = [None] * fields
-        diffusion = [-4.0 * own[f] for f in range(fields)]
+            block = recv_refs[0][f]
+            for b in range(1, 4):
+                block = jnp.where(group == (m + b) % groups, recv_refs[b][f], block)
+            ghosts.append(block)
+        totals = [None] * fields
         for face in range(4):
-            entry = tall(entry_ref[face])
-            outside = entry >= cells
-            inside_index = jnp.bitwise_and(entry, lanes - 1)
-            outside_index = ghost_ref[face, rows, :]
-            for j in range(fields):
-                near = jnp.where(
-                    outside,
-                    lane_take(ghosts[j], outside_index),
-                    lane_take(own[j], inside_index),
-                )
-                diffusion[j] = diffusion[j] + near
-                for i in range(fields):
-                    at = (face * fields + j) * fields + i
-                    term = splat_ref[pl.ds(at, 1), :] * near
-                    advection[i] = term if advection[i] is None else advection[i] + term
+            near = [lane_take(ghosts[f], outside_ref[face, rows, :]) for f in range(fields)]
+            neighbours(near, coef_ref, totals, face)
         following = []
         for f in range(fields):
-            slope = advect * advection[f] + diffuse * diffusion[f]
-            kept = acc_ref[f, rows, :] + kept_coef * slope
-            if last:
-                advanced_ref[f, rows, :] = jnp.where(live, kept, 0.0)
-            else:
-                next_acc_ref[f, rows, :] = kept
-                after = q_ref[f, rows, :] + next_coef * slope
-                next_ref[f, rows, :] = after
+            kept = part_refs[0][f, rows, :] + kept_coef * totals[f]
+            refs[0][f, rows, :] = kept * centre_ref[1] if last else kept
+            if not last:
+                after = part_refs[1][f, rows, :] + next_coef * totals[f]
+                refs[1][f, rows, :] = after
                 following.append(after)
-        if not last:
-            for m in range(chunk):
-                states.append([x[m * sublanes : (m + 1) * sublanes] for x in following])
+        states.append(following)
     if not last:
-        pack(states, send_table_ref, out_refs, groups, slots)
+        pack(states, group, send_table_ref, refs[2:], groups)
         return
     half = vectors // 2
-    wide = jnp.concatenate([advanced_ref[f] for f in range(fields)], axis=1)
+    wide = jnp.concatenate([refs[0][f] for f in range(fields)], axis=1)
     gram = lax.dot_general(
         wide,
         jnp.concatenate([wide, jnp.zeros_like(wide)], axis=0),
@@ -223,7 +219,7 @@
         precision=HIGHEST,
         preferred_element_type=jnp.float32,
     )
-    gram_ref[...] = gram[:half] + pltpu.roll(gram[half:], vectors, 1)
+    refs[1][...] = gram[:half] + pltpu.roll(gram[half:], vectors, 1)
 
 
 def factor_kernel(scale, gram_ref, advanced_ref, basis_ref, factor_ref):
@@ -323,11 +319,13 @@
     volume = inverse_volume.reshape(1, cells)
     state = jax.ShapeDtypeStruct(test_vectors.shape, jnp.float32)
     block = jax.ShapeDtypeStruct((fields, sublanes, lanes), jnp.float32)
+    coefs = jax.ShapeDtypeStruct((4 * fields * fields, lanes), jnp.float32)
     tables = [
-        jax.ShapeDtypeStruct((3, sublanes, lanes), jnp.float32),
+        jax.ShapeDtypeStruct((2, sublanes, lanes), jnp.float32),
         jax.ShapeDtypeStruct((4, sublanes, lanes), jnp.int32),
         jax.ShapeDtypeStruct((4, vectors, lanes), jnp.int32),
-        jax.ShapeDtypeStruct((4 * fields * fields, lanes), jnp.float32),
+        coefs,
+        coefs,
     ]
     params = pltpu.CompilerParams(vmem_limit_bytes=16 * 1024 * 1024)
     pairs = matchings(rows, cols)
@@ -338,37 +336,62 @@
             got[which] = lax.ppermute(sent[which], ("gx", "gy"), pairs[which])
         return got
 
+    ahead = pl.CostEstimate(flops=4 * 10**9, bytes_accessed=8 * 10**6, transcendentals=0)
+    tile = jax.ShapeDtypeStruct((sublanes, lanes), jnp.int32)
+    group = pl.pallas_call(
+        functools.partial(groups_kernel, slots),
+        out_shape=tile,
+        out_specs=vmem,
+        compiler_params=params,
+        cost_estimate=ahead,
+        name="groups",
+    )()
     send_table, *sent = pl.pallas_call(
         prepare_kernel,
         out_shape=[jax.ShapeDtypeStruct((vectors, lanes), jnp.int32)] + [block] * 4,
-        in_specs=[vmem] * 2,
+        in_specs=[vmem] * 3,
         out_specs=[vmem] * 5,
         compiler_params=params,
         name="prepare",
-    )(send_rows, test_vectors)
-    tables = pl.pallas_call(
+    )(group, test_vectors, send_rows)
+    centre, inside, outside, own_coef, ghost_coef = pl.pallas_call(
         functools.partial(tables_kernel, slots),
         out_shape=tables,
         in_specs=[vmem] * 6,
-        out_specs=[vmem] * 4,
+        out_specs=[vmem] * 5,
         compiler_params=params,
         name="tables",
-    )(cell_count.reshape(1, 1), face_jacobians, connectivity, speed, visc, volume)
+    )(
+        cell_count.reshape(1, 1),
+        face_jacobians.transpose(1, 0, 2),
+        connectivity,
+        speed,
+        visc,
+        volume,
+    )
     held = []
     for stage in range(4):
+        last = stage == 3
         got = exchange(sent)
-        last = stage == 3
+        partial = pl.pallas_call(
+            functools.partial(own_kernel, stage),
+            out_shape=[state] * (1 if last else 2),
+            in_specs=[vmem] * (4 + len(held)),
+            out_specs=[vmem] * (1 if last else 2),
+            compiler_params=params,
+            name="own",
+        )(centre, inside, own_coef, test_vectors, *held)
         gram_shape = jax.ShapeDtypeStruct((vectors // 2, lanes), jnp.float32)
         result = pl.pallas_call(
-            functools.partial(stage_kernel, stage, 1),
+            functools.partial(ghost_kernel, stage),
             out_shape=[state, gram_shape] if last else [state, state] + [block] * 4,
-            in_specs=[vmem] * (6 + len(held) + 4),
+            in_specs=[vmem] * (5 + len(partial) + 4),
             out_specs=[vmem] * (2 if last else 6),
             compiler_params=params,
-            name="stage",
-        )(*tables, send_table, test_vectors, *held, *got)
-        held, sent = result[:2], result[2:]
-    advanced, gram = held
+            name="ghost",
+        )(outside, ghost_coef, centre, group, send_table, *partial, *got)
+        held, sent = result[1::-1], result[2:]
+    gram, advanced = held
     gram = summed(gram, rows, cols)
     scale = 1.0 / float(fields * cells * rows * cols)
     return pl.pallas_call(

time: 48.1 us -> 45.6 us (0.948)
  waiting for transfers between devices: 14.2 us -> 12.5 us
  local copies, waits for them, and re-layouts: 2.27 us -> 1.56 us
    ppermute x16, waiting for transfers between devices: 5.99 us -> 4.39 us  [exchange(): got[which] = lax.ppermute(sent[which], ('gx', 'gy'), pairs[which])]
    unnamed x17 -> x14, local copies, waits for them, and re-layouts: 2.27 us -> 1.56 us
    pallas_call x4 -> x9, Pallas kernels: 3.95 us -> 3.63 us  [the longest x4 2.18 us: shards(): pl.pallas_call(functools.partial(ghost_kernel, stage), out_shape=[state,...]
  transfers between devices with their start and end apart: 21 -> 21, of which waited for: 12 -> 12; matrix products, arithmetic and copies ran while one was open for 0% -> 0% of each run, Pallas kernels for 0% -> 4%
where the time goes in v3:
time: 45.6 us; the launch traced here: 45.5 us
  starting transfers between devices  22.9 us (50%)
  waiting for transfers between devices  12.5 us (27%)
  Pallas kernels  6.94 us (15%)
  local copies, waits for them, and re-layouts  1.56 us (3%)
  between operations  1.48 us (3%)
    ppermute x16, starting transfers between devices, exchange(): got[which] = lax.ppermute(sent[which], ('gx', 'gy'), pairs[which])  15.9 us
    ppermute x5, waiting for transfers between devices, summed(): value = value + lax.ppermute(value, ('gx', 'gy'), pairs)  8.14 us
    ppermute x5, starting transfers between devices, summed(): value = value + lax.ppermute(value, ('gx', 'gy'), pairs)  7.04 us
    ppermute x16, waiting for transfers between devices, exchange(): got[which] = lax.ppermute(sent[which], ('gx', 'gy'), pairs[which])  4.39 us
    pallas_call x1, Pallas kernels, shards(): pl.pallas_call(functools.partial(factor_kernel, scale), out_shape=[state,...  2.82 us
    pallas_call x4, Pallas kernels, shards(): pl.pallas_call(functools.partial(ghost_kernel, stage), out_shape=[state,...  2.18 us
    unnamed x14, local copies, waits for them, and re-layouts  1.56 us
    pallas_call x4, Pallas kernels, shards(): pl.pallas_call(functools.partial(own_kernel, stage), out_shape=[state] *...  1.45 us
  transfers between devices with their start and end apart: 21, of which 12 were waited for; matrix products, arithmetic and copies ran while one was open for 0% of the time, Pallas kernels for 4%

profile of v3, /device:TPU:0, one launch (start us, length us, event | category | flops | bytes accessed | tf_op | source)
XLA Modules:
  0.0 45.5 jit_solution(17699152704909964242)
XLA Ops:
  0.7 0.9 %copy-done = f32[5,64,128]{2,1,0:T(8,128)S(1)} copy-done((f32[5,64,128]{2,1,0:T(8,128)S(1)}, f32[5,64,128]{2,1,0:T(8,128)}, u32[]{:S(2)}) %copy-start) | copy-done | bytes 163864
  1.8 0.5 %collective-permute-start = (f32[5,8,128]{2,1,0:T(8,128)S(1)}, f32[5,8,128]{2,1,0:T(8,128)S(1)}, u32[]{:S(2)}, u32[]{:S(2)}) collective-permute-start(f32[5,8,128]{2,1,0:T(8,128)S(1)} %get-tuple-element.46), channel_id=1, source_target_pairs={{0,4},{1,5},{2,6},{3,7},{4,0},{5,1},{6,2},{7,3},{8,12},{9,13},{10,... | collective-permute-start | bytes 61448 | tf_op jit(solution)/shard_map/ppermute | solution.py:336
  2.4 3.6 %collective-permute-start.1 = (f32[5,8,128]{2,1,0:T(8,128)S(1)}, f32[5,8,128]{2,1,0:T(8,128)S(1)}, u32[]{:S(2)}, u32[]{:S(2)}) collective-permute-start(f32[5,8,128]{2,1,0:T(8,128)S(1)} %get-tuple-element.47), channel_id=1, source_target_pairs={{0,28},{1,29},{2,30},{3,31},{4,8},{5,9},{6,10},{7,11},{8,4},{9,5},... | collective-permute-start | bytes 61448 | tf_op jit(solution)/shard_map/ppermute | solution.py:336
  5.9 1.6 %collective-permute-start.2 = (f32[5,8,128]{2,1,0:T(8,128)S(1)}, f32[5,8,128]{2,1,0:T(8,128)S(1)}, u32[]{:S(2)}, u32[]{:S(2)}) collective-permute-start(f32[5,8,128]{2,1,0:T(8,128)S(1)} %get-tuple-element.48), channel_id=1, source_target_pairs={{0,1},{1,0},{2,3},{3,2},{4,5},{5,4},{6,7},{7,6},{8,9},{9,8},{10,11... | collective-permute-start | bytes 61448 | tf_op jit(solution)/shard_map/ppermute | solution.py:336
  8.2 0.6 %copy-done.3 = s32[4,128]{1,0:T(4,128)S(1)} copy-done((s32[4,128]{1,0:T(4,128)S(1)}, s32[4,128]{1,0:T(4,128)}, u32[]{:S(2)}) %copy-start.3) | copy-done | bytes 2072
  9.1 0.4 own.4
  9.7 0.4 ghost.4
  10.8 2.9 %collective-permute-start.6 = (f32[5,8,128]{2,1,0:T(8,128)S(1)}, f32[5,8,128]{2,1,0:T(8,128)S(1)}, u32[]{:S(2)}, u32[]{:S(2)}) collective-permute-start(f32[5,8,128]{2,1,0:T(8,128)S(1)} %get-tuple-element.56), channel_id=1, source_target_pairs={{0,1},{1,0},{2,3},{3,2},{4,5},{5,4},{6,7},{7,6},{8,9},{9,8},{10,11... | collective-permute-start | bytes 61448 | tf_op jit(solution)/shard_map/ppermute | solution.py:336
  13.8 0.4 own.5
  14.2 0.4 collective-permute-done.5.refs_3_
  14.6 0.9 %collective-permute-done.6.refs_4_ = f32[5,8,128]{2,1,0:T(8,128)S(1)} collective-permute-done((f32[5,8,128]{2,1,0:T(8,128)S(1)}, f32[5,8,128]{2,1,0:T(8,128)S(1)}, u32[]{:S(2)}, u32[]{:S(2)}) %collective-permute-start.6) | collective-permute-done | bytes 20512 | tf_op jit(solution)/shard_map/ppermute | solution.py:336
  15.5 0.4 ghost.5
  16.0 1.5 %collective-permute-start.9 = (f32[5,8,128]{2,1,0:T(8,128)S(1)}, f32[5,8,128]{2,1,0:T(8,128)S(1)}, u32[]{:S(2)}, u32[]{:S(2)}) collective-permute-start(f32[5,8,128]{2,1,0:T(8,128)S(1)} %get-tuple-element.63), channel_id=1, source_target_pairs={{0,28},{1,29},{2,30},{3,31},{4,8},{5,9},{6,10},{7,11},{8,4},{9,5},... | collective-permute-start | bytes 61448 | tf_op jit(solution)/shard_map/ppermute | solution.py:336
  17.6 2.2 %collective-permute-start.10 = (f32[5,8,128]{2,1,0:T(8,128)S(1)}, f32[5,8,128]{2,1,0:T(8,128)S(1)}, u32[]{:S(2)}, u32[]{:S(2)}) collective-permute-start(f32[5,8,128]{2,1,0:T(8,128)S(1)} %get-tuple-element.64), channel_id=1, source_target_pairs={{0,1},{1,0},{2,3},{3,2},{4,5},{5,4},{6,7},{7,6},{8,9},{9,8},{10,11... | collective-permute-start | bytes 61448 | tf_op jit(solution)/shard_map/ppermute | solution.py:336
  19.8 0.4 own.6
  20.2 1.3 %collective-permute-done.10.refs_4_ = f32[5,8,128]{2,1,0:T(8,128)S(1)} collective-permute-done((f32[5,8,128]{2,1,0:T(8,128)S(1)}, f32[5,8,128]{2,1,0:T(8,128)S(1)}, u32[]{:S(2)}, u32[]{:S(2)}) %collective-permute-start.10) | collective-permute-done | bytes 20512 | tf_op jit(solution)/shard_map/ppermute | solution.py:336
  21.5 0.4 ghost.6
  22.0 0.5 %collective-permute-start.13 = (f32[5,8,128]{2,1,0:T(8,128)S(1)}, f32[5,8,128]{2,1,0:T(8,128)S(1)}, u32[]{:S(2)}, u32[]{:S(2)}) collective-permute-start(f32[5,8,128]{2,1,0:T(8,128)S(1)} %get-tuple-element.69), channel_id=1, source_target_pairs={{0,28},{1,29},{2,30},{3,31},{4,8},{5,9},{6,10},{7,11},{8,4},{9,5},... | collective-permute-start | bytes 61448 | tf_op jit(solution)/shard_map/ppermute | solution.py:336
  22.6 2.2 %collective-permute-start.14 = (f32[5,8,128]{2,1,0:T(8,128)S(1)}, f32[5,8,128]{2,1,0:T(8,128)S(1)}, u32[]{:S(2)}, u32[]{:S(2)}) collective-permute-start(f32[5,8,128]{2,1,0:T(8,128)S(1)} %get-tuple-element.70), channel_id=1, source_target_pairs={{0,1},{1,0},{2,3},{3,2},{4,5},{5,4},{6,7},{7,6},{8,9},{9,8},{10,11... | collective-permute-start | bytes 61448 | tf_op jit(solution)/shard_map/ppermute | solution.py:336
  24.8 0.4 own.7.refs_0_
  25.2 1.0 %collective-permute-done.13.refs_2_ = f32[5,8,128]{2,1,0:T(8,128)S(1)} collective-permute-done((f32[5,8,128]{2,1,0:T(8,128)S(1)}, f32[5,8,128]{2,1,0:T(8,128)S(1)}, u32[]{:S(2)}, u32[]{:S(2)}) %collective-permute-start.13) | collective-permute-done | bytes 20512 | tf_op jit(solution)/shard_map/ppermute | solution.py:336
  26.5 0.9 %ghost.7 = (f32[5,64,128]{2,1,0:T(8,128)S(1)}, f32[32,128]{1,0:T(8,128)S(1)}) custom-call(s32[4,64,128]{2,1,0:T(8,128)S(1)} %get-tuple-element.38.outside_ref, f32[100,128]{1,0:T(8,128)S(1)} %get-tuple-element.39.coef_ref, f32[2,8,128]{2,1,0:T(8,128)S(1)} %get-tuple-element.40.centre_ref, s32[8,128]{1,0:T(8,128)S(1)} %groups.1.group_ref, ...), custom_call_target="tpu_custom_call" | custom-call | tf_op jit(solution)/shard_map/ghost/pallas_call | solution.py:385
  27.4 1.2 %collective-permute-done.16 = f32[32,128]{1,0:T(8,128)S(1)} collective-permute-done((f32[32,128]{1,0:T(8,128)S(1)}, f32[32,128]{1,0:T(8,128)S(1)}, u32[]{:S(2)}, u32[]{:S(2)}) %collective-permute-start.16) | collective-permute-done | bytes 16416 | tf_op jit(solution)/shard_map/ppermute | solution.py:296
  28.6 1.2 %collective-permute-start.17 = (f32[32,128]{1,0:T(8,128)S(1)}, f32[32,128]{1,0:T(8,128)S(1)}, u32[]{:S(2)}, u32[]{:S(2)}) collective-permute-start(f32[32,128]{1,0:T(8,128)S(1)} %add.15), channel_id=1, source_target_pairs={{0,12},{1,13},{2,14},{3,15},{4,8},{5,9},{6,10},{7,11},{8,4},{9,5},... | collective-permute-start | bytes 49160 | tf_op jit(solution)/shard_map/ppermute | solution.py:296
  29.8 2.0 %collective-permute-done.17 = f32[32,128]{1,0:T(8,128)S(1)} collective-permute-done((f32[32,128]{1,0:T(8,128)S(1)}, f32[32,128]{1,0:T(8,128)S(1)}, u32[]{:S(2)}, u32[]{:S(2)}) %collective-permute-start.17) | collective-permute-done | bytes 16416 | tf_op jit(solution)/shard_map/ppermute | solution.py:296
  31.8 1.0 %collective-permute-start.18 = (f32[32,128]{1,0:T(8,128)S(1)}, f32[32,128]{1,0:T(8,128)S(1)}, u32[]{:S(2)}, u32[]{:S(2)}) collective-permute-start(f32[32,128]{1,0:T(8,128)S(1)} %add.16), channel_id=1, source_target_pairs={{0,20},{1,21},{2,22},{3,23},{4,16},{5,17},{6,18},{7,19},{8,28},{9,... | collective-permute-start | bytes 49160 | tf_op jit(solution)/shard_map/ppermute | solution.py:296
  32.8 2.1 %collective-permute-done.18 = f32[32,128]{1,0:T(8,128)S(1)} collective-permute-done((f32[32,128]{1,0:T(8,128)S(1)}, f32[32,128]{1,0:T(8,128)S(1)}, u32[]{:S(2)}, u32[]{:S(2)}) %collective-permute-start.18) | collective-permute-done | bytes 16416 | tf_op jit(solution)/shard_map/ppermute | solution.py:296
  35.0 1.8 %collective-permute-start.19 = (f32[32,128]{1,0:T(8,128)S(1)}, f32[32,128]{1,0:T(8,128)S(1)}, u32[]{:S(2)}, u32[]{:S(2)}) collective-permute-start(f32[32,128]{1,0:T(8,128)S(1)} %add.17), channel_id=1, source_target_pairs={{0,5},{1,4},{2,7},{3,6},{4,1},{5,0},{6,3},{7,2},{8,13},{9,12},{10,... | collective-permute-start | bytes 49160 | tf_op jit(solution)/shard_map/ppermute | solution.py:296
  36.7 1.4 %collective-permute-done.19 = f32[32,128]{1,0:T(8,128)S(1)} collective-permute-done((f32[32,128]{1,0:T(8,128)S(1)}, f32[32,128]{1,0:T(8,128)S(1)}, u32[]{:S(2)}, u32[]{:S(2)}) %collective-permute-start.19) | collective-permute-done | bytes 16416 | tf_op jit(solution)/shard_map/ppermute | solution.py:296
  38.2 3.0 %collective-permute-start.20 = (f32[32,128]{1,0:T(8,128)S(1)}, f32[32,128]{1,0:T(8,128)S(1)}, u32[]{:S(2)}, u32[]{:S(2)}) collective-permute-start(f32[32,128]{1,0:T(8,128)S(1)} %add.18), channel_id=1, source_target_pairs={{0,6},{1,7},{2,4},{3,5},{4,2},{5,3},{6,0},{7,1},{8,14},{9,15},{10,... | collective-permute-start | bytes 49160 | tf_op jit(solution)/shard_map/ppermute | solution.py:296
  41.2 1.4 %collective-permute-done.20 = f32[32,128]{1,0:T(8,128)S(1)} collective-permute-done((f32[32,128]{1,0:T(8,128)S(1)}, f32[32,128]{1,0:T(8,128)S(1)}, u32[]{:S(2)}, u32[]{:S(2)}) %collective-permute-start.20) | collective-permute-done | bytes 16416 | tf_op jit(solution)/shard_map/ppermute | solution.py:296
  42.6 2.8 %factor.1 = (f32[5,64,128]{2,1,0:T(8,128)}, f32[64,64]{1,0:T(8,128)}) custom-call(f32[32,128]{1,0:T(8,128)S(1)} %add.19.gram_ref, f32[5,64,128]{2,1,0:T(8,128)S(1)} %get-tuple-element.73.advanced_ref), custom_call_target="tpu_custom_call" | custom-call | tf_op jit(solution)/shard_map/factor/pallas_call | solution.py:397
  (41 shorter events, 2.1 us)
Async XLA Ops:
  0.6 0.9 %copy-start = (f32[5,64,128]{2,1,0:T(8,128)S(1)}, f32[5,64,128]{2,1,0:T(8,128)}, u32[]{:S(2)}) copy-start(f32[5,64,128]{2,1,0:T(8,128)} %q_ref.9) | copy-start | bytes 491524
  0.6 0.9 %copy-start.2 = (s32[4,16]{1,0:T(4,128)S(1)}, s32[4,16]{1,0:T(4,128)}, u32[]{:S(2)}) copy-start(s32[4,16]{1,0:T(4,128)} %send_ref.1) | copy-start | bytes 772
  1.8 6.4 %copy-start.1 = (f32[4,5,5]{2,0,1:T(4,128)S(1)}, f32[4,5,5]{2,0,1:T(4,128)}, u32[]{:S(2)}) copy-start(f32[4,5,5]{2,0,1:T(4,128)} %param.9) | copy-start | bytes 1204
  1.8 7.6 %collective-permute-start = (f32[5,8,128]{2,1,0:T(8,128)S(1)}, f32[5,8,128]{2,1,0:T(8,128)S(1)}, u32[]{:S(2)}, u32[]{:S(2)}) collective-permute-start(f32[5,8,128]{2,1,0:T(8,128)S(1)} %get-tuple-element.46), channel_id=1, source_target_pairs={{0,4},{1,5},{2,6},{3,7},{4,0},{5,1},{6,2},{7,3},{8,12},{9,13},{10,... | collective-permute-start | bytes 61448 | tf_op jit(solution)/shard_map/ppermute | solution.py:336
  2.4 7.1 %collective-permute-start.1 = (f32[5,8,128]{2,1,0:T(8,128)S(1)}, f32[5,8,128]{2,1,0:T(8,128)S(1)}, u32[]{:S(2)}, u32[]{:S(2)}) collective-permute-start(f32[5,8,128]{2,1,0:T(8,128)S(1)} %get-tuple-element.47), channel_id=1, source_target_pairs={{0,28},{1,29},{2,30},{3,31},{4,8},{5,9},{6,10},{7,11},{8,4},{9,5},... | collective-permute-start | bytes 61448 | tf_op jit(solution)/shard_map/ppermute | solution.py:336
  5.9 3.8 %collective-permute-start.2 = (f32[5,8,128]{2,1,0:T(8,128)S(1)}, f32[5,8,128]{2,1,0:T(8,128)S(1)}, u32[]{:S(2)}, u32[]{:S(2)}) collective-permute-start(f32[5,8,128]{2,1,0:T(8,128)S(1)} %get-tuple-element.48), channel_id=1, source_target_pairs={{0,1},{1,0},{2,3},{3,2},{4,5},{5,4},{6,7},{7,6},{8,9},{9,8},{10,11... | collective-permute-start | bytes 61448 | tf_op jit(solution)/shard_map/ppermute | solution.py:336
  7.5 2.2 %collective-permute-start.3 = (f32[5,8,128]{2,1,0:T(8,128)S(1)}, f32[5,8,128]{2,1,0:T(8,128)S(1)}, u32[]{:S(2)}, u32[]{:S(2)}) collective-permute-start(f32[5,8,128]{2,1,0:T(8,128)S(1)} %get-tuple-element.49), channel_id=1, source_target_pairs={{0,4},{1,2},{2,1},{3,7},{4,0},{5,6},{6,5},{7,3},{8,12},{9,10},{10,... | collective-permute-start | bytes 61448 | tf_op jit(solution)/shard_map/ppermute | solution.py:336
  8.1 0.7 %copy-start.3 = (s32[4,128]{1,0:T(4,128)S(1)}, s32[4,128]{1,0:T(4,128)}, u32[]{:S(2)}) copy-start(s32[4,128]{1,0:T(4,128)} %conn_ref.1) | copy-start | bytes 6148
  8.2 0.7 %copy-start.4 = (f32[128]{0:T(128)S(1)}, f32[128]{0:T(128)}, u32[]{:S(2)}) copy-start(f32[128]{0:T(128)} %param.10) | copy-start | bytes 1540
  8.2 0.7 %copy-start.5 = (f32[128]{0:T(128)S(1)}, f32[128]{0:T(128)}, u32[]{:S(2)}) copy-start(f32[128]{0:T(128)} %param.11) | copy-start | bytes 1540
  8.2 0.7 %copy-start.6 = (f32[128]{0:T(128)S(1)}, f32[128]{0:T(128)}, u32[]{:S(2)}) copy-start(f32[128]{0:T(128)} %param.12) | copy-start | bytes 1540
  10.1 4.0 %collective-permute-start.4 = (f32[5,8,128]{2,1,0:T(8,128)S(1)}, f32[5,8,128]{2,1,0:T(8,128)S(1)}, u32[]{:S(2)}, u32[]{:S(2)}) collective-permute-start(f32[5,8,128]{2,1,0:T(8,128)S(1)} %get-tuple-element.54), channel_id=1, source_target_pairs={{0,4},{1,5},{2,6},{3,7},{4,0},{5,1},{6,2},{7,3},{8,12},{9,13},{10,... | collective-permute-start | bytes 61448 | tf_op jit(solution)/shard_map/ppermute | solution.py:336
  10.5 4.1 %collective-permute-start.5 = (f32[5,8,128]{2,1,0:T(8,128)S(1)}, f32[5,8,128]{2,1,0:T(8,128)S(1)}, u32[]{:S(2)}, u32[]{:S(2)}) collective-permute-start(f32[5,8,128]{2,1,0:T(8,128)S(1)} %get-tuple-element.55), channel_id=1, source_target_pairs={{0,28},{1,29},{2,30},{3,31},{4,8},{5,9},{6,10},{7,11},{8,4},{9,5},... | collective-permute-start | bytes 61448 | tf_op jit(solution)/shard_map/ppermute | solution.py:336
  10.8 4.7 %collective-permute-start.6 = (f32[5,8,128]{2,1,0:T(8,128)S(1)}, f32[5,8,128]{2,1,0:T(8,128)S(1)}, u32[]{:S(2)}, u32[]{:S(2)}) collective-permute-start(f32[5,8,128]{2,1,0:T(8,128)S(1)} %get-tuple-element.56), channel_id=1, source_target_pairs={{0,1},{1,0},{2,3},{3,2},{4,5},{5,4},{6,7},{7,6},{8,9},{9,8},{10,11... | collective-permute-start | bytes 61448 | tf_op jit(solution)/shard_map/ppermute | solution.py:336
  13.8 1.8 %collective-permute-start.7 = (f32[5,8,128]{2,1,0:T(8,128)S(1)}, f32[5,8,128]{2,1,0:T(8,128)S(1)}, u32[]{:S(2)}, u32[]{:S(2)}) collective-permute-start(f32[5,8,128]{2,1,0:T(8,128)S(1)} %get-tuple-element.57), channel_id=1, source_target_pairs={{0,4},{1,2},{2,1},{3,7},{4,0},{5,6},{6,5},{7,3},{8,12},{9,10},{10,... | collective-permute-start | bytes 61448 | tf_op jit(solution)/shard_map/ppermute | solution.py:336
  16.0 4.2 %collective-permute-start.8 = (f32[5,8,128]{2,1,0:T(8,128)S(1)}, f32[5,8,128]{2,1,0:T(8,128)S(1)}, u32[]{:S(2)}, u32[]{:S(2)}) collective-permute-start(f32[5,8,128]{2,1,0:T(8,128)S(1)} %get-tuple-element.62), channel_id=1, source_target_pairs={{0,4},{1,5},{2,6},{3,7},{4,0},{5,1},{6,2},{7,3},{8,12},{9,13},{10,... | collective-permute-start | bytes 61448 | tf_op jit(solution)/shard_map/ppermute | solution.py:336
  16.0 4.2 %collective-permute-start.9 = (f32[5,8,128]{2,1,0:T(8,128)S(1)}, f32[5,8,128]{2,1,0:T(8,128)S(1)}, u32[]{:S(2)}, u32[]{:S(2)}) collective-permute-start(f32[5,8,128]{2,1,0:T(8,128)S(1)} %get-tuple-element.63), channel_id=1, source_target_pairs={{0,28},{1,29},{2,30},{3,31},{4,8},{5,9},{6,10},{7,11},{8,4},{9,5},... | collective-permute-start | bytes 61448 | tf_op jit(solution)/shard_map/ppermute | solution.py:336
  17.6 3.9 %collective-permute-start.10 = (f32[5,8,128]{2,1,0:T(8,128)S(1)}, f32[5,8,128]{2,1,0:T(8,128)S(1)}, u32[]{:S(2)}, u32[]{:S(2)}) collective-permute-start(f32[5,8,128]{2,1,0:T(8,128)S(1)} %get-tuple-element.64), channel_id=1, source_target_pairs={{0,1},{1,0},{2,3},{3,2},{4,5},{5,4},{6,7},{7,6},{8,9},{9,8},{10,11... | collective-permute-start | bytes 61448 | tf_op jit(solution)/shard_map/ppermute | solution.py:336
  19.8 1.8 %collective-permute-start.11 = (f32[5,8,128]{2,1,0:T(8,128)S(1)}, f32[5,8,128]{2,1,0:T(8,128)S(1)}, u32[]{:S(2)}, u32[]{:S(2)}) collective-permute-start(f32[5,8,128]{2,1,0:T(8,128)S(1)} %get-tuple-element.65), channel_id=1, source_target_pairs={{0,4},{1,2},{2,1},{3,7},{4,0},{5,6},{6,5},{7,3},{8,12},{9,10},{10,... | collective-permute-start | bytes 61448 | tf_op jit(solution)/shard_map/ppermute | solution.py:336
  22.0 3.2 %collective-permute-start.12 = (f32[5,8,128]{2,1,0:T(8,128)S(1)}, f32[5,8,128]{2,1,0:T(8,128)S(1)}, u32[]{:S(2)}, u32[]{:S(2)}) collective-permute-start(f32[5,8,128]{2,1,0:T(8,128)S(1)} %get-tuple-element.68), channel_id=1, source_target_pairs={{0,4},{1,5},{2,6},{3,7},{4,0},{5,1},{6,2},{7,3},{8,12},{9,13},{10,... | collective-permute-start | bytes 61448 | tf_op jit(solution)/shard_map/ppermute | solution.py:336
  22.0 4.2 %collective-permute-start.13 = (f32[5,8,128]{2,1,0:T(8,128)S(1)}, f32[5,8,128]{2,1,0:T(8,128)S(1)}, u32[]{:S(2)}, u32[]{:S(2)}) collective-permute-start(f32[5,8,128]{2,1,0:T(8,128)S(1)} %get-tuple-element.69), channel_id=1, source_target_pairs={{0,28},{1,29},{2,30},{3,31},{4,8},{5,9},{6,10},{7,11},{8,4},{9,5},... | collective-permute-start | bytes 61448 | tf_op jit(solution)/shard_map/ppermute | solution.py:336
  22.6 4.0 %collective-permute-start.14 = (f32[5,8,128]{2,1,0:T(8,128)S(1)}, f32[5,8,128]{2,1,0:T(8,128)S(1)}, u32[]{:S(2)}, u32[]{:S(2)}) collective-permute-start(f32[5,8,128]{2,1,0:T(8,128)S(1)} %get-tuple-element.70), channel_id=1, source_target_pairs={{0,1},{1,0},{2,3},{3,2},{4,5},{5,4},{6,7},{7,6},{8,9},{9,8},{10,11... | collective-permute-start | bytes 61448 | tf_op jit(solution)/shard_map/ppermute | solution.py:336
  24.8 1.8 %collective-permute-start.15 = (f32[5,8,128]{2,1,0:T(8,128)S(1)}, f32[5,8,128]{2,1,0:T(8,128)S(1)}, u32[]{:S(2)}, u32[]{:S(2)}) collective-permute-start(f32[5,8,128]{2,1,0:T(8,128)S(1)} %get-tuple-element.71), channel_id=1, source_target_pairs={{0,4},{1,2},{2,1},{3,7},{4,0},{5,6},{6,5},{7,3},{8,12},{9,10},{10,... | collective-permute-start | bytes 61448 | tf_op jit(solution)/shard_map/ppermute | solution.py:336
  27.4 1.2 %collective-permute-start.16 = (f32[32,128]{1,0:T(8,128)S(1)}, f32[32,128]{1,0:T(8,128)S(1)}, u32[]{:S(2)}, u32[]{:S(2)}) collective-permute-start(f32[32,128]{1,0:T(8,128)S(1)} %get-tuple-element.72), channel_id=1, source_target_pairs={{0,4},{1,5},{2,6},{3,7},{4,0},{5,1},{6,2},{7,3},{8,12},{9,13},{10,... | collective-permute-start | bytes 49160 | tf_op jit(solution)/shard_map/ppermute | solution.py:296
  28.6 3.2 %collective-permute-start.17 = (f32[32,128]{1,0:T(8,128)S(1)}, f32[32,128]{1,0:T(8,128)S(1)}, u32[]{:S(2)}, u32[]{:S(2)}) collective-permute-start(f32[32,128]{1,0:T(8,128)S(1)} %add.15), channel_id=1, source_target_pairs={{0,12},{1,13},{2,14},{3,15},{4,8},{5,9},{6,10},{7,11},{8,4},{9,5},... | collective-permute-start | bytes 49160 | tf_op jit(solution)/shard_map/ppermute | solution.py:296
  31.8 3.2 %collective-permute-start.18 = (f32[32,128]{1,0:T(8,128)S(1)}, f32[32,128]{1,0:T(8,128)S(1)}, u32[]{:S(2)}, u32[]{:S(2)}) collective-permute-start(f32[32,128]{1,0:T(8,128)S(1)} %add.16), channel_id=1, source_target_pairs={{0,20},{1,21},{2,22},{3,23},{4,16},{5,17},{6,18},{7,19},{8,28},{9,... | collective-permute-start | bytes 49160 | tf_op jit(solution)/shard_map/ppermute | solution.py:296
  35.0 3.2 %collective-permute-start.19 = (f32[32,128]{1,0:T(8,128)S(1)}, f32[32,128]{1,0:T(8,128)S(1)}, u32[]{:S(2)}, u32[]{:S(2)}) collective-permute-start(f32[32,128]{1,0:T(8,128)S(1)} %add.17), channel_id=1, source_target_pairs={{0,5},{1,4},{2,7},{3,6},{4,1},{5,0},{6,3},{7,2},{8,13},{9,12},{10,... | collective-permute-start | bytes 49160 | tf_op jit(solution)/shard_map/ppermute | solution.py:296
  38.2 4.4 %collective-permute-start.20 = (f32[32,128]{1,0:T(8,128)S(1)}, f32[32,128]{1,0:T(8,128)S(1)}, u32[]{:S(2)}, u32[]{:S(2)}) collective-permute-start(f32[32,128]{1,0:T(8,128)S(1)} %add.18), channel_id=1, source_target_pairs={{0,6},{1,7},{2,4},{3,5},{4,2},{5,3},{6,0},{7,1},{8,14},{9,15},{10,... | collective-permute-start | bytes 49160 | tf_op jit(solution)/shard_map/ppermute | solution.py:296

commit v4 on v3

--- a/solution.py
+++ b/solution.py
@@ -8,6 +8,7 @@
 from jax.sharding import PartitionSpec as P
 
 time_step = 0.4
+arrival = (1, 2, 3, 0)
 lanes = 128
 sublanes = 8
 HIGHEST = lax.Precision.HIGHEST
@@ -180,7 +181,7 @@
     refs = list(refs)
     last = stage == 3
     part_refs = [refs.pop(0) for _ in range(1 if last else 2)]
-    recv_refs = [refs.pop(0) for _ in range(4)]
+    recv_refs = dict(zip(arrival, (refs.pop(0) for _ in range(4))))
     kept_coef, next_coef = coefficients(stage)
     fields, vectors, cells = part_refs[0].shape
     groups = vectors // sublanes
@@ -332,7 +333,7 @@
 
     def exchange(sent):
         got = [None] * 4
-        for which in (0, 3, 2, 1):
+        for which in arrival:
             got[which] = lax.ppermute(sent[which], ("gx", "gy"), pairs[which])
         return got
 
@@ -389,7 +390,7 @@
             out_specs=[vmem] * (2 if last else 6),
             compiler_params=params,
             name="ghost",
-        )(outside, ghost_coef, centre, group, send_table, *partial, *got)
+        )(outside, ghost_coef, centre, group, send_table, *partial, *[got[b] for b in arrival])
         held, sent = result[1::-1], result[2:]
     gram, advanced = held
     gram = summed(gram, rows, cols)

time: 45.6 us -> 44.2 us (0.969)
  waiting for transfers between devices: 12.5 us -> 11.6 us
    ppermute x16, waiting for transfers between devices: 4.39 us -> 2.8 us  [exchange(): got[which] = lax.ppermute(sent[which], ('gx', 'gy'), pairs[which])]
    ppermute x5, starting transfers between devices: 7.04 us -> 6.03 us  [summed(): value = value + lax.ppermute(value, ('gx', 'gy'), pairs)]
    ppermute x5, waiting for transfers between devices: 8.14 us -> 8.78 us  [summed(): value = value + lax.ppermute(value, ('gx', 'gy'), pairs)]
    ppermute x16, starting transfers between devices: 15.9 us -> 16.4 us  [exchange(): got[which] = lax.ppermute(sent[which], ('gx', 'gy'), pairs[which])]
  transfers between devices with their start and end apart: 21 -> 21, of which waited for: 12 -> 9; matrix products, arithmetic and copies ran while one was open for 0% -> 0% of each run, Pallas kernels for 4% -> 4%
where the time goes in v4:
time: 44.2 us; the launch traced here: 44 us
  starting transfers between devices  22.5 us (51%)
  waiting for transfers between devices  11.6 us (26%)
  Pallas kernels  6.96 us (16%)
  local copies, waits for them, and re-layouts  1.56 us (4%)
  between operations  1.47 us (3%)
    ppermute x16, starting transfers between devices, exchange(): got[which] = lax.ppermute(sent[which], ('gx', 'gy'), pairs[which])  16.4 us
    ppermute x5, waiting for transfers between devices, summed(): value = value + lax.ppermute(value, ('gx', 'gy'), pairs)  8.78 us
    ppermute x5, starting transfers between devices, summed(): value = value + lax.ppermute(value, ('gx', 'gy'), pairs)  6.03 us
    pallas_call x1, Pallas kernels, shards(): pl.pallas_call(functools.partial(factor_kernel, scale), out_shape=[state,...  2.82 us
    ppermute x16, waiting for transfers between devices, exchange(): got[which] = lax.ppermute(sent[which], ('gx', 'gy'), pairs[which])  2.8 us
    pallas_call x4, Pallas kernels, shards(): pl.pallas_call(functools.partial(ghost_kernel, stage), out_shape=[state,...  2.19 us
    unnamed x14, local copies, waits for them, and re-layouts  1.56 us
    pallas_call x4, Pallas kernels, shards(): pl.pallas_call(functools.partial(own_kernel, stage), out_shape=[state] *...  1.45 us
  transfers between devices with their start and end apart: 21, of which 9 were waited for; matrix products, arithmetic and copies ran while one was open for 0% of the time, Pallas kernels for 4%

profile of v4, /device:TPU:0, one launch (start us, length us, event | category | flops | bytes accessed | tf_op | source)
XLA Modules:
  0.0 44.0 jit_solution(6038885467244079813)
XLA Ops:
  0.7 0.9 %copy-done = f32[5,64,128]{2,1,0:T(8,128)S(1)} copy-done((f32[5,64,128]{2,1,0:T(8,128)S(1)}, f32[5,64,128]{2,1,0:T(8,128)}, u32[]{:S(2)}) %copy-start) | copy-done | bytes 163864
  1.8 3.4 %collective-permute-start = (f32[5,8,128]{2,1,0:T(8,128)S(1)}, f32[5,8,128]{2,1,0:T(8,128)S(1)}, u32[]{:S(2)}, u32[]{:S(2)}) collective-permute-start(f32[5,8,128]{2,1,0:T(8,128)S(1)} %get-tuple-element.46), channel_id=1, source_target_pairs={{0,28},{1,29},{2,30},{3,31},{4,8},{5,9},{6,10},{7,11},{8,4},{9,5},... | collective-permute-start | bytes 61448 | tf_op jit(solution)/shard_map/ppermute | solution.py:337
  5.2 1.6 %collective-permute-start.1 = (f32[5,8,128]{2,1,0:T(8,128)S(1)}, f32[5,8,128]{2,1,0:T(8,128)S(1)}, u32[]{:S(2)}, u32[]{:S(2)}) collective-permute-start(f32[5,8,128]{2,1,0:T(8,128)S(1)} %get-tuple-element.47), channel_id=1, source_target_pairs={{0,1},{1,0},{2,3},{3,2},{4,5},{5,4},{6,7},{7,6},{8,9},{9,8},{10,11... | collective-permute-start | bytes 61448 | tf_op jit(solution)/shard_map/ppermute | solution.py:337
  6.8 0.5 %collective-permute-start.3 = (f32[5,8,128]{2,1,0:T(8,128)S(1)}, f32[5,8,128]{2,1,0:T(8,128)S(1)}, u32[]{:S(2)}, u32[]{:S(2)}) collective-permute-start(f32[5,8,128]{2,1,0:T(8,128)S(1)} %get-tuple-element.49), channel_id=1, source_target_pairs={{0,4},{1,5},{2,6},{3,7},{4,0},{5,1},{6,2},{7,3},{8,12},{9,13},{10,... | collective-permute-start | bytes 61448 | tf_op jit(solution)/shard_map/ppermute | solution.py:337
  8.0 0.6 %copy-done.3 = s32[4,128]{1,0:T(4,128)S(1)} copy-done((s32[4,128]{1,0:T(4,128)S(1)}, s32[4,128]{1,0:T(4,128)}, u32[]{:S(2)}) %copy-start.3) | copy-done | bytes 2072
  9.3 0.4 ghost.4
  9.8 0.5 %collective-permute-start.4 = (f32[5,8,128]{2,1,0:T(8,128)S(1)}, f32[5,8,128]{2,1,0:T(8,128)S(1)}, u32[]{:S(2)}, u32[]{:S(2)}) collective-permute-start(f32[5,8,128]{2,1,0:T(8,128)S(1)} %get-tuple-element.54), channel_id=1, source_target_pairs={{0,28},{1,29},{2,30},{3,31},{4,8},{5,9},{6,10},{7,11},{8,4},{9,5},... | collective-permute-start | bytes 61448 | tf_op jit(solution)/shard_map/ppermute | solution.py:337
  10.3 2.9 %collective-permute-start.5 = (f32[5,8,128]{2,1,0:T(8,128)S(1)}, f32[5,8,128]{2,1,0:T(8,128)S(1)}, u32[]{:S(2)}, u32[]{:S(2)}) collective-permute-start(f32[5,8,128]{2,1,0:T(8,128)S(1)} %get-tuple-element.55), channel_id=1, source_target_pairs={{0,1},{1,0},{2,3},{3,2},{4,5},{5,4},{6,7},{7,6},{8,9},{9,8},{10,11... | collective-permute-start | bytes 61448 | tf_op jit(solution)/shard_map/ppermute | solution.py:337
  13.2 0.5 %collective-permute-start.7 = (f32[5,8,128]{2,1,0:T(8,128)S(1)}, f32[5,8,128]{2,1,0:T(8,128)S(1)}, u32[]{:S(2)}, u32[]{:S(2)}) collective-permute-start(f32[5,8,128]{2,1,0:T(8,128)S(1)} %get-tuple-element.57), channel_id=1, source_target_pairs={{0,4},{1,5},{2,6},{3,7},{4,0},{5,1},{6,2},{7,3},{8,12},{9,13},{10,... | collective-permute-start | bytes 61448 | tf_op jit(solution)/shard_map/ppermute | solution.py:337
  14.1 0.9 %collective-permute-done.5.refs_3_ = f32[5,8,128]{2,1,0:T(8,128)S(1)} collective-permute-done((f32[5,8,128]{2,1,0:T(8,128)S(1)}, f32[5,8,128]{2,1,0:T(8,128)S(1)}, u32[]{:S(2)}, u32[]{:S(2)}) %collective-permute-start.5) | collective-permute-done | bytes 20512 | tf_op jit(solution)/shard_map/ppermute | solution.py:337
  15.0 0.4 %ghost.5 = (f32[5,64,128]{2,1,0:T(8,128)S(1)}, f32[5,64,128]{2,1,0:T(8,128)S(1)}, f32[5,8,128]{2,1,0:T(8,128)S(1)}, f32[5,8,128]{2,1,0:T(8,128)S(1)}, f32[5,8,12...) custom-call(s32[4,64,128]{2,1,0:T(8,128)S(1)} %get-tuple-element.38.outside_ref, f32[100,128]{1,0:T(8,128)S(1)} %get-tuple-element.39.coef_ref, ...), custom_call_target="tpu_custom_call" | custom-call | tf_op jit(solution)/shard_map/ghost/pallas_call | solution.py:386
  15.4 1.3 %collective-permute-start.8 = (f32[5,8,128]{2,1,0:T(8,128)S(1)}, f32[5,8,128]{2,1,0:T(8,128)S(1)}, u32[]{:S(2)}, u32[]{:S(2)}) collective-permute-start(f32[5,8,128]{2,1,0:T(8,128)S(1)} %get-tuple-element.62), channel_id=1, source_target_pairs={{0,28},{1,29},{2,30},{3,31},{4,8},{5,9},{6,10},{7,11},{8,4},{9,5},... | collective-permute-start | bytes 61448 | tf_op jit(solution)/shard_map/ppermute | solution.py:337
  16.7 2.1 %collective-permute-start.9 = (f32[5,8,128]{2,1,0:T(8,128)S(1)}, f32[5,8,128]{2,1,0:T(8,128)S(1)}, u32[]{:S(2)}, u32[]{:S(2)}) collective-permute-start(f32[5,8,128]{2,1,0:T(8,128)S(1)} %get-tuple-element.63), channel_id=1, source_target_pairs={{0,1},{1,0},{2,3},{3,2},{4,5},{5,4},{6,7},{7,6},{8,9},{9,8},{10,11... | collective-permute-start | bytes 61448 | tf_op jit(solution)/shard_map/ppermute | solution.py:337
  18.8 0.5 %collective-permute-start.11 = (f32[5,8,128]{2,1,0:T(8,128)S(1)}, f32[5,8,128]{2,1,0:T(8,128)S(1)}, u32[]{:S(2)}, u32[]{:S(2)}) collective-permute-start(f32[5,8,128]{2,1,0:T(8,128)S(1)} %get-tuple-element.65), channel_id=1, source_target_pairs={{0,4},{1,5},{2,6},{3,7},{4,0},{5,1},{6,2},{7,3},{8,12},{9,13},{10,... | collective-permute-start | bytes 61448 | tf_op jit(solution)/shard_map/ppermute | solution.py:337
  19.6 0.9 %collective-permute-done.9.refs_3_ = f32[5,8,128]{2,1,0:T(8,128)S(1)} collective-permute-done((f32[5,8,128]{2,1,0:T(8,128)S(1)}, f32[5,8,128]{2,1,0:T(8,128)S(1)}, u32[]{:S(2)}, u32[]{:S(2)}) %collective-permute-start.9) | collective-permute-done | bytes 20512 | tf_op jit(solution)/shard_map/ppermute | solution.py:337
  20.5 0.4 %ghost.6 = (f32[5,64,128]{2,1,0:T(8,128)S(1)}, f32[5,64,128]{2,1,0:T(8,128)S(1)}, f32[5,8,128]{2,1,0:T(8,128)S(1)}, f32[5,8,128]{2,1,0:T(8,128)S(1)}, f32[5,8,12...) custom-call(s32[4,64,128]{2,1,0:T(8,128)S(1)} %get-tuple-element.38.outside_ref, f32[100,128]{1,0:T(8,128)S(1)} %get-tuple-element.39.coef_ref, ...), custom_call_target="tpu_custom_call" | custom-call | tf_op jit(solution)/shard_map/ghost/pallas_call | solution.py:386
  21.0 0.8 %collective-permute-start.12 = (f32[5,8,128]{2,1,0:T(8,128)S(1)}, f32[5,8,128]{2,1,0:T(8,128)S(1)}, u32[]{:S(2)}, u32[]{:S(2)}) collective-permute-start(f32[5,8,128]{2,1,0:T(8,128)S(1)} %get-tuple-element.68), channel_id=1, source_target_pairs={{0,28},{1,29},{2,30},{3,31},{4,8},{5,9},{6,10},{7,11},{8,4},{9,5},... | collective-permute-start | bytes 61448 | tf_op jit(solution)/shard_map/ppermute | solution.py:337
  21.7 1.9 %collective-permute-start.13 = (f32[5,8,128]{2,1,0:T(8,128)S(1)}, f32[5,8,128]{2,1,0:T(8,128)S(1)}, u32[]{:S(2)}, u32[]{:S(2)}) collective-permute-start(f32[5,8,128]{2,1,0:T(8,128)S(1)} %get-tuple-element.69), channel_id=1, source_target_pairs={{0,1},{1,0},{2,3},{3,2},{4,5},{5,4},{6,7},{7,6},{8,9},{9,8},{10,11... | collective-permute-start | bytes 61448 | tf_op jit(solution)/shard_map/ppermute | solution.py:337
  23.6 0.5 %collective-permute-start.15 = (f32[5,8,128]{2,1,0:T(8,128)S(1)}, f32[5,8,128]{2,1,0:T(8,128)S(1)}, u32[]{:S(2)}, u32[]{:S(2)}) collective-permute-start(f32[5,8,128]{2,1,0:T(8,128)S(1)} %get-tuple-element.71), channel_id=1, source_target_pairs={{0,4},{1,5},{2,6},{3,7},{4,0},{5,1},{6,2},{7,3},{8,12},{9,13},{10,... | collective-permute-start | bytes 61448 | tf_op jit(solution)/shard_map/ppermute | solution.py:337
  24.5 0.7 %collective-permute-done.12.refs_1_ = f32[5,8,128]{2,1,0:T(8,128)S(1)} collective-permute-done((f32[5,8,128]{2,1,0:T(8,128)S(1)}, f32[5,8,128]{2,1,0:T(8,128)S(1)}, u32[]{:S(2)}, u32[]{:S(2)}) %collective-permute-start.12) | collective-permute-done | bytes 20512 | tf_op jit(solution)/shard_map/ppermute | solution.py:337
  25.1 0.4 collective-permute-done.13.refs_2_
  25.5 0.9 %ghost.7 = (f32[5,64,128]{2,1,0:T(8,128)S(1)}, f32[32,128]{1,0:T(8,128)S(1)}) custom-call(s32[4,64,128]{2,1,0:T(8,128)S(1)} %get-tuple-element.38.outside_ref, f32[100,128]{1,0:T(8,128)S(1)} %get-tuple-element.39.coef_ref, f32[2,8,128]{2,1,0:T(8,128)S(1)} %get-tuple-element.40.centre_ref, s32[8,128]{1,0:T(8,128)S(1)} %groups.1.group_ref, ...), custom_call_target="tpu_custom_call" | custom-call | tf_op jit(solution)/shard_map/ghost/pallas_call | solution.py:386
  26.4 1.2 %collective-permute-done.16 = f32[32,128]{1,0:T(8,128)S(1)} collective-permute-done((f32[32,128]{1,0:T(8,128)S(1)}, f32[32,128]{1,0:T(8,128)S(1)}, u32[]{:S(2)}, u32[]{:S(2)}) %collective-permute-start.16) | collective-permute-done | bytes 16416 | tf_op jit(solution)/shard_map/ppermute | solution.py:297
  27.6 0.9 %collective-permute-start.17 = (f32[32,128]{1,0:T(8,128)S(1)}, f32[32,128]{1,0:T(8,128)S(1)}, u32[]{:S(2)}, u32[]{:S(2)}) collective-permute-start(f32[32,128]{1,0:T(8,128)S(1)} %add.15), channel_id=1, source_target_pairs={{0,12},{1,13},{2,14},{3,15},{4,8},{5,9},{6,10},{7,11},{8,4},{9,5},... | collective-permute-start | bytes 49160 | tf_op jit(solution)/shard_map/ppermute | solution.py:297
  28.5 2.2 %collective-permute-done.17 = f32[32,128]{1,0:T(8,128)S(1)} collective-permute-done((f32[32,128]{1,0:T(8,128)S(1)}, f32[32,128]{1,0:T(8,128)S(1)}, u32[]{:S(2)}, u32[]{:S(2)}) %collective-permute-start.17) | collective-permute-done | bytes 16416 | tf_op jit(solution)/shard_map/ppermute | solution.py:297
  30.7 0.8 %collective-permute-start.18 = (f32[32,128]{1,0:T(8,128)S(1)}, f32[32,128]{1,0:T(8,128)S(1)}, u32[]{:S(2)}, u32[]{:S(2)}) collective-permute-start(f32[32,128]{1,0:T(8,128)S(1)} %add.16), channel_id=1, source_target_pairs={{0,20},{1,21},{2,22},{3,23},{4,16},{5,17},{6,18},{7,19},{8,28},{9,... | collective-permute-start | bytes 49160 | tf_op jit(solution)/shard_map/ppermute | solution.py:297
  31.5 2.4 %collective-permute-done.18 = f32[32,128]{1,0:T(8,128)S(1)} collective-permute-done((f32[32,128]{1,0:T(8,128)S(1)}, f32[32,128]{1,0:T(8,128)S(1)}, u32[]{:S(2)}, u32[]{:S(2)}) %collective-permute-start.18) | collective-permute-done | bytes 16416 | tf_op jit(solution)/shard_map/ppermute | solution.py:297
  33.9 1.8 %collective-permute-start.19 = (f32[32,128]{1,0:T(8,128)S(1)}, f32[32,128]{1,0:T(8,128)S(1)}, u32[]{:S(2)}, u32[]{:S(2)}) collective-permute-start(f32[32,128]{1,0:T(8,128)S(1)} %add.17), channel_id=1, source_target_pairs={{0,5},{1,4},{2,7},{3,6},{4,1},{5,0},{6,3},{7,2},{8,13},{9,12},{10,... | collective-permute-start | bytes 49160 | tf_op jit(solution)/shard_map/ppermute | solution.py:297
  35.7 1.4 %collective-permute-done.19 = f32[32,128]{1,0:T(8,128)S(1)} collective-permute-done((f32[32,128]{1,0:T(8,128)S(1)}, f32[32,128]{1,0:T(8,128)S(1)}, u32[]{:S(2)}, u32[]{:S(2)}) %collective-permute-start.19) | collective-permute-done | bytes 16416 | tf_op jit(solution)/shard_map/ppermute | solution.py:297
  37.2 2.5 %collective-permute-start.20 = (f32[32,128]{1,0:T(8,128)S(1)}, f32[32,128]{1,0:T(8,128)S(1)}, u32[]{:S(2)}, u32[]{:S(2)}) collective-permute-start(f32[32,128]{1,0:T(8,128)S(1)} %add.18), channel_id=1, source_target_pairs={{0,6},{1,7},{2,4},{3,5},{4,2},{5,3},{6,0},{7,1},{8,14},{9,15},{10,... | collective-permute-start | bytes 49160 | tf_op jit(solution)/shard_map/ppermute | solution.py:297
  39.7 1.5 %collective-permute-done.20 = f32[32,128]{1,0:T(8,128)S(1)} collective-permute-done((f32[32,128]{1,0:T(8,128)S(1)}, f32[32,128]{1,0:T(8,128)S(1)}, u32[]{:S(2)}, u32[]{:S(2)}) %collective-permute-start.20) | collective-permute-done | bytes 16416 | tf_op jit(solution)/shard_map/ppermute | solution.py:297
  41.2 2.8 %factor.1 = (f32[5,64,128]{2,1,0:T(8,128)}, f32[64,64]{1,0:T(8,128)}) custom-call(f32[32,128]{1,0:T(8,128)S(1)} %add.19.gram_ref, f32[5,64,128]{2,1,0:T(8,128)S(1)} %get-tuple-element.73.advanced_ref), custom_call_target="tpu_custom_call" | custom-call | tf_op jit(solution)/shard_map/factor/pallas_call | solution.py:398
  (41 shorter events, 2.1 us)
Async XLA Ops:
  0.6 0.9 %copy-start = (f32[5,64,128]{2,1,0:T(8,128)S(1)}, f32[5,64,128]{2,1,0:T(8,128)}, u32[]{:S(2)}) copy-start(f32[5,64,128]{2,1,0:T(8,128)} %q_ref.9) | copy-start | bytes 491524
  0.6 0.9 %copy-start.2 = (s32[4,16]{1,0:T(4,128)S(1)}, s32[4,16]{1,0:T(4,128)}, u32[]{:S(2)}) copy-start(s32[4,16]{1,0:T(4,128)} %send_ref.1) | copy-start | bytes 772
  1.8 6.2 %copy-start.1 = (f32[4,5,5]{2,0,1:T(4,128)S(1)}, f32[4,5,5]{2,0,1:T(4,128)}, u32[]{:S(2)}) copy-start(f32[4,5,5]{2,0,1:T(4,128)} %param.9) | copy-start | bytes 1204
  1.8 7.4 %collective-permute-start = (f32[5,8,128]{2,1,0:T(8,128)S(1)}, f32[5,8,128]{2,1,0:T(8,128)S(1)}, u32[]{:S(2)}, u32[]{:S(2)}) collective-permute-start(f32[5,8,128]{2,1,0:T(8,128)S(1)} %get-tuple-element.46), channel_id=1, source_target_pairs={{0,28},{1,29},{2,30},{3,31},{4,8},{5,9},{6,10},{7,11},{8,4},{9,5},... | collective-permute-start | bytes 61448 | tf_op jit(solution)/shard_map/ppermute | solution.py:337
  5.2 4.0 %collective-permute-start.1 = (f32[5,8,128]{2,1,0:T(8,128)S(1)}, f32[5,8,128]{2,1,0:T(8,128)S(1)}, u32[]{:S(2)}, u32[]{:S(2)}) collective-permute-start(f32[5,8,128]{2,1,0:T(8,128)S(1)} %get-tuple-element.47), channel_id=1, source_target_pairs={{0,1},{1,0},{2,3},{3,2},{4,5},{5,4},{6,7},{7,6},{8,9},{9,8},{10,11... | collective-permute-start | bytes 61448 | tf_op jit(solution)/shard_map/ppermute | solution.py:337
  6.8 2.5 %collective-permute-start.2 = (f32[5,8,128]{2,1,0:T(8,128)S(1)}, f32[5,8,128]{2,1,0:T(8,128)S(1)}, u32[]{:S(2)}, u32[]{:S(2)}) collective-permute-start(f32[5,8,128]{2,1,0:T(8,128)S(1)} %get-tuple-element.48), channel_id=1, source_target_pairs={{0,4},{1,2},{2,1},{3,7},{4,0},{5,6},{6,5},{7,3},{8,12},{9,10},{10,... | collective-permute-start | bytes 61448 | tf_op jit(solution)/shard_map/ppermute | solution.py:337
  6.8 2.5 %collective-permute-start.3 = (f32[5,8,128]{2,1,0:T(8,128)S(1)}, f32[5,8,128]{2,1,0:T(8,128)S(1)}, u32[]{:S(2)}, u32[]{:S(2)}) collective-permute-start(f32[5,8,128]{2,1,0:T(8,128)S(1)} %get-tuple-element.49), channel_id=1, source_target_pairs={{0,4},{1,5},{2,6},{3,7},{4,0},{5,1},{6,2},{7,3},{8,12},{9,13},{10,... | collective-permute-start | bytes 61448 | tf_op jit(solution)/shard_map/ppermute | solution.py:337
  8.0 0.7 %copy-start.3 = (s32[4,128]{1,0:T(4,128)S(1)}, s32[4,128]{1,0:T(4,128)}, u32[]{:S(2)}) copy-start(s32[4,128]{1,0:T(4,128)} %conn_ref.1) | copy-start | bytes 6148
  8.0 0.7 %copy-start.4 = (f32[128]{0:T(128)S(1)}, f32[128]{0:T(128)}, u32[]{:S(2)}) copy-start(f32[128]{0:T(128)} %param.10) | copy-start | bytes 1540
  8.0 0.7 %copy-start.5 = (f32[128]{0:T(128)S(1)}, f32[128]{0:T(128)}, u32[]{:S(2)}) copy-start(f32[128]{0:T(128)} %param.11) | copy-start | bytes 1540
  8.0 0.7 %copy-start.6 = (f32[128]{0:T(128)S(1)}, f32[128]{0:T(128)}, u32[]{:S(2)}) copy-start(f32[128]{0:T(128)} %param.12) | copy-start | bytes 1540
  9.8 4.3 %collective-permute-start.4 = (f32[5,8,128]{2,1,0:T(8,128)S(1)}, f32[5,8,128]{2,1,0:T(8,128)S(1)}, u32[]{:S(2)}, u32[]{:S(2)}) collective-permute-start(f32[5,8,128]{2,1,0:T(8,128)S(1)} %get-tuple-element.54), channel_id=1, source_target_pairs={{0,28},{1,29},{2,30},{3,31},{4,8},{5,9},{6,10},{7,11},{8,4},{9,5},... | collective-permute-start | bytes 61448 | tf_op jit(solution)/shard_map/ppermute | solution.py:337
  10.3 4.7 %collective-permute-start.5 = (f32[5,8,128]{2,1,0:T(8,128)S(1)}, f32[5,8,128]{2,1,0:T(8,128)S(1)}, u32[]{:S(2)}, u32[]{:S(2)}) collective-permute-start(f32[5,8,128]{2,1,0:T(8,128)S(1)} %get-tuple-element.55), channel_id=1, source_target_pairs={{0,1},{1,0},{2,3},{3,2},{4,5},{5,4},{6,7},{7,6},{8,9},{9,8},{10,11... | collective-permute-start | bytes 61448 | tf_op jit(solution)/shard_map/ppermute | solution.py:337
  13.2 1.8 %collective-permute-start.6 = (f32[5,8,128]{2,1,0:T(8,128)S(1)}, f32[5,8,128]{2,1,0:T(8,128)S(1)}, u32[]{:S(2)}, u32[]{:S(2)}) collective-permute-start(f32[5,8,128]{2,1,0:T(8,128)S(1)} %get-tuple-element.56), channel_id=1, source_target_pairs={{0,4},{1,2},{2,1},{3,7},{4,0},{5,6},{6,5},{7,3},{8,12},{9,10},{10,... | collective-permute-start | bytes 61448 | tf_op jit(solution)/shard_map/ppermute | solution.py:337
  13.2 1.8 %collective-permute-start.7 = (f32[5,8,128]{2,1,0:T(8,128)S(1)}, f32[5,8,128]{2,1,0:T(8,128)S(1)}, u32[]{:S(2)}, u32[]{:S(2)}) collective-permute-start(f32[5,8,128]{2,1,0:T(8,128)S(1)} %get-tuple-element.57), channel_id=1, source_target_pairs={{0,4},{1,5},{2,6},{3,7},{4,0},{5,1},{6,2},{7,3},{8,12},{9,13},{10,... | collective-permute-start | bytes 61448 | tf_op jit(solution)/shard_map/ppermute | solution.py:337
  15.4 4.2 %collective-permute-start.8 = (f32[5,8,128]{2,1,0:T(8,128)S(1)}, f32[5,8,128]{2,1,0:T(8,128)S(1)}, u32[]{:S(2)}, u32[]{:S(2)}) collective-permute-start(f32[5,8,128]{2,1,0:T(8,128)S(1)} %get-tuple-element.62), channel_id=1, source_target_pairs={{0,28},{1,29},{2,30},{3,31},{4,8},{5,9},{6,10},{7,11},{8,4},{9,5},... | collective-permute-start | bytes 61448 | tf_op jit(solution)/shard_map/ppermute | solution.py:337
  16.7 3.8 %collective-permute-start.9 = (f32[5,8,128]{2,1,0:T(8,128)S(1)}, f32[5,8,128]{2,1,0:T(8,128)S(1)}, u32[]{:S(2)}, u32[]{:S(2)}) collective-permute-start(f32[5,8,128]{2,1,0:T(8,128)S(1)} %get-tuple-element.63), channel_id=1, source_target_pairs={{0,1},{1,0},{2,3},{3,2},{4,5},{5,4},{6,7},{7,6},{8,9},{9,8},{10,11... | collective-permute-start | bytes 61448 | tf_op jit(solution)/shard_map/ppermute | solution.py:337
  18.8 1.8 %collective-permute-start.10 = (f32[5,8,128]{2,1,0:T(8,128)S(1)}, f32[5,8,128]{2,1,0:T(8,128)S(1)}, u32[]{:S(2)}, u32[]{:S(2)}) collective-permute-start(f32[5,8,128]{2,1,0:T(8,128)S(1)} %get-tuple-element.64), channel_id=1, source_target_pairs={{0,4},{1,2},{2,1},{3,7},{4,0},{5,6},{6,5},{7,3},{8,12},{9,10},{10,... | collective-permute-start | bytes 61448 | tf_op jit(solution)/shard_map/ppermute | solution.py:337
  18.8 1.8 %collective-permute-start.11 = (f32[5,8,128]{2,1,0:T(8,128)S(1)}, f32[5,8,128]{2,1,0:T(8,128)S(1)}, u32[]{:S(2)}, u32[]{:S(2)}) collective-permute-start(f32[5,8,128]{2,1,0:T(8,128)S(1)} %get-tuple-element.65), channel_id=1, source_target_pairs={{0,4},{1,5},{2,6},{3,7},{4,0},{5,1},{6,2},{7,3},{8,12},{9,13},{10,... | collective-permute-start | bytes 61448 | tf_op jit(solution)/shard_map/ppermute | solution.py:337
  21.0 4.2 %collective-permute-start.12 = (f32[5,8,128]{2,1,0:T(8,128)S(1)}, f32[5,8,128]{2,1,0:T(8,128)S(1)}, u32[]{:S(2)}, u32[]{:S(2)}) collective-permute-start(f32[5,8,128]{2,1,0:T(8,128)S(1)} %get-tuple-element.68), channel_id=1, source_target_pairs={{0,28},{1,29},{2,30},{3,31},{4,8},{5,9},{6,10},{7,11},{8,4},{9,5},... | collective-permute-start | bytes 61448 | tf_op jit(solution)/shard_map/ppermute | solution.py:337
  21.7 3.8 %collective-permute-start.13 = (f32[5,8,128]{2,1,0:T(8,128)S(1)}, f32[5,8,128]{2,1,0:T(8,128)S(1)}, u32[]{:S(2)}, u32[]{:S(2)}) collective-permute-start(f32[5,8,128]{2,1,0:T(8,128)S(1)} %get-tuple-element.69), channel_id=1, source_target_pairs={{0,1},{1,0},{2,3},{3,2},{4,5},{5,4},{6,7},{7,6},{8,9},{9,8},{10,11... | collective-permute-start | bytes 61448 | tf_op jit(solution)/shard_map/ppermute | solution.py:337
  23.6 1.9 %collective-permute-start.14 = (f32[5,8,128]{2,1,0:T(8,128)S(1)}, f32[5,8,128]{2,1,0:T(8,128)S(1)}, u32[]{:S(2)}, u32[]{:S(2)}) collective-permute-start(f32[5,8,128]{2,1,0:T(8,128)S(1)} %get-tuple-element.70), channel_id=1, source_target_pairs={{0,4},{1,2},{2,1},{3,7},{4,0},{5,6},{6,5},{7,3},{8,12},{9,10},{10,... | collective-permute-start | bytes 61448 | tf_op jit(solution)/shard_map/ppermute | solution.py:337
  23.6 1.9 %collective-permute-start.15 = (f32[5,8,128]{2,1,0:T(8,128)S(1)}, f32[5,8,128]{2,1,0:T(8,128)S(1)}, u32[]{:S(2)}, u32[]{:S(2)}) collective-permute-start(f32[5,8,128]{2,1,0:T(8,128)S(1)} %get-tuple-element.71), channel_id=1, source_target_pairs={{0,4},{1,5},{2,6},{3,7},{4,0},{5,1},{6,2},{7,3},{8,12},{9,13},{10,... | collective-permute-start | bytes 61448 | tf_op jit(solution)/shard_map/ppermute | solution.py:337
  26.4 1.2 %collective-permute-start.16 = (f32[32,128]{1,0:T(8,128)S(1)}, f32[32,128]{1,0:T(8,128)S(1)}, u32[]{:S(2)}, u32[]{:S(2)}) collective-permute-start(f32[32,128]{1,0:T(8,128)S(1)} %get-tuple-element.72), channel_id=1, source_target_pairs={{0,4},{1,5},{2,6},{3,7},{4,0},{5,1},{6,2},{7,3},{8,12},{9,13},{10,... | collective-permute-start | bytes 49160 | tf_op jit(solution)/shard_map/ppermute | solution.py:297
  27.6 3.2 %collective-permute-start.17 = (f32[32,128]{1,0:T(8,128)S(1)}, f32[32,128]{1,0:T(8,128)S(1)}, u32[]{:S(2)}, u32[]{:S(2)}) collective-permute-start(f32[32,128]{1,0:T(8,128)S(1)} %add.15), channel_id=1, source_target_pairs={{0,12},{1,13},{2,14},{3,15},{4,8},{5,9},{6,10},{7,11},{8,4},{9,5},... | collective-permute-start | bytes 49160 | tf_op jit(solution)/shard_map/ppermute | solution.py:297
  30.7 3.2 %collective-permute-start.18 = (f32[32,128]{1,0:T(8,128)S(1)}, f32[32,128]{1,0:T(8,128)S(1)}, u32[]{:S(2)}, u32[]{:S(2)}) collective-permute-start(f32[32,128]{1,0:T(8,128)S(1)} %add.16), channel_id=1, source_target_pairs={{0,20},{1,21},{2,22},{3,23},{4,16},{5,17},{6,18},{7,19},{8,28},{9,... | collective-permute-start | bytes 49160 | tf_op jit(solution)/shard_map/ppermute | solution.py:297
  33.9 3.2 %collective-permute-start.19 = (f32[32,128]{1,0:T(8,128)S(1)}, f32[32,128]{1,0:T(8,128)S(1)}, u32[]{:S(2)}, u32[]{:S(2)}) collective-permute-start(f32[32,128]{1,0:T(8,128)S(1)} %add.17), channel_id=1, source_target_pairs={{0,5},{1,4},{2,7},{3,6},{4,1},{5,0},{6,3},{7,2},{8,13},{9,12},{10,... | collective-permute-start | bytes 49160 | tf_op jit(solution)/shard_map/ppermute | solution.py:297
  37.2 4.1 %collective-permute-start.20 = (f32[32,128]{1,0:T(8,128)S(1)}, f32[32,128]{1,0:T(8,128)S(1)}, u32[]{:S(2)}, u32[]{:S(2)}) collective-permute-start(f32[32,128]{1,0:T(8,128)S(1)} %add.18), channel_id=1, source_target_pairs={{0,6},{1,7},{2,4},{3,5},{4,2},{5,3},{6,0},{7,1},{8,14},{9,15},{10,... | collective-permute-start | bytes 49160 | tf_op jit(solution)/shard_map/ppermute | solution.py:297

commit v5 on v4

--- a/solution.py
+++ b/solution.py
@@ -8,6 +8,7 @@
 from jax.sharding import PartitionSpec as P
 
 time_step = 0.4
+slope_coef = (0.5 * time_step, 0.5 * time_step, time_step, time_step / 6.0)
 arrival = (1, 2, 3, 0)
 lanes = 128
 sublanes = 8
@@ -144,11 +145,6 @@
             ghost_coef_ref[rows, :] = jnp.where((owned | far)[:fields], 0.0, coef)
 
 
-def coefficients(stage):
-    kept = time_step / 6.0 if stage in (0, 3) else time_step / 3.0
-    return kept, (0.5 * time_step, 0.5 * time_step, time_step, None)[stage]
-
-
 def neighbours(near, coef_ref, totals, face):
     fields = len(near)
     for j in range(fields):
@@ -159,31 +155,30 @@
 
 
 def own_kernel(stage, centre_ref, inside_ref, coef_ref, q_ref, *refs):
-    refs = list(refs)
-    state_ref = q_ref if stage == 0 else refs.pop(0)
-    acc_ref = q_ref if stage == 0 else refs.pop(0)
-    kept_coef, next_coef = coefficients(stage)
+    *state_refs, part_ref = refs
+    newest_ref = state_refs[-1] if state_refs else q_ref
     fields, vectors, _ = q_ref.shape
     for start in range(0, vectors, sublanes):
         rows = pl.ds(start, sublanes)
-        own = [state_ref[f, rows, :] for f in range(fields)]
+        own = [newest_ref[f, rows, :] for f in range(fields)]
         totals = [centre_ref[0] * own[f] for f in range(fields)]
         for face in range(4):
             near = [lane_take(own[f], inside_ref[face]) for f in range(fields)]
             neighbours(near, coef_ref, totals, face)
         for f in range(fields):
-            refs[0][f, rows, :] = acc_ref[f, rows, :] + kept_coef * totals[f]
-            if next_coef is not None:
-                refs[1][f, rows, :] = q_ref[f, rows, :] + next_coef * totals[f]
+            beside = q_ref[f, rows, :]
+            if stage == 3:
+                second, third = (ref[f, rows, :] for ref in state_refs[:2])
+                beside = (second + 2.0 * third + own[f] - beside) * (1.0 / 3.0)
+            part_ref[f, rows, :] = beside + slope_coef[stage] * totals[f]
 
 
 def ghost_kernel(stage, outside_ref, coef_ref, centre_ref, group_ref, send_table_ref, *refs):
     refs = list(refs)
     last = stage == 3
-    part_refs = [refs.pop(0) for _ in range(1 if last else 2)]
+    part_ref = refs.pop(0)
     recv_refs = dict(zip(arrival, (refs.pop(0) for _ in range(4))))
-    kept_coef, next_coef = coefficients(stage)
-    fields, vectors, cells = part_refs[0].shape
+    fields, vectors, _ = part_ref.shape
     groups = vectors // sublanes
     group = group_ref[...]
     states = []
@@ -201,73 +196,88 @@
             neighbours(near, coef_ref, totals, face)
         following = []
         for f in range(fields):
-            kept = part_refs[0][f, rows, :] + kept_coef * totals[f]
-            refs[0][f, rows, :] = kept * centre_ref[1] if last else kept
-            if not last:
-                after = part_refs[1][f, rows, :] + next_coef * totals[f]
-                refs[1][f, rows, :] = after
-                following.append(after)
+            after = part_ref[f, rows, :] + slope_coef[stage] * totals[f]
+            if last:
+                after = after * centre_ref[1]
+            refs[0][f, rows, :] = after
+            following.append(after)
         states.append(following)
     if not last:
-        pack(states, group, send_table_ref, refs[2:], groups)
+        pack(states, group, send_table_ref, refs[1:], groups)
         return
     half = vectors // 2
     wide = jnp.concatenate([refs[0][f] for f in range(fields)], axis=1)
     gram = lax.dot_general(
         wide,
-        jnp.concatenate([wide, jnp.zeros_like(wide)], axis=0),
+        wide,
         (((1,), (1,)), ((), ())),
         precision=HIGHEST,
         preferred_element_type=jnp.float32,
     )
+    gram = jnp.concatenate([gram, jnp.zeros_like(gram)], axis=1)
     refs[1][...] = gram[:half] + pltpu.roll(gram[half:], vectors, 1)
 
 
-def factor_kernel(scale, gram_ref, advanced_ref, basis_ref, factor_ref):
+def factor_kernel(scale, gram_ref, advanced_ref, basis_hbm, factor_hbm, basis_ref, factor_ref, sem_ref):
     fields, vectors, cells = advanced_ref.shape
-    half = vectors // 2
     folded = gram_ref[...] * scale
-    turned = pltpu.roll(folded, vectors, 1)
-    work = jnp.concatenate([folded, turned], axis=0)
+    work = jnp.concatenate([folded, pltpu.roll(folded, vectors, 1)], axis=0)
     row = lax.broadcasted_iota(jnp.int32, (vectors, lanes), 0)
     lane = lax.broadcasted_iota(jnp.int32, (vectors, lanes), 1)
-    work = jnp.where(lane < vectors, work, jnp.where(lane == row + vectors, 1.0, 0.0))
-    blocks = [work[b * sublanes : (b + 1) * sublanes] for b in range(vectors // sublanes)]
-    sub = lax.broadcasted_iota(jnp.int32, (sublanes, lanes), 0)
-    scales = []
+    shape = (sublanes, lanes)
+    sub = lax.broadcasted_iota(jnp.int32, shape, 0)
+    diagonal = jnp.where(lane == row, work, 0.0)
+    by_row = lax.rsqrt(jnp.sum(diagonal, axis=1, keepdims=True))
+    by_lane = jnp.sum(diagonal, axis=0, keepdims=True)
+    lane_root = lax.rsqrt(by_lane)
+    work = jnp.where(
+        lane < vectors,
+        work * by_row * lane_root,
+        jnp.where(lane == row + vectors, 1.0, 0.0),
+    )
+    restore = jnp.where(
+        lane[:1] < vectors, by_lane * lane_root, pltpu.roll(lane_root, vectors, 1)
+    )
+    blocks = [work[at : at + sublanes] for at in range(0, vectors, sublanes)]
+
+    def spread(tile, k):
+        return jnp.broadcast_to(tile[k : k + 1], shape)
+
     for b in range(len(blocks)):
         start = b * sublanes
-        count = len(blocks) - b
+        later = range(b, len(blocks))
         columns = [
-            [
-                jnp.broadcast_to(blocks[c][:, start + k : start + k + 1], (sublanes, lanes))
-                for c in range(b, len(blocks))
-            ]
+            [lane_take(blocks[c], jnp.full(shape, start + k, jnp.int32)) for c in later]
             for k in range(sublanes)
         ]
-        for k in range(sublanes):
-            pivot = jnp.broadcast_to(columns[k][0][k : k + 1], (sublanes, lanes))
-            scales.append(pivot)
-            inverse = 1.0 / pivot
-            row_k = jnp.broadcast_to(blocks[b][k : k + 1], (sublanes, lanes)) * inverse
-            later = [
-                jnp.broadcast_to(columns[n][0][k : k + 1], (sublanes, lanes)) * inverse
-                for n in range(k + 1, sublanes)
-            ]
-            for c in range(count):
-                ratio = columns[k][c]
+        pivots = None
+        for k in range(0, sublanes, 2):
+            left, right = columns[k], columns[k + 1]
+            p, q, r = spread(left[0], k), spread(right[0], k), spread(right[0], k + 1)
+            first = 1.0 / p
+            second = p * (1.0 / (p * r - q * q))
+            ratio = q * first
+            right = [right[c] - ratio * left[c] for c in range(len(later))]
+            top, bottom = spread(blocks[b], k), spread(blocks[b], k + 1)
+            bottom = bottom - ratio * top
+            upper, lower = top * first, bottom * second
+            for n in range(k + 2, sublanes):
+                high, low = spread(columns[n][0], k), spread(columns[n][0], k + 1)
+                high, low = high * first, (low - ratio * high) * second
+                for c in range(len(later)):
+                    columns[n][c] = columns[n][c] - (left[c] * high + right[c] * low)
+            for c in range(len(later)):
+                change = left[c] * upper + right[c] * lower
                 if c == 0:
-                    ratio = jnp.where(sub > k, ratio, 0.0)
-                blocks[b + c] = blocks[b + c] - ratio * row_k
-                for n in range(k + 1, sublanes):
-                    columns[n][c] = columns[n][c] - ratio * later[n - k - 1]
-    for b in range(len(blocks)):
-        pivots = scales[b * sublanes]
-        for k in range(1, sublanes):
-            pivots = jnp.where(sub == k, scales[b * sublanes + k], pivots)
+                    change = jnp.where(sub > k + 1, change, jnp.where(sub == k + 1, ratio * top, 0.0))
+                blocks[b + c] = blocks[b + c] - change
+            pivots = p if pivots is None else jnp.where(sub >= k, p, pivots)
+            pivots = jnp.where(sub > k, r - ratio * q, pivots)
         blocks[b] = blocks[b] * lax.rsqrt(pivots)
-    done = jnp.concatenate(blocks, axis=0)
+    done = jnp.concatenate(blocks, axis=0) * restore
     factor_ref[...] = jnp.where(lane >= row, done, 0.0)[:, :vectors]
+    copies = [pltpu.make_async_copy(factor_ref, factor_hbm, sem_ref.at[fields])]
+    copies[0].start()
     inverse_lower = pltpu.roll(done, vectors, 1)[:, :vectors]
     for f in range(fields):
         basis_ref[f] = jnp.dot(
@@ -276,6 +286,10 @@
             precision=HIGHEST,
             preferred_element_type=jnp.float32,
         )
+        copies.append(pltpu.make_async_copy(basis_ref.at[f], basis_hbm.at[f], sem_ref.at[f]))
+        copies[-1].start()
+    for copy in copies:
+        copy.wait()
 
 
 def summed(value, rows, cols):
@@ -376,30 +390,37 @@
         got = exchange(sent)
         partial = pl.pallas_call(
             functools.partial(own_kernel, stage),
-            out_shape=[state] * (1 if last else 2),
+            out_shape=state,
             in_specs=[vmem] * (4 + len(held)),
-            out_specs=[vmem] * (1 if last else 2),
+            out_specs=vmem,
             compiler_params=params,
             name="own",
         )(centre, inside, own_coef, test_vectors, *held)
         gram_shape = jax.ShapeDtypeStruct((vectors // 2, lanes), jnp.float32)
-        result = pl.pallas_call(
+        newest, *sent = pl.pallas_call(
             functools.partial(ghost_kernel, stage),
-            out_shape=[state, gram_shape] if last else [state, state] + [block] * 4,
-            in_specs=[vmem] * (5 + len(partial) + 4),
-            out_specs=[vmem] * (2 if last else 6),
+            out_shape=[state, gram_shape] if last else [state] + [block] * 4,
+            in_specs=[vmem] * 10,
+            out_specs=[vmem] * (2 if last else 5),
             compiler_params=params,
             name="ghost",
-        )(outside, ghost_coef, centre, group, send_table, *partial, *[got[b] for b in arrival])
-        held, sent = result[1::-1], result[2:]
-    gram, advanced = held
+        )(outside, ghost_coef, centre, group, send_table, partial, *[got[b] for b in arrival])
+        held.append(newest)
+    advanced, gram = held[-1], sent[0]
     gram = summed(gram, rows, cols)
     scale = 1.0 / float(fields * cells * rows * cols)
+    lower = jax.ShapeDtypeStruct((vectors, vectors), jnp.float32)
+    hbm = pl.BlockSpec(memory_space=pltpu.HBM)
     return pl.pallas_call(
         functools.partial(factor_kernel, scale),
-        out_shape=[state, jax.ShapeDtypeStruct((vectors, vectors), jnp.float32)],
+        out_shape=[state, lower],
         in_specs=[vmem] * 2,
-        out_specs=[vmem] * 2,
+        out_specs=[hbm] * 2,
+        scratch_shapes=[
+            pltpu.VMEM(state.shape, jnp.float32),
+            pltpu.VMEM(lower.shape, jnp.float32),
+            pltpu.SemaphoreType.DMA((fields + 1,)),
+        ],
         compiler_params=params,
         name="factor",
     )(gram, advanced)

time: 44.2 us -> 43.8 us (level)
    pallas_call x1, Pallas kernels: 2.82 us -> 2.36 us  [shards(): pl.pallas_call(functools.partial(factor_kernel, scale), out_shape=[state,...]
where the time goes in v5:
time: 43.8 us; the launch traced here: 43.6 us
  starting transfers between devices  22.5 us (51%)
  waiting for transfers between devices  11.6 us (26%)
  Pallas kernels  6.53 us (15%)
  local copies, waits for them, and re-layouts  1.56 us (4%)
  between operations  1.47 us (3%)
    ppermute x16, starting transfers between devices, exchange(): got[which] = lax.ppermute(sent[which], ('gx', 'gy'), pairs[which])  16.4 us
    ppermute x5, waiting for transfers between devices, summed(): value = value + lax.ppermute(value, ('gx', 'gy'), pairs)  8.77 us
    ppermute x5, starting transfers between devices, summed(): value = value + lax.ppermute(value, ('gx', 'gy'), pairs)  6.04 us
    ppermute x16, waiting for transfers between devices, exchange(): got[which] = lax.ppermute(sent[which], ('gx', 'gy'), pairs[which])  2.8 us
    pallas_call x1, Pallas kernels, shards(): pl.pallas_call(functools.partial(factor_kernel, scale), out_shape=[state,...  2.36 us
    pallas_call x4, Pallas kernels, shards(): pl.pallas_call(functools.partial(ghost_kernel, stage), out_shape=[state,...  2.24 us
    unnamed x14, local copies, waits for them, and re-layouts  1.56 us
    pallas_call x4, Pallas kernels, shards(): pl.pallas_call(functools.partial(own_kernel, stage), out_shape=state, in_...  1.43 us
  transfers between devices with their start and end apart: 21, of which 9 were waited for; matrix products, arithmetic and copies ran while one was open for 0% of the time, Pallas kernels for 4%

profile of v5, /device:TPU:0, one launch (start us, length us, event | category | flops | bytes accessed | tf_op | source)
XLA Modules:
  0.0 43.6 jit_solution(14684566764261914009)
XLA Ops:
  0.7 0.9 %copy-done = f32[5,64,128]{2,1,0:T(8,128)S(1)} copy-done((f32[5,64,128]{2,1,0:T(8,128)S(1)}, f32[5,64,128]{2,1,0:T(8,128)}, u32[]{:S(2)}) %copy-start) | copy-done | bytes 163864
  1.8 3.4 %collective-permute-start = (f32[5,8,128]{2,1,0:T(8,128)S(1)}, f32[5,8,128]{2,1,0:T(8,128)S(1)}, u32[]{:S(2)}, u32[]{:S(2)}) collective-permute-start(f32[5,8,128]{2,1,0:T(8,128)S(1)} %get-tuple-element.35), channel_id=1, source_target_pairs={{0,28},{1,29},{2,30},{3,31},{4,8},{5,9},{6,10},{7,11},{8,4},{9,5},... | collective-permute-start | bytes 61448 | tf_op jit(solution)/shard_map/ppermute | solution.py:351
  5.2 1.6 %collective-permute-start.1 = (f32[5,8,128]{2,1,0:T(8,128)S(1)}, f32[5,8,128]{2,1,0:T(8,128)S(1)}, u32[]{:S(2)}, u32[]{:S(2)}) collective-permute-start(f32[5,8,128]{2,1,0:T(8,128)S(1)} %get-tuple-element.36), channel_id=1, source_target_pairs={{0,1},{1,0},{2,3},{3,2},{4,5},{5,4},{6,7},{7,6},{8,9},{9,8},{10,11... | collective-permute-start | bytes 61448 | tf_op jit(solution)/shard_map/ppermute | solution.py:351
  6.8 0.5 %collective-permute-start.3 = (f32[5,8,128]{2,1,0:T(8,128)S(1)}, f32[5,8,128]{2,1,0:T(8,128)S(1)}, u32[]{:S(2)}, u32[]{:S(2)}) collective-permute-start(f32[5,8,128]{2,1,0:T(8,128)S(1)} %get-tuple-element.38), channel_id=1, source_target_pairs={{0,4},{1,5},{2,6},{3,7},{4,0},{5,1},{6,2},{7,3},{8,12},{9,13},{10,... | collective-permute-start | bytes 61448 | tf_op jit(solution)/shard_map/ppermute | solution.py:351
  8.0 0.6 %copy-done.3 = s32[4,128]{1,0:T(4,128)S(1)} copy-done((s32[4,128]{1,0:T(4,128)S(1)}, s32[4,128]{1,0:T(4,128)}, u32[]{:S(2)}) %copy-start.3) | copy-done | bytes 2072
  9.3 0.5 %ghost.4 = (f32[5,64,128]{2,1,0:T(8,128)S(1)}, f32[5,8,128]{2,1,0:T(8,128)S(1)}, f32[5,8,128]{2,1,0:T(8,128)S(1)}, f32[5,8,128]{2,1,0:T(8,128)S(1)}, f32[5,8,128]{2,1,0:T(8,128)S(1)}) custom-call(s32[4,64,128]{2,1,0:T(8,128)S(1)} %get-tuple-element.29.outside_ref, f32[100,128]{1,0:T(8,128)S(1)} %get-tuple-element.30.coef_ref, ...), custom_call_target="tpu_custom_call" | custom-call | tf_op jit(solution)/shard_map/ghost/pallas_call | solution.py:400
  9.8 0.5 %collective-permute-start.4 = (f32[5,8,128]{2,1,0:T(8,128)S(1)}, f32[5,8,128]{2,1,0:T(8,128)S(1)}, u32[]{:S(2)}, u32[]{:S(2)}) collective-permute-start(f32[5,8,128]{2,1,0:T(8,128)S(1)} %get-tuple-element.40), channel_id=1, source_target_pairs={{0,28},{1,29},{2,30},{3,31},{4,8},{5,9},{6,10},{7,11},{8,4},{9,5},... | collective-permute-start | bytes 61448 | tf_op jit(solution)/shard_map/ppermute | solution.py:351
  10.3 2.9 %collective-permute-start.5 = (f32[5,8,128]{2,1,0:T(8,128)S(1)}, f32[5,8,128]{2,1,0:T(8,128)S(1)}, u32[]{:S(2)}, u32[]{:S(2)}) collective-permute-start(f32[5,8,128]{2,1,0:T(8,128)S(1)} %get-tuple-element.41), channel_id=1, source_target_pairs={{0,1},{1,0},{2,3},{3,2},{4,5},{5,4},{6,7},{7,6},{8,9},{9,8},{10,11... | collective-permute-start | bytes 61448 | tf_op jit(solution)/shard_map/ppermute | solution.py:351
  13.2 0.5 %collective-permute-start.7 = (f32[5,8,128]{2,1,0:T(8,128)S(1)}, f32[5,8,128]{2,1,0:T(8,128)S(1)}, u32[]{:S(2)}, u32[]{:S(2)}) collective-permute-start(f32[5,8,128]{2,1,0:T(8,128)S(1)} %get-tuple-element.43), channel_id=1, source_target_pairs={{0,4},{1,5},{2,6},{3,7},{4,0},{5,1},{6,2},{7,3},{8,12},{9,13},{10,... | collective-permute-start | bytes 61448 | tf_op jit(solution)/shard_map/ppermute | solution.py:351
  14.1 0.9 %collective-permute-done.5.refs_2_ = f32[5,8,128]{2,1,0:T(8,128)S(1)} collective-permute-done((f32[5,8,128]{2,1,0:T(8,128)S(1)}, f32[5,8,128]{2,1,0:T(8,128)S(1)}, u32[]{:S(2)}, u32[]{:S(2)}) %collective-permute-start.5) | collective-permute-done | bytes 20512 | tf_op jit(solution)/shard_map/ppermute | solution.py:351
  15.0 0.4 %ghost.5 = (f32[5,64,128]{2,1,0:T(8,128)S(1)}, f32[5,8,128]{2,1,0:T(8,128)S(1)}, f32[5,8,128]{2,1,0:T(8,128)S(1)}, f32[5,8,128]{2,1,0:T(8,128)S(1)}, f32[5,8,128]{2,1,0:T(8,128)S(1)}) custom-call(s32[4,64,128]{2,1,0:T(8,128)S(1)} %get-tuple-element.29.outside_ref, f32[100,128]{1,0:T(8,128)S(1)} %get-tuple-element.30.coef_ref, ...), custom_call_target="tpu_custom_call" | custom-call | tf_op jit(solution)/shard_map/ghost/pallas_call | solution.py:400
  15.4 1.3 %collective-permute-start.8 = (f32[5,8,128]{2,1,0:T(8,128)S(1)}, f32[5,8,128]{2,1,0:T(8,128)S(1)}, u32[]{:S(2)}, u32[]{:S(2)}) collective-permute-start(f32[5,8,128]{2,1,0:T(8,128)S(1)} %get-tuple-element.45), channel_id=1, source_target_pairs={{0,28},{1,29},{2,30},{3,31},{4,8},{5,9},{6,10},{7,11},{8,4},{9,5},... | collective-permute-start | bytes 61448 | tf_op jit(solution)/shard_map/ppermute | solution.py:351
  16.7 2.1 %collective-permute-start.9 = (f32[5,8,128]{2,1,0:T(8,128)S(1)}, f32[5,8,128]{2,1,0:T(8,128)S(1)}, u32[]{:S(2)}, u32[]{:S(2)}) collective-permute-start(f32[5,8,128]{2,1,0:T(8,128)S(1)} %get-tuple-element.46), channel_id=1, source_target_pairs={{0,1},{1,0},{2,3},{3,2},{4,5},{5,4},{6,7},{7,6},{8,9},{9,8},{10,11... | collective-permute-start | bytes 61448 | tf_op jit(solution)/shard_map/ppermute | solution.py:351
  18.8 0.5 %collective-permute-start.11 = (f32[5,8,128]{2,1,0:T(8,128)S(1)}, f32[5,8,128]{2,1,0:T(8,128)S(1)}, u32[]{:S(2)}, u32[]{:S(2)}) collective-permute-start(f32[5,8,128]{2,1,0:T(8,128)S(1)} %get-tuple-element.48), channel_id=1, source_target_pairs={{0,4},{1,5},{2,6},{3,7},{4,0},{5,1},{6,2},{7,3},{8,12},{9,13},{10,... | collective-permute-start | bytes 61448 | tf_op jit(solution)/shard_map/ppermute | solution.py:351
  19.6 0.9 %collective-permute-done.9.refs_2_ = f32[5,8,128]{2,1,0:T(8,128)S(1)} collective-permute-done((f32[5,8,128]{2,1,0:T(8,128)S(1)}, f32[5,8,128]{2,1,0:T(8,128)S(1)}, u32[]{:S(2)}, u32[]{:S(2)}) %collective-permute-start.9) | collective-permute-done | bytes 20512 | tf_op jit(solution)/shard_map/ppermute | solution.py:351
  20.5 0.4 %ghost.6 = (f32[5,64,128]{2,1,0:T(8,128)S(1)}, f32[5,8,128]{2,1,0:T(8,128)S(1)}, f32[5,8,128]{2,1,0:T(8,128)S(1)}, f32[5,8,128]{2,1,0:T(8,128)S(1)}, f32[5,8,128]{2,1,0:T(8,128)S(1)}) custom-call(s32[4,64,128]{2,1,0:T(8,128)S(1)} %get-tuple-element.29.outside_ref, f32[100,128]{1,0:T(8,128)S(1)} %get-tuple-element.30.coef_ref, ...), custom_call_target="tpu_custom_call" | custom-call | tf_op jit(solution)/shard_map/ghost/pallas_call | solution.py:400
  21.0 0.8 %collective-permute-start.12 = (f32[5,8,128]{2,1,0:T(8,128)S(1)}, f32[5,8,128]{2,1,0:T(8,128)S(1)}, u32[]{:S(2)}, u32[]{:S(2)}) collective-permute-start(f32[5,8,128]{2,1,0:T(8,128)S(1)} %get-tuple-element.50), channel_id=1, source_target_pairs={{0,28},{1,29},{2,30},{3,31},{4,8},{5,9},{6,10},{7,11},{8,4},{9,5},... | collective-permute-start | bytes 61448 | tf_op jit(solution)/shard_map/ppermute | solution.py:351
  21.7 1.9 %collective-permute-start.13 = (f32[5,8,128]{2,1,0:T(8,128)S(1)}, f32[5,8,128]{2,1,0:T(8,128)S(1)}, u32[]{:S(2)}, u32[]{:S(2)}) collective-permute-start(f32[5,8,128]{2,1,0:T(8,128)S(1)} %get-tuple-element.51), channel_id=1, source_target_pairs={{0,1},{1,0},{2,3},{3,2},{4,5},{5,4},{6,7},{7,6},{8,9},{9,8},{10,11... | collective-permute-start | bytes 61448 | tf_op jit(solution)/shard_map/ppermute | solution.py:351
  23.6 0.5 %collective-permute-start.15 = (f32[5,8,128]{2,1,0:T(8,128)S(1)}, f32[5,8,128]{2,1,0:T(8,128)S(1)}, u32[]{:S(2)}, u32[]{:S(2)}) collective-permute-start(f32[5,8,128]{2,1,0:T(8,128)S(1)} %get-tuple-element.53), channel_id=1, source_target_pairs={{0,4},{1,5},{2,6},{3,7},{4,0},{5,1},{6,2},{7,3},{8,12},{9,13},{10,... | collective-permute-start | bytes 61448 | tf_op jit(solution)/shard_map/ppermute | solution.py:351
  24.5 0.7 %collective-permute-done.12.refs_1_ = f32[5,8,128]{2,1,0:T(8,128)S(1)} collective-permute-done((f32[5,8,128]{2,1,0:T(8,128)S(1)}, f32[5,8,128]{2,1,0:T(8,128)S(1)}, u32[]{:S(2)}, u32[]{:S(2)}) %collective-permute-start.12) | collective-permute-done | bytes 20512 | tf_op jit(solution)/shard_map/ppermute | solution.py:351
  25.1 0.4 collective-permute-done.13.refs_2_
  25.5 0.9 %ghost.7 = (f32[5,64,128]{2,1,0:T(8,128)S(1)}, f32[32,128]{1,0:T(8,128)S(1)}) custom-call(s32[4,64,128]{2,1,0:T(8,128)S(1)} %get-tuple-element.29.outside_ref, f32[100,128]{1,0:T(8,128)S(1)} %get-tuple-element.30.coef_ref, f32[2,8,128]{2,1,0:T(8,128)S(1)} %get-tuple-element.31.centre_ref, s32[8,128]{1,0:T(8,128)S(1)} %groups.1.group_ref, ...), custom_call_target="tpu_custom_call" | custom-call | tf_op jit(solution)/shard_map/ghost/pallas_call | solution.py:400
  26.4 1.2 %collective-permute-done.16 = f32[32,128]{1,0:T(8,128)S(1)} collective-permute-done((f32[32,128]{1,0:T(8,128)S(1)}, f32[32,128]{1,0:T(8,128)S(1)}, u32[]{:S(2)}, u32[]{:S(2)}) %collective-permute-start.16) | collective-permute-done | bytes 16416 | tf_op jit(solution)/shard_map/ppermute | solution.py:311
  27.6 0.9 %collective-permute-start.17 = (f32[32,128]{1,0:T(8,128)S(1)}, f32[32,128]{1,0:T(8,128)S(1)}, u32[]{:S(2)}, u32[]{:S(2)}) collective-permute-start(f32[32,128]{1,0:T(8,128)S(1)} %add.15), channel_id=1, source_target_pairs={{0,12},{1,13},{2,14},{3,15},{4,8},{5,9},{6,10},{7,11},{8,4},{9,5},... | collective-permute-start | bytes 49160 | tf_op jit(solution)/shard_map/ppermute | solution.py:311
  28.5 2.2 %collective-permute-done.17 = f32[32,128]{1,0:T(8,128)S(1)} collective-permute-done((f32[32,128]{1,0:T(8,128)S(1)}, f32[32,128]{1,0:T(8,128)S(1)}, u32[]{:S(2)}, u32[]{:S(2)}) %collective-permute-start.17) | collective-permute-done | bytes 16416 | tf_op jit(solution)/shard_map/ppermute | solution.py:311
  30.8 0.8 %collective-permute-start.18 = (f32[32,128]{1,0:T(8,128)S(1)}, f32[32,128]{1,0:T(8,128)S(1)}, u32[]{:S(2)}, u32[]{:S(2)}) collective-permute-start(f32[32,128]{1,0:T(8,128)S(1)} %add.16), channel_id=1, source_target_pairs={{0,20},{1,21},{2,22},{3,23},{4,16},{5,17},{6,18},{7,19},{8,28},{9,... | collective-permute-start | bytes 49160 | tf_op jit(solution)/shard_map/ppermute | solution.py:311
  31.6 2.4 %collective-permute-done.18 = f32[32,128]{1,0:T(8,128)S(1)} collective-permute-done((f32[32,128]{1,0:T(8,128)S(1)}, f32[32,128]{1,0:T(8,128)S(1)}, u32[]{:S(2)}, u32[]{:S(2)}) %collective-permute-start.18) | collective-permute-done | bytes 16416 | tf_op jit(solution)/shard_map/ppermute | solution.py:311
  34.0 1.8 %collective-permute-start.19 = (f32[32,128]{1,0:T(8,128)S(1)}, f32[32,128]{1,0:T(8,128)S(1)}, u32[]{:S(2)}, u32[]{:S(2)}) collective-permute-start(f32[32,128]{1,0:T(8,128)S(1)} %add.17), channel_id=1, source_target_pairs={{0,5},{1,4},{2,7},{3,6},{4,1},{5,0},{6,3},{7,2},{8,13},{9,12},{10,... | collective-permute-start | bytes 49160 | tf_op jit(solution)/shard_map/ppermute | solution.py:311
  35.7 1.4 %collective-permute-done.19 = f32[32,128]{1,0:T(8,128)S(1)} collective-permute-done((f32[32,128]{1,0:T(8,128)S(1)}, f32[32,128]{1,0:T(8,128)S(1)}, u32[]{:S(2)}, u32[]{:S(2)}) %collective-permute-start.19) | collective-permute-done | bytes 16416 | tf_op jit(solution)/shard_map/ppermute | solution.py:311
  37.2 2.5 %collective-permute-start.20 = (f32[32,128]{1,0:T(8,128)S(1)}, f32[32,128]{1,0:T(8,128)S(1)}, u32[]{:S(2)}, u32[]{:S(2)}) collective-permute-start(f32[32,128]{1,0:T(8,128)S(1)} %add.18), channel_id=1, source_target_pairs={{0,6},{1,7},{2,4},{3,5},{4,2},{5,3},{6,0},{7,1},{8,14},{9,15},{10,... | collective-permute-start | bytes 49160 | tf_op jit(solution)/shard_map/ppermute | solution.py:311
  39.7 1.5 %collective-permute-done.20 = f32[32,128]{1,0:T(8,128)S(1)} collective-permute-done((f32[32,128]{1,0:T(8,128)S(1)}, f32[32,128]{1,0:T(8,128)S(1)}, u32[]{:S(2)}, u32[]{:S(2)}) %collective-permute-start.20) | collective-permute-done | bytes 16416 | tf_op jit(solution)/shard_map/ppermute | solution.py:311
  41.3 2.4 %factor.1 = (f32[5,64,128]{2,1,0:T(8,128)}, f32[64,64]{1,0:T(8,128)}) custom-call(f32[32,128]{1,0:T(8,128)S(1)} %add.19.gram_ref, f32[5,64,128]{2,1,0:T(8,128)S(1)} %get-tuple-element.55.advanced_ref), custom_call_target="tpu_custom_call" | custom-call | tf_op jit(solution)/shard_map/factor/pallas_call | solution.py:414
  (41 shorter events, 2.1 us)
Async XLA Ops:
  0.6 0.9 %copy-start = (f32[5,64,128]{2,1,0:T(8,128)S(1)}, f32[5,64,128]{2,1,0:T(8,128)}, u32[]{:S(2)}) copy-start(f32[5,64,128]{2,1,0:T(8,128)} %q_ref.9) | copy-start | bytes 491524
  0.6 0.9 %copy-start.2 = (s32[4,16]{1,0:T(4,128)S(1)}, s32[4,16]{1,0:T(4,128)}, u32[]{:S(2)}) copy-start(s32[4,16]{1,0:T(4,128)} %send_ref.1) | copy-start | bytes 772
  1.8 6.2 %copy-start.1 = (f32[4,5,5]{2,0,1:T(4,128)S(1)}, f32[4,5,5]{2,0,1:T(4,128)}, u32[]{:S(2)}) copy-start(f32[4,5,5]{2,0,1:T(4,128)} %param.9) | copy-start | bytes 1204
  1.8 7.4 %collective-permute-start = (f32[5,8,128]{2,1,0:T(8,128)S(1)}, f32[5,8,128]{2,1,0:T(8,128)S(1)}, u32[]{:S(2)}, u32[]{:S(2)}) collective-permute-start(f32[5,8,128]{2,1,0:T(8,128)S(1)} %get-tuple-element.35), channel_id=1, source_target_pairs={{0,28},{1,29},{2,30},{3,31},{4,8},{5,9},{6,10},{7,11},{8,4},{9,5},... | collective-permute-start | bytes 61448 | tf_op jit(solution)/shard_map/ppermute | solution.py:351
  5.2 4.0 %collective-permute-start.1 = (f32[5,8,128]{2,1,0:T(8,128)S(1)}, f32[5,8,128]{2,1,0:T(8,128)S(1)}, u32[]{:S(2)}, u32[]{:S(2)}) collective-permute-start(f32[5,8,128]{2,1,0:T(8,128)S(1)} %get-tuple-element.36), channel_id=1, source_target_pairs={{0,1},{1,0},{2,3},{3,2},{4,5},{5,4},{6,7},{7,6},{8,9},{9,8},{10,11... | collective-permute-start | bytes 61448 | tf_op jit(solution)/shard_map/ppermute | solution.py:351
  6.8 2.5 %collective-permute-start.2 = (f32[5,8,128]{2,1,0:T(8,128)S(1)}, f32[5,8,128]{2,1,0:T(8,128)S(1)}, u32[]{:S(2)}, u32[]{:S(2)}) collective-permute-start(f32[5,8,128]{2,1,0:T(8,128)S(1)} %get-tuple-element.37), channel_id=1, source_target_pairs={{0,4},{1,2},{2,1},{3,7},{4,0},{5,6},{6,5},{7,3},{8,12},{9,10},{10,... | collective-permute-start | bytes 61448 | tf_op jit(solution)/shard_map/ppermute | solution.py:351
  6.8 2.5 %collective-permute-start.3 = (f32[5,8,128]{2,1,0:T(8,128)S(1)}, f32[5,8,128]{2,1,0:T(8,128)S(1)}, u32[]{:S(2)}, u32[]{:S(2)}) collective-permute-start(f32[5,8,128]{2,1,0:T(8,128)S(1)} %get-tuple-element.38), channel_id=1, source_target_pairs={{0,4},{1,5},{2,6},{3,7},{4,0},{5,1},{6,2},{7,3},{8,12},{9,13},{10,... | collective-permute-start | bytes 61448 | tf_op jit(solution)/shard_map/ppermute | solution.py:351
  8.0 0.7 %copy-start.3 = (s32[4,128]{1,0:T(4,128)S(1)}, s32[4,128]{1,0:T(4,128)}, u32[]{:S(2)}) copy-start(s32[4,128]{1,0:T(4,128)} %conn_ref.1) | copy-start | bytes 6148
  8.0 0.7 %copy-start.4 = (f32[128]{0:T(128)S(1)}, f32[128]{0:T(128)}, u32[]{:S(2)}) copy-start(f32[128]{0:T(128)} %param.10) | copy-start | bytes 1540
  8.0 0.7 %copy-start.5 = (f32[128]{0:T(128)S(1)}, f32[128]{0:T(128)}, u32[]{:S(2)}) copy-start(f32[128]{0:T(128)} %param.11) | copy-start | bytes 1540
  8.0 0.7 %copy-start.6 = (f32[128]{0:T(128)S(1)}, f32[128]{0:T(128)}, u32[]{:S(2)}) copy-start(f32[128]{0:T(128)} %param.12) | copy-start | bytes 1540
  9.8 4.3 %collective-permute-start.4 = (f32[5,8,128]{2,1,0:T(8,128)S(1)}, f32[5,8,128]{2,1,0:T(8,128)S(1)}, u32[]{:S(2)}, u32[]{:S(2)}) collective-permute-start(f32[5,8,128]{2,1,0:T(8,128)S(1)} %get-tuple-element.40), channel_id=1, source_target_pairs={{0,28},{1,29},{2,30},{3,31},{4,8},{5,9},{6,10},{7,11},{8,4},{9,5},... | collective-permute-start | bytes 61448 | tf_op jit(solution)/shard_map/ppermute | solution.py:351
  10.3 4.7 %collective-permute-start.5 = (f32[5,8,128]{2,1,0:T(8,128)S(1)}, f32[5,8,128]{2,1,0:T(8,128)S(1)}, u32[]{:S(2)}, u32[]{:S(2)}) collective-permute-start(f32[5,8,128]{2,1,0:T(8,128)S(1)} %get-tuple-element.41), channel_id=1, source_target_pairs={{0,1},{1,0},{2,3},{3,2},{4,5},{5,4},{6,7},{7,6},{8,9},{9,8},{10,11... | collective-permute-start | bytes 61448 | tf_op jit(solution)/shard_map/ppermute | solution.py:351
  13.2 1.8 %collective-permute-start.6 = (f32[5,8,128]{2,1,0:T(8,128)S(1)}, f32[5,8,128]{2,1,0:T(8,128)S(1)}, u32[]{:S(2)}, u32[]{:S(2)}) collective-permute-start(f32[5,8,128]{2,1,0:T(8,128)S(1)} %get-tuple-element.42), channel_id=1, source_target_pairs={{0,4},{1,2},{2,1},{3,7},{4,0},{5,6},{6,5},{7,3},{8,12},{9,10},{10,... | collective-permute-start | bytes 61448 | tf_op jit(solution)/shard_map/ppermute | solution.py:351
  13.2 1.8 %collective-permute-start.7 = (f32[5,8,128]{2,1,0:T(8,128)S(1)}, f32[5,8,128]{2,1,0:T(8,128)S(1)}, u32[]{:S(2)}, u32[]{:S(2)}) collective-permute-start(f32[5,8,128]{2,1,0:T(8,128)S(1)} %get-tuple-element.43), channel_id=1, source_target_pairs={{0,4},{1,5},{2,6},{3,7},{4,0},{5,1},{6,2},{7,3},{8,12},{9,13},{10,... | collective-permute-start | bytes 61448 | tf_op jit(solution)/shard_map/ppermute | solution.py:351
  15.4 4.2 %collective-permute-start.8 = (f32[5,8,128]{2,1,0:T(8,128)S(1)}, f32[5,8,128]{2,1,0:T(8,128)S(1)}, u32[]{:S(2)}, u32[]{:S(2)}) collective-permute-start(f32[5,8,128]{2,1,0:T(8,128)S(1)} %get-tuple-element.45), channel_id=1, source_target_pairs={{0,28},{1,29},{2,30},{3,31},{4,8},{5,9},{6,10},{7,11},{8,4},{9,5},... | collective-permute-start | bytes 61448 | tf_op jit(solution)/shard_map/ppermute | solution.py:351
  16.7 3.8 %collective-permute-start.9 = (f32[5,8,128]{2,1,0:T(8,128)S(1)}, f32[5,8,128]{2,1,0:T(8,128)S(1)}, u32[]{:S(2)}, u32[]{:S(2)}) collective-permute-start(f32[5,8,128]{2,1,0:T(8,128)S(1)} %get-tuple-element.46), channel_id=1, source_target_pairs={{0,1},{1,0},{2,3},{3,2},{4,5},{5,4},{6,7},{7,6},{8,9},{9,8},{10,11... | collective-permute-start | bytes 61448 | tf_op jit(solution)/shard_map/ppermute | solution.py:351
  18.8 1.8 %collective-permute-start.10 = (f32[5,8,128]{2,1,0:T(8,128)S(1)}, f32[5,8,128]{2,1,0:T(8,128)S(1)}, u32[]{:S(2)}, u32[]{:S(2)}) collective-permute-start(f32[5,8,128]{2,1,0:T(8,128)S(1)} %get-tuple-element.47), channel_id=1, source_target_pairs={{0,4},{1,2},{2,1},{3,7},{4,0},{5,6},{6,5},{7,3},{8,12},{9,10},{10,... | collective-permute-start | bytes 61448 | tf_op jit(solution)/shard_map/ppermute | solution.py:351
  18.8 1.8 %collective-permute-start.11 = (f32[5,8,128]{2,1,0:T(8,128)S(1)}, f32[5,8,128]{2,1,0:T(8,128)S(1)}, u32[]{:S(2)}, u32[]{:S(2)}) collective-permute-start(f32[5,8,128]{2,1,0:T(8,128)S(1)} %get-tuple-element.48), channel_id=1, source_target_pairs={{0,4},{1,5},{2,6},{3,7},{4,0},{5,1},{6,2},{7,3},{8,12},{9,13},{10,... | collective-permute-start | bytes 61448 | tf_op jit(solution)/shard_map/ppermute | solution.py:351
  21.0 4.2 %collective-permute-start.12 = (f32[5,8,128]{2,1,0:T(8,128)S(1)}, f32[5,8,128]{2,1,0:T(8,128)S(1)}, u32[]{:S(2)}, u32[]{:S(2)}) collective-permute-start(f32[5,8,128]{2,1,0:T(8,128)S(1)} %get-tuple-element.50), channel_id=1, source_target_pairs={{0,28},{1,29},{2,30},{3,31},{4,8},{5,9},{6,10},{7,11},{8,4},{9,5},... | collective-permute-start | bytes 61448 | tf_op jit(solution)/shard_map/ppermute | solution.py:351
  21.7 3.8 %collective-permute-start.13 = (f32[5,8,128]{2,1,0:T(8,128)S(1)}, f32[5,8,128]{2,1,0:T(8,128)S(1)}, u32[]{:S(2)}, u32[]{:S(2)}) collective-permute-start(f32[5,8,128]{2,1,0:T(8,128)S(1)} %get-tuple-element.51), channel_id=1, source_target_pairs={{0,1},{1,0},{2,3},{3,2},{4,5},{5,4},{6,7},{7,6},{8,9},{9,8},{10,11... | collective-permute-start | bytes 61448 | tf_op jit(solution)/shard_map/ppermute | solution.py:351
  23.6 1.9 %collective-permute-start.14 = (f32[5,8,128]{2,1,0:T(8,128)S(1)}, f32[5,8,128]{2,1,0:T(8,128)S(1)}, u32[]{:S(2)}, u32[]{:S(2)}) collective-permute-start(f32[5,8,128]{2,1,0:T(8,128)S(1)} %get-tuple-element.52), channel_id=1, source_target_pairs={{0,4},{1,2},{2,1},{3,7},{4,0},{5,6},{6,5},{7,3},{8,12},{9,10},{10,... | collective-permute-start | bytes 61448 | tf_op jit(solution)/shard_map/ppermute | solution.py:351
  23.6 1.9 %collective-permute-start.15 = (f32[5,8,128]{2,1,0:T(8,128)S(1)}, f32[5,8,128]{2,1,0:T(8,128)S(1)}, u32[]{:S(2)}, u32[]{:S(2)}) collective-permute-start(f32[5,8,128]{2,1,0:T(8,128)S(1)} %get-tuple-element.53), channel_id=1, source_target_pairs={{0,4},{1,5},{2,6},{3,7},{4,0},{5,1},{6,2},{7,3},{8,12},{9,13},{10,... | collective-permute-start | bytes 61448 | tf_op jit(solution)/shard_map/ppermute | solution.py:351
  26.4 1.2 %collective-permute-start.16 = (f32[32,128]{1,0:T(8,128)S(1)}, f32[32,128]{1,0:T(8,128)S(1)}, u32[]{:S(2)}, u32[]{:S(2)}) collective-permute-start(f32[32,128]{1,0:T(8,128)S(1)} %get-tuple-element.54), channel_id=1, source_target_pairs={{0,4},{1,5},{2,6},{3,7},{4,0},{5,1},{6,2},{7,3},{8,12},{9,13},{10,... | collective-permute-start | bytes 49160 | tf_op jit(solution)/shard_map/ppermute | solution.py:311
  27.6 3.2 %collective-permute-start.17 = (f32[32,128]{1,0:T(8,128)S(1)}, f32[32,128]{1,0:T(8,128)S(1)}, u32[]{:S(2)}, u32[]{:S(2)}) collective-permute-start(f32[32,128]{1,0:T(8,128)S(1)} %add.15), channel_id=1, source_target_pairs={{0,12},{1,13},{2,14},{3,15},{4,8},{5,9},{6,10},{7,11},{8,4},{9,5},... | collective-permute-start | bytes 49160 | tf_op jit(solution)/shard_map/ppermute | solution.py:311
  30.8 3.2 %collective-permute-start.18 = (f32[32,128]{1,0:T(8,128)S(1)}, f32[32,128]{1,0:T(8,128)S(1)}, u32[]{:S(2)}, u32[]{:S(2)}) collective-permute-start(f32[32,128]{1,0:T(8,128)S(1)} %add.16), channel_id=1, source_target_pairs={{0,20},{1,21},{2,22},{3,23},{4,16},{5,17},{6,18},{7,19},{8,28},{9,... | collective-permute-start | bytes 49160 | tf_op jit(solution)/shard_map/ppermute | solution.py:311
  34.0 3.2 %collective-permute-start.19 = (f32[32,128]{1,0:T(8,128)S(1)}, f32[32,128]{1,0:T(8,128)S(1)}, u32[]{:S(2)}, u32[]{:S(2)}) collective-permute-start(f32[32,128]{1,0:T(8,128)S(1)} %add.17), channel_id=1, source_target_pairs={{0,5},{1,4},{2,7},{3,6},{4,1},{5,0},{6,3},{7,2},{8,13},{9,12},{10,... | collective-permute-start | bytes 49160 | tf_op jit(solution)/shard_map/ppermute | solution.py:311
  37.2 4.1 %collective-permute-start.20 = (f32[32,128]{1,0:T(8,128)S(1)}, f32[32,128]{1,0:T(8,128)S(1)}, u32[]{:S(2)}, u32[]{:S(2)}) collective-permute-start(f32[32,128]{1,0:T(8,128)S(1)} %add.18), channel_id=1, source_target_pairs={{0,6},{1,7},{2,4},{3,5},{4,2},{5,3},{6,0},{7,1},{8,14},{9,15},{10,... | collective-permute-start | bytes 49160 | tf_op jit(solution)/shard_map/ppermute | solution.py:311

commit v6 on v5

--- a/solution.py
+++ b/solution.py
@@ -145,6 +145,13 @@
             ghost_coef_ref[rows, :] = jnp.where((owned | far)[:fields], 0.0, coef)
 
 
+def first_kernel(slots, *refs):
+    small_refs, q_ref, table_refs, part_ref = refs[:6], refs[6], refs[7:12], refs[12]
+    tables_kernel(slots, *small_refs, *table_refs)
+    centre_ref, inside_ref, _, own_coef_ref, _ = table_refs
+    own_kernel(0, centre_ref, inside_ref, own_coef_ref, q_ref, part_ref)
+
+
 def neighbours(near, coef_ref, totals, face):
     fields = len(near)
     for j in range(fields):
@@ -227,27 +234,29 @@
     shape = (sublanes, lanes)
     sub = lax.broadcasted_iota(jnp.int32, shape, 0)
     diagonal = jnp.where(lane == row, work, 0.0)
-    by_row = lax.rsqrt(jnp.sum(diagonal, axis=1, keepdims=True))
+    by_row = jnp.broadcast_to(
+        lax.rsqrt(jnp.sum(diagonal, axis=1, keepdims=True)), (vectors, lanes)
+    )
     by_lane = jnp.sum(diagonal, axis=0, keepdims=True)
     lane_root = lax.rsqrt(by_lane)
-    work = jnp.where(
-        lane < vectors,
-        work * by_row * lane_root,
-        jnp.where(lane == row + vectors, 1.0, 0.0),
-    )
-    restore = jnp.where(
-        lane[:1] < vectors, by_lane * lane_root, pltpu.roll(lane_root, vectors, 1)
-    )
-    blocks = [work[at : at + sublanes] for at in range(0, vectors, sublanes)]
+    work = jnp.where(lane < vectors, work * by_row * lane_root, 0.0)
+    blocks = []
+    for at in range(0, vectors, sublanes):
+        here = [work[at : at + sublanes]]
+        for f in range(fields):
+            here.append(advanced_ref[f, pl.ds(at, sublanes), :] * by_row[at : at + sublanes])
+        blocks.append(here)
 
     def spread(tile, k):
         return jnp.broadcast_to(tile[k : k + 1], shape)
 
+    copies = []
+    done = []
     for b in range(len(blocks)):
         start = b * sublanes
         later = range(b, len(blocks))
         columns = [
-            [lane_take(blocks[c], jnp.full(shape, start + k, jnp.int32)) for c in later]
+            [lane_take(blocks[c][0], jnp.full(shape, start + k, jnp.int32)) for c in later]
             for k in range(sublanes)
         ]
         pivots = None
@@ -258,36 +267,39 @@
             second = p * (1.0 / (p * r - q * q))
             ratio = q * first
             right = [right[c] - ratio * left[c] for c in range(len(later))]
-            top, bottom = spread(blocks[b], k), spread(blocks[b], k + 1)
-            bottom = bottom - ratio * top
-            upper, lower = top * first, bottom * second
             for n in range(k + 2, sublanes):
                 high, low = spread(columns[n][0], k), spread(columns[n][0], k + 1)
                 high, low = high * first, (low - ratio * high) * second
                 for c in range(len(later)):
                     columns[n][c] = columns[n][c] - (left[c] * high + right[c] * low)
-            for c in range(len(later)):
-                change = left[c] * upper + right[c] * lower
-                if c == 0:
-                    change = jnp.where(sub > k + 1, change, jnp.where(sub == k + 1, ratio * top, 0.0))
-                blocks[b + c] = blocks[b + c] - change
+            for t in range(1 + fields):
+                top = spread(blocks[b][t], k)
+                upper = top * first
+                lower = (spread(blocks[b][t], k + 1) - ratio * top) * second
+                for c in range(len(later)):
+                    change = left[c] * upper + right[c] * lower
+                    if c == 0:
+                        change = jnp.where(
+                            sub > k + 1, change, jnp.where(sub == k + 1, ratio * top, 0.0)
+                        )
+                    blocks[b + c][t] = blocks[b + c][t] - change
             pivots = p if pivots is None else jnp.where(sub >= k, p, pivots)
             pivots = jnp.where(sub > k, r - ratio * q, pivots)
-        blocks[b] = blocks[b] * lax.rsqrt(pivots)
-    done = jnp.concatenate(blocks, axis=0) * restore
-    factor_ref[...] = jnp.where(lane >= row, done, 0.0)[:, :vectors]
-    copies = [pltpu.make_async_copy(factor_ref, factor_hbm, sem_ref.at[fields])]
-    copies[0].start()
-    inverse_lower = pltpu.roll(done, vectors, 1)[:, :vectors]
-    for f in range(fields):
-        basis_ref[f] = jnp.dot(
-            inverse_lower,
-            advanced_ref[f],
-            precision=HIGHEST,
-            preferred_element_type=jnp.float32,
+        root = lax.rsqrt(pivots)
+        rows = pl.ds(start, sublanes)
+        done.append(blocks[b][0] * root)
+        for f in range(fields):
+            basis_ref[f, rows, :] = blocks[b][1 + f] * root
+        copies.append(
+            pltpu.make_async_copy(
+                basis_ref.at[:, rows, :], basis_hbm.at[:, rows, :], sem_ref.at[b]
+            )
         )
-        copies.append(pltpu.make_async_copy(basis_ref.at[f], basis_hbm.at[f], sem_ref.at[f]))
         copies[-1].start()
+    upper = jnp.concatenate(done, axis=0) * (by_lane * lane_root)
+    factor_ref[...] = jnp.where(lane >= row, upper, 0.0)[:, :vectors]
+    copies.append(pltpu.make_async_copy(factor_ref, factor_hbm, sem_ref.at[len(blocks)]))
+    copies[-1].start()
     for copy in copies:
         copy.wait()
 
@@ -369,11 +381,11 @@
         compiler_params=params,
         name="prepare",
     )(group, test_vectors, send_rows)
-    centre, inside, outside, own_coef, ghost_coef = pl.pallas_call(
-        functools.partial(tables_kernel, slots),
-        out_shape=tables,
-        in_specs=[vmem] * 6,
-        out_specs=[vmem] * 5,
+    centre, inside, outside, own_coef, ghost_coef, partial = pl.pallas_call(
+        functools.partial(first_kernel, slots),
+        out_shape=tables + [state],
+        in_specs=[vmem] * 7,
+        out_specs=[vmem] * 6,
         compiler_params=params,
         name="tables",
     )(
@@ -383,19 +395,21 @@
         speed,
         visc,
         volume,
+        test_vectors,
     )
     held = []
     for stage in range(4):
         last = stage == 3
         got = exchange(sent)
-        partial = pl.pallas_call(
-            functools.partial(own_kernel, stage),
-            out_shape=state,
-            in_specs=[vmem] * (4 + len(held)),
-            out_specs=vmem,
-            compiler_params=params,
-            name="own",
-        )(centre, inside, own_coef, test_vectors, *held)
+        if stage > 0:
+            partial = pl.pallas_call(
+                functools.partial(own_kernel, stage),
+                out_shape=state,
+                in_specs=[vmem] * (4 + len(held)),
+                out_specs=vmem,
+                compiler_params=params,
+                name="own",
+            )(centre, inside, own_coef, test_vectors, *held)
         gram_shape = jax.ShapeDtypeStruct((vectors // 2, lanes), jnp.float32)
         newest, *sent = pl.pallas_call(
             functools.partial(ghost_kernel, stage),
@@ -419,7 +433,7 @@
         scratch_shapes=[
             pltpu.VMEM(state.shape, jnp.float32),
             pltpu.VMEM(lower.shape, jnp.float32),
-            pltpu.SemaphoreType.DMA((fields + 1,)),
+            pltpu.SemaphoreType.DMA((vectors // sublanes + 1,)),
         ],
         compiler_params=params,
         name="factor",

time: 43.8 us -> 43.7 us (level)
    pallas_call x4 -> x3, Pallas kernels: 1.43 us -> 1.08 us  [shards(): pl.pallas_call(functools.partial(own_kernel, stage), out_shape=state, in_...]
where the time goes in v6:
time: 43.7 us; the launch traced here: 43.5 us
  starting transfers between devices  22.5 us (51%)
  waiting for transfers between devices  11.5 us (26%)
  Pallas kernels  6.39 us (15%)
  local copies, waits for them, and re-layouts  1.56 us (4%)
  between operations  1.47 us (3%)
    ppermute x16, starting transfers between devices, exchange(): got[which] = lax.ppermute(sent[which], ('gx', 'gy'), pairs[which])  16.4 us
    ppermute x5, waiting for transfers between devices, summed(): value = value + lax.ppermute(value, ('gx', 'gy'), pairs)  8.7 us
    ppermute x5, starting transfers between devices, summed(): value = value + lax.ppermute(value, ('gx', 'gy'), pairs)  6.11 us
    ppermute x16, waiting for transfers between devices, exchange(): got[which] = lax.ppermute(sent[which], ('gx', 'gy'), pairs[which])  2.8 us
    pallas_call x1, Pallas kernels, shards(): pl.pallas_call(functools.partial(factor_kernel, scale), out_shape=[state,...  2.3 us
    pallas_call x4, Pallas kernels, shards(): pl.pallas_call(functools.partial(ghost_kernel, stage), out_shape=[state,...  2.24 us
    unnamed x14, local copies, waits for them, and re-layouts  1.56 us
    pallas_call x3, Pallas kernels, shards(): pl.pallas_call(functools.partial(own_kernel, stage), out_shape=state, in_...  1.08 us
  transfers between devices with their start and end apart: 21, of which 9 were waited for; matrix products, arithmetic and copies ran while one was open for 0% of the time, Pallas kernels for 4%

profile of v6, /device:TPU:0, one launch (start us, length us, event | category | flops | bytes accessed | tf_op | source)
XLA Modules:
  0.0 43.5 jit_solution(8537625542407597052)
XLA Ops:
  0.7 0.9 %copy-done = f32[5,64,128]{2,1,0:T(8,128)S(1)} copy-done((f32[5,64,128]{2,1,0:T(8,128)S(1)}, f32[5,64,128]{2,1,0:T(8,128)}, u32[]{:S(2)}) %copy-start) | copy-done | bytes 163864
  1.8 3.4 %collective-permute-start = (f32[5,8,128]{2,1,0:T(8,128)S(1)}, f32[5,8,128]{2,1,0:T(8,128)S(1)}, u32[]{:S(2)}, u32[]{:S(2)}) collective-permute-start(f32[5,8,128]{2,1,0:T(8,128)S(1)} %get-tuple-element.37), channel_id=1, source_target_pairs={{0,28},{1,29},{2,30},{3,31},{4,8},{5,9},{6,10},{7,11},{8,4},{9,5},... | collective-permute-start | bytes 61448 | tf_op jit(solution)/shard_map/ppermute | solution.py:363
  5.2 1.6 %collective-permute-start.1 = (f32[5,8,128]{2,1,0:T(8,128)S(1)}, f32[5,8,128]{2,1,0:T(8,128)S(1)}, u32[]{:S(2)}, u32[]{:S(2)}) collective-permute-start(f32[5,8,128]{2,1,0:T(8,128)S(1)} %get-tuple-element.38), channel_id=1, source_target_pairs={{0,1},{1,0},{2,3},{3,2},{4,5},{5,4},{6,7},{7,6},{8,9},{9,8},{10,11... | collective-permute-start | bytes 61448 | tf_op jit(solution)/shard_map/ppermute | solution.py:363
  6.8 0.5 %collective-permute-start.3 = (f32[5,8,128]{2,1,0:T(8,128)S(1)}, f32[5,8,128]{2,1,0:T(8,128)S(1)}, u32[]{:S(2)}, u32[]{:S(2)}) collective-permute-start(f32[5,8,128]{2,1,0:T(8,128)S(1)} %get-tuple-element.40), channel_id=1, source_target_pairs={{0,4},{1,5},{2,6},{3,7},{4,0},{5,1},{6,2},{7,3},{8,12},{9,13},{10,... | collective-permute-start | bytes 61448 | tf_op jit(solution)/shard_map/ppermute | solution.py:363
  8.0 0.6 %copy-done.3 = s32[4,128]{1,0:T(4,128)S(1)} copy-done((s32[4,128]{1,0:T(4,128)S(1)}, s32[4,128]{1,0:T(4,128)}, u32[]{:S(2)}) %copy-start.3) | copy-done | bytes 2072
  8.7 0.5 %tables.1 = (f32[2,8,128]{2,1,0:T(8,128)S(1)}, s32[4,8,128]{2,1,0:T(8,128)S(1)}, s32[4,64,128]{2,1,0:T(8,128)S(1)}, f32[100,128]{1,0:T(8,128)S(1)}, f32[100,128]{1,0:T(8,128)S(1)}, /*index=5*/f32[5,64,128]{2,1,0:T(8,128)S(1)}) custom-call(s32[1,1]{1,0:T(1,128)} %bitcast.5.refs_0_, f32[5,4,5]{2,1,0:T(4,128)S(1)} %bitcast.6, s32[4,128]{1,0:T(4,128)S(1)} %copy-done.3, ...), custom_call_target="tpu_custom_call" | custom-call | tf_op jit(solution)/shard_map/tables/pallas_call | solution.py:384
  9.2 0.5 %ghost.4 = (f32[5,64,128]{2,1,0:T(8,128)S(1)}, f32[5,8,128]{2,1,0:T(8,128)S(1)}, f32[5,8,128]{2,1,0:T(8,128)S(1)}, f32[5,8,128]{2,1,0:T(8,128)S(1)}, f32[5,8,128]{2,1,0:T(8,128)S(1)}) custom-call(s32[4,64,128]{2,1,0:T(8,128)S(1)} %get-tuple-element.30.outside_ref, f32[100,128]{1,0:T(8,128)S(1)} %get-tuple-element.31.coef_ref, ...), custom_call_target="tpu_custom_call" | custom-call | tf_op jit(solution)/shard_map/ghost/pallas_call | solution.py:414
  9.7 0.5 %collective-permute-start.4 = (f32[5,8,128]{2,1,0:T(8,128)S(1)}, f32[5,8,128]{2,1,0:T(8,128)S(1)}, u32[]{:S(2)}, u32[]{:S(2)}) collective-permute-start(f32[5,8,128]{2,1,0:T(8,128)S(1)} %get-tuple-element.42), channel_id=1, source_target_pairs={{0,28},{1,29},{2,30},{3,31},{4,8},{5,9},{6,10},{7,11},{8,4},{9,5},... | collective-permute-start | bytes 61448 | tf_op jit(solution)/shard_map/ppermute | solution.py:363
  10.2 2.9 %collective-permute-start.5 = (f32[5,8,128]{2,1,0:T(8,128)S(1)}, f32[5,8,128]{2,1,0:T(8,128)S(1)}, u32[]{:S(2)}, u32[]{:S(2)}) collective-permute-start(f32[5,8,128]{2,1,0:T(8,128)S(1)} %get-tuple-element.43), channel_id=1, source_target_pairs={{0,1},{1,0},{2,3},{3,2},{4,5},{5,4},{6,7},{7,6},{8,9},{9,8},{10,11... | collective-permute-start | bytes 61448 | tf_op jit(solution)/shard_map/ppermute | solution.py:363
  13.1 0.5 %collective-permute-start.7 = (f32[5,8,128]{2,1,0:T(8,128)S(1)}, f32[5,8,128]{2,1,0:T(8,128)S(1)}, u32[]{:S(2)}, u32[]{:S(2)}) collective-permute-start(f32[5,8,128]{2,1,0:T(8,128)S(1)} %get-tuple-element.45), channel_id=1, source_target_pairs={{0,4},{1,5},{2,6},{3,7},{4,0},{5,1},{6,2},{7,3},{8,12},{9,13},{10,... | collective-permute-start | bytes 61448 | tf_op jit(solution)/shard_map/ppermute | solution.py:363
  14.0 0.9 %collective-permute-done.5.refs_2_ = f32[5,8,128]{2,1,0:T(8,128)S(1)} collective-permute-done((f32[5,8,128]{2,1,0:T(8,128)S(1)}, f32[5,8,128]{2,1,0:T(8,128)S(1)}, u32[]{:S(2)}, u32[]{:S(2)}) %collective-permute-start.5) | collective-permute-done | bytes 20512 | tf_op jit(solution)/shard_map/ppermute | solution.py:363
  14.9 0.4 %ghost.5 = (f32[5,64,128]{2,1,0:T(8,128)S(1)}, f32[5,8,128]{2,1,0:T(8,128)S(1)}, f32[5,8,128]{2,1,0:T(8,128)S(1)}, f32[5,8,128]{2,1,0:T(8,128)S(1)}, f32[5,8,128]{2,1,0:T(8,128)S(1)}) custom-call(s32[4,64,128]{2,1,0:T(8,128)S(1)} %get-tuple-element.30.outside_ref, f32[100,128]{1,0:T(8,128)S(1)} %get-tuple-element.31.coef_ref, ...), custom_call_target="tpu_custom_call" | custom-call | tf_op jit(solution)/shard_map/ghost/pallas_call | solution.py:414
  15.3 1.3 %collective-permute-start.8 = (f32[5,8,128]{2,1,0:T(8,128)S(1)}, f32[5,8,128]{2,1,0:T(8,128)S(1)}, u32[]{:S(2)}, u32[]{:S(2)}) collective-permute-start(f32[5,8,128]{2,1,0:T(8,128)S(1)} %get-tuple-element.47), channel_id=1, source_target_pairs={{0,28},{1,29},{2,30},{3,31},{4,8},{5,9},{6,10},{7,11},{8,4},{9,5},... | collective-permute-start | bytes 61448 | tf_op jit(solution)/shard_map/ppermute | solution.py:363
  16.6 2.1 %collective-permute-start.9 = (f32[5,8,128]{2,1,0:T(8,128)S(1)}, f32[5,8,128]{2,1,0:T(8,128)S(1)}, u32[]{:S(2)}, u32[]{:S(2)}) collective-permute-start(f32[5,8,128]{2,1,0:T(8,128)S(1)} %get-tuple-element.48), channel_id=1, source_target_pairs={{0,1},{1,0},{2,3},{3,2},{4,5},{5,4},{6,7},{7,6},{8,9},{9,8},{10,11... | collective-permute-start | bytes 61448 | tf_op jit(solution)/shard_map/ppermute | solution.py:363
  18.7 0.5 %collective-permute-start.11 = (f32[5,8,128]{2,1,0:T(8,128)S(1)}, f32[5,8,128]{2,1,0:T(8,128)S(1)}, u32[]{:S(2)}, u32[]{:S(2)}) collective-permute-start(f32[5,8,128]{2,1,0:T(8,128)S(1)} %get-tuple-element.50), channel_id=1, source_target_pairs={{0,4},{1,5},{2,6},{3,7},{4,0},{5,1},{6,2},{7,3},{8,12},{9,13},{10,... | collective-permute-start | bytes 61448 | tf_op jit(solution)/shard_map/ppermute | solution.py:363
  19.6 0.9 %collective-permute-done.9.refs_2_ = f32[5,8,128]{2,1,0:T(8,128)S(1)} collective-permute-done((f32[5,8,128]{2,1,0:T(8,128)S(1)}, f32[5,8,128]{2,1,0:T(8,128)S(1)}, u32[]{:S(2)}, u32[]{:S(2)}) %collective-permute-start.9) | collective-permute-done | bytes 20512 | tf_op jit(solution)/shard_map/ppermute | solution.py:363
  20.4 0.4 %ghost.6 = (f32[5,64,128]{2,1,0:T(8,128)S(1)}, f32[5,8,128]{2,1,0:T(8,128)S(1)}, f32[5,8,128]{2,1,0:T(8,128)S(1)}, f32[5,8,128]{2,1,0:T(8,128)S(1)}, f32[5,8,128]{2,1,0:T(8,128)S(1)}) custom-call(s32[4,64,128]{2,1,0:T(8,128)S(1)} %get-tuple-element.30.outside_ref, f32[100,128]{1,0:T(8,128)S(1)} %get-tuple-element.31.coef_ref, ...), custom_call_target="tpu_custom_call" | custom-call | tf_op jit(solution)/shard_map/ghost/pallas_call | solution.py:414
  20.9 0.8 %collective-permute-start.12 = (f32[5,8,128]{2,1,0:T(8,128)S(1)}, f32[5,8,128]{2,1,0:T(8,128)S(1)}, u32[]{:S(2)}, u32[]{:S(2)}) collective-permute-start(f32[5,8,128]{2,1,0:T(8,128)S(1)} %get-tuple-element.52), channel_id=1, source_target_pairs={{0,28},{1,29},{2,30},{3,31},{4,8},{5,9},{6,10},{7,11},{8,4},{9,5},... | collective-permute-start | bytes 61448 | tf_op jit(solution)/shard_map/ppermute | solution.py:363
  21.6 1.9 %collective-permute-start.13 = (f32[5,8,128]{2,1,0:T(8,128)S(1)}, f32[5,8,128]{2,1,0:T(8,128)S(1)}, u32[]{:S(2)}, u32[]{:S(2)}) collective-permute-start(f32[5,8,128]{2,1,0:T(8,128)S(1)} %get-tuple-element.53), channel_id=1, source_target_pairs={{0,1},{1,0},{2,3},{3,2},{4,5},{5,4},{6,7},{7,6},{8,9},{9,8},{10,11... | collective-permute-start | bytes 61448 | tf_op jit(solution)/shard_map/ppermute | solution.py:363
  23.5 0.5 %collective-permute-start.15 = (f32[5,8,128]{2,1,0:T(8,128)S(1)}, f32[5,8,128]{2,1,0:T(8,128)S(1)}, u32[]{:S(2)}, u32[]{:S(2)}) collective-permute-start(f32[5,8,128]{2,1,0:T(8,128)S(1)} %get-tuple-element.55), channel_id=1, source_target_pairs={{0,4},{1,5},{2,6},{3,7},{4,0},{5,1},{6,2},{7,3},{8,12},{9,13},{10,... | collective-permute-start | bytes 61448 | tf_op jit(solution)/shard_map/ppermute | solution.py:363
  24.4 0.7 %collective-permute-done.12.refs_1_ = f32[5,8,128]{2,1,0:T(8,128)S(1)} collective-permute-done((f32[5,8,128]{2,1,0:T(8,128)S(1)}, f32[5,8,128]{2,1,0:T(8,128)S(1)}, u32[]{:S(2)}, u32[]{:S(2)}) %collective-permute-start.12) | collective-permute-done | bytes 20512 | tf_op jit(solution)/shard_map/ppermute | solution.py:363
  25.4 0.9 %ghost.7 = (f32[5,64,128]{2,1,0:T(8,128)S(1)}, f32[32,128]{1,0:T(8,128)S(1)}) custom-call(s32[4,64,128]{2,1,0:T(8,128)S(1)} %get-tuple-element.30.outside_ref, f32[100,128]{1,0:T(8,128)S(1)} %get-tuple-element.31.coef_ref, f32[2,8,128]{2,1,0:T(8,128)S(1)} %get-tuple-element.32.centre_ref, s32[8,128]{1,0:T(8,128)S(1)} %groups.1.group_ref, ...), custom_call_target="tpu_custom_call" | custom-call | tf_op jit(solution)/shard_map/ghost/pallas_call | solution.py:414
  26.4 1.2 %collective-permute-done.16 = f32[32,128]{1,0:T(8,128)S(1)} collective-permute-done((f32[32,128]{1,0:T(8,128)S(1)}, f32[32,128]{1,0:T(8,128)S(1)}, u32[]{:S(2)}, u32[]{:S(2)}) %collective-permute-start.16) | collective-permute-done | bytes 16416 | tf_op jit(solution)/shard_map/ppermute | solution.py:323
  27.5 0.9 %collective-permute-start.17 = (f32[32,128]{1,0:T(8,128)S(1)}, f32[32,128]{1,0:T(8,128)S(1)}, u32[]{:S(2)}, u32[]{:S(2)}) collective-permute-start(f32[32,128]{1,0:T(8,128)S(1)} %add.15), channel_id=1, source_target_pairs={{0,12},{1,13},{2,14},{3,15},{4,8},{5,9},{6,10},{7,11},{8,4},{9,5},... | collective-permute-start | bytes 49160 | tf_op jit(solution)/shard_map/ppermute | solution.py:323
  28.5 2.2 %collective-permute-done.17 = f32[32,128]{1,0:T(8,128)S(1)} collective-permute-done((f32[32,128]{1,0:T(8,128)S(1)}, f32[32,128]{1,0:T(8,128)S(1)}, u32[]{:S(2)}, u32[]{:S(2)}) %collective-permute-start.17) | collective-permute-done | bytes 16416 | tf_op jit(solution)/shard_map/ppermute | solution.py:323
  30.7 0.8 %collective-permute-start.18 = (f32[32,128]{1,0:T(8,128)S(1)}, f32[32,128]{1,0:T(8,128)S(1)}, u32[]{:S(2)}, u32[]{:S(2)}) collective-permute-start(f32[32,128]{1,0:T(8,128)S(1)} %add.16), channel_id=1, source_target_pairs={{0,20},{1,21},{2,22},{3,23},{4,16},{5,17},{6,18},{7,19},{8,28},{9,... | collective-permute-start | bytes 49160 | tf_op jit(solution)/shard_map/ppermute | solution.py:323
  31.5 2.4 %collective-permute-done.18 = f32[32,128]{1,0:T(8,128)S(1)} collective-permute-done((f32[32,128]{1,0:T(8,128)S(1)}, f32[32,128]{1,0:T(8,128)S(1)}, u32[]{:S(2)}, u32[]{:S(2)}) %collective-permute-start.18) | collective-permute-done | bytes 16416 | tf_op jit(solution)/shard_map/ppermute | solution.py:323
  33.9 1.8 %collective-permute-start.19 = (f32[32,128]{1,0:T(8,128)S(1)}, f32[32,128]{1,0:T(8,128)S(1)}, u32[]{:S(2)}, u32[]{:S(2)}) collective-permute-start(f32[32,128]{1,0:T(8,128)S(1)} %add.17), channel_id=1, source_target_pairs={{0,5},{1,4},{2,7},{3,6},{4,1},{5,0},{6,3},{7,2},{8,13},{9,12},{10,... | collective-permute-start | bytes 49160 | tf_op jit(solution)/shard_map/ppermute | solution.py:323
  35.7 1.4 %collective-permute-done.19 = f32[32,128]{1,0:T(8,128)S(1)} collective-permute-done((f32[32,128]{1,0:T(8,128)S(1)}, f32[32,128]{1,0:T(8,128)S(1)}, u32[]{:S(2)}, u32[]{:S(2)}) %collective-permute-start.19) | collective-permute-done | bytes 16416 | tf_op jit(solution)/shard_map/ppermute | solution.py:323
  37.1 2.6 %collective-permute-start.20 = (f32[32,128]{1,0:T(8,128)S(1)}, f32[32,128]{1,0:T(8,128)S(1)}, u32[]{:S(2)}, u32[]{:S(2)}) collective-permute-start(f32[32,128]{1,0:T(8,128)S(1)} %add.18), channel_id=1, source_target_pairs={{0,6},{1,7},{2,4},{3,5},{4,2},{5,3},{6,0},{7,1},{8,14},{9,15},{10,... | collective-permute-start | bytes 49160 | tf_op jit(solution)/shard_map/ppermute | solution.py:323
  39.7 1.4 %collective-permute-done.20 = f32[32,128]{1,0:T(8,128)S(1)} collective-permute-done((f32[32,128]{1,0:T(8,128)S(1)}, f32[32,128]{1,0:T(8,128)S(1)}, u32[]{:S(2)}, u32[]{:S(2)}) %collective-permute-start.20) | collective-permute-done | bytes 16416 | tf_op jit(solution)/shard_map/ppermute | solution.py:323
  41.2 2.3 %factor.1 = (f32[5,64,128]{2,1,0:T(8,128)}, f32[64,64]{1,0:T(8,128)}) custom-call(f32[32,128]{1,0:T(8,128)S(1)} %add.19.gram_ref, f32[5,64,128]{2,1,0:T(8,128)S(1)} %get-tuple-element.57.advanced_ref), custom_call_target="tpu_custom_call" | custom-call | tf_op jit(solution)/shard_map/factor/pallas_call | solution.py:428
  (40 shorter events, 1.9 us)
Async XLA Ops:
  0.6 0.9 %copy-start = (f32[5,64,128]{2,1,0:T(8,128)S(1)}, f32[5,64,128]{2,1,0:T(8,128)}, u32[]{:S(2)}) copy-start(f32[5,64,128]{2,1,0:T(8,128)} %q_ref.7) | copy-start | bytes 491524
  0.6 0.9 %copy-start.2 = (s32[4,16]{1,0:T(4,128)S(1)}, s32[4,16]{1,0:T(4,128)}, u32[]{:S(2)}) copy-start(s32[4,16]{1,0:T(4,128)} %send_ref.1) | copy-start | bytes 772
  1.8 6.2 %copy-start.1 = (f32[4,5,5]{2,0,1:T(4,128)S(1)}, f32[4,5,5]{2,0,1:T(4,128)}, u32[]{:S(2)}) copy-start(f32[4,5,5]{2,0,1:T(4,128)} %param.9) | copy-start | bytes 1204
  1.8 7.4 %collective-permute-start = (f32[5,8,128]{2,1,0:T(8,128)S(1)}, f32[5,8,128]{2,1,0:T(8,128)S(1)}, u32[]{:S(2)}, u32[]{:S(2)}) collective-permute-start(f32[5,8,128]{2,1,0:T(8,128)S(1)} %get-tuple-element.37), channel_id=1, source_target_pairs={{0,28},{1,29},{2,30},{3,31},{4,8},{5,9},{6,10},{7,11},{8,4},{9,5},... | collective-permute-start | bytes 61448 | tf_op jit(solution)/shard_map/ppermute | solution.py:363
  5.2 4.0 %collective-permute-start.1 = (f32[5,8,128]{2,1,0:T(8,128)S(1)}, f32[5,8,128]{2,1,0:T(8,128)S(1)}, u32[]{:S(2)}, u32[]{:S(2)}) collective-permute-start(f32[5,8,128]{2,1,0:T(8,128)S(1)} %get-tuple-element.38), channel_id=1, source_target_pairs={{0,1},{1,0},{2,3},{3,2},{4,5},{5,4},{6,7},{7,6},{8,9},{9,8},{10,11... | collective-permute-start | bytes 61448 | tf_op jit(solution)/shard_map/ppermute | solution.py:363
  6.8 2.4 %collective-permute-start.2 = (f32[5,8,128]{2,1,0:T(8,128)S(1)}, f32[5,8,128]{2,1,0:T(8,128)S(1)}, u32[]{:S(2)}, u32[]{:S(2)}) collective-permute-start(f32[5,8,128]{2,1,0:T(8,128)S(1)} %get-tuple-element.39), channel_id=1, source_target_pairs={{0,4},{1,2},{2,1},{3,7},{4,0},{5,6},{6,5},{7,3},{8,12},{9,10},{10,... | collective-permute-start | bytes 61448 | tf_op jit(solution)/shard_map/ppermute | solution.py:363
  6.8 2.4 %collective-permute-start.3 = (f32[5,8,128]{2,1,0:T(8,128)S(1)}, f32[5,8,128]{2,1,0:T(8,128)S(1)}, u32[]{:S(2)}, u32[]{:S(2)}) collective-permute-start(f32[5,8,128]{2,1,0:T(8,128)S(1)} %get-tuple-element.40), channel_id=1, source_target_pairs={{0,4},{1,5},{2,6},{3,7},{4,0},{5,1},{6,2},{7,3},{8,12},{9,13},{10,... | collective-permute-start | bytes 61448 | tf_op jit(solution)/shard_map/ppermute | solution.py:363
  8.0 0.7 %copy-start.3 = (s32[4,128]{1,0:T(4,128)S(1)}, s32[4,128]{1,0:T(4,128)}, u32[]{:S(2)}) copy-start(s32[4,128]{1,0:T(4,128)} %refs_2_.1) | copy-start | bytes 6148
  8.0 0.7 %copy-start.4 = (f32[128]{0:T(128)S(1)}, f32[128]{0:T(128)}, u32[]{:S(2)}) copy-start(f32[128]{0:T(128)} %param.10) | copy-start | bytes 1540
  8.0 0.7 %copy-start.5 = (f32[128]{0:T(128)S(1)}, f32[128]{0:T(128)}, u32[]{:S(2)}) copy-start(f32[128]{0:T(128)} %param.11) | copy-start | bytes 1540
  8.0 0.7 %copy-start.6 = (f32[128]{0:T(128)S(1)}, f32[128]{0:T(128)}, u32[]{:S(2)}) copy-start(f32[128]{0:T(128)} %param.12) | copy-start | bytes 1540
  9.7 4.3 %collective-permute-start.4 = (f32[5,8,128]{2,1,0:T(8,128)S(1)}, f32[5,8,128]{2,1,0:T(8,128)S(1)}, u32[]{:S(2)}, u32[]{:S(2)}) collective-permute-start(f32[5,8,128]{2,1,0:T(8,128)S(1)} %get-tuple-element.42), channel_id=1, source_target_pairs={{0,28},{1,29},{2,30},{3,31},{4,8},{5,9},{6,10},{7,11},{8,4},{9,5},... | collective-permute-start | bytes 61448 | tf_op jit(solution)/shard_map/ppermute | solution.py:363
  10.2 4.7 %collective-permute-start.5 = (f32[5,8,128]{2,1,0:T(8,128)S(1)}, f32[5,8,128]{2,1,0:T(8,128)S(1)}, u32[]{:S(2)}, u32[]{:S(2)}) collective-permute-start(f32[5,8,128]{2,1,0:T(8,128)S(1)} %get-tuple-element.43), channel_id=1, source_target_pairs={{0,1},{1,0},{2,3},{3,2},{4,5},{5,4},{6,7},{7,6},{8,9},{9,8},{10,11... | collective-permute-start | bytes 61448 | tf_op jit(solution)/shard_map/ppermute | solution.py:363
  13.1 1.8 %collective-permute-start.6 = (f32[5,8,128]{2,1,0:T(8,128)S(1)}, f32[5,8,128]{2,1,0:T(8,128)S(1)}, u32[]{:S(2)}, u32[]{:S(2)}) collective-permute-start(f32[5,8,128]{2,1,0:T(8,128)S(1)} %get-tuple-element.44), channel_id=1, source_target_pairs={{0,4},{1,2},{2,1},{3,7},{4,0},{5,6},{6,5},{7,3},{8,12},{9,10},{10,... | collective-permute-start | bytes 61448 | tf_op jit(solution)/shard_map/ppermute | solution.py:363
  13.1 1.8 %collective-permute-start.7 = (f32[5,8,128]{2,1,0:T(8,128)S(1)}, f32[5,8,128]{2,1,0:T(8,128)S(1)}, u32[]{:S(2)}, u32[]{:S(2)}) collective-permute-start(f32[5,8,128]{2,1,0:T(8,128)S(1)} %get-tuple-element.45), channel_id=1, source_target_pairs={{0,4},{1,5},{2,6},{3,7},{4,0},{5,1},{6,2},{7,3},{8,12},{9,13},{10,... | collective-permute-start | bytes 61448 | tf_op jit(solution)/shard_map/ppermute | solution.py:363
  15.3 4.2 %collective-permute-start.8 = (f32[5,8,128]{2,1,0:T(8,128)S(1)}, f32[5,8,128]{2,1,0:T(8,128)S(1)}, u32[]{:S(2)}, u32[]{:S(2)}) collective-permute-start(f32[5,8,128]{2,1,0:T(8,128)S(1)} %get-tuple-element.47), channel_id=1, source_target_pairs={{0,28},{1,29},{2,30},{3,31},{4,8},{5,9},{6,10},{7,11},{8,4},{9,5},... | collective-permute-start | bytes 61448 | tf_op jit(solution)/shard_map/ppermute | solution.py:363
  16.6 3.8 %collective-permute-start.9 = (f32[5,8,128]{2,1,0:T(8,128)S(1)}, f32[5,8,128]{2,1,0:T(8,128)S(1)}, u32[]{:S(2)}, u32[]{:S(2)}) collective-permute-start(f32[5,8,128]{2,1,0:T(8,128)S(1)} %get-tuple-element.48), channel_id=1, source_target_pairs={{0,1},{1,0},{2,3},{3,2},{4,5},{5,4},{6,7},{7,6},{8,9},{9,8},{10,11... | collective-permute-start | bytes 61448 | tf_op jit(solution)/shard_map/ppermute | solution.py:363
  18.7 1.8 %collective-permute-start.10 = (f32[5,8,128]{2,1,0:T(8,128)S(1)}, f32[5,8,128]{2,1,0:T(8,128)S(1)}, u32[]{:S(2)}, u32[]{:S(2)}) collective-permute-start(f32[5,8,128]{2,1,0:T(8,128)S(1)} %get-tuple-element.49), channel_id=1, source_target_pairs={{0,4},{1,2},{2,1},{3,7},{4,0},{5,6},{6,5},{7,3},{8,12},{9,10},{10,... | collective-permute-start | bytes 61448 | tf_op jit(solution)/shard_map/ppermute | solution.py:363
  18.7 1.8 %collective-permute-start.11 = (f32[5,8,128]{2,1,0:T(8,128)S(1)}, f32[5,8,128]{2,1,0:T(8,128)S(1)}, u32[]{:S(2)}, u32[]{:S(2)}) collective-permute-start(f32[5,8,128]{2,1,0:T(8,128)S(1)} %get-tuple-element.50), channel_id=1, source_target_pairs={{0,4},{1,5},{2,6},{3,7},{4,0},{5,1},{6,2},{7,3},{8,12},{9,13},{10,... | collective-permute-start | bytes 61448 | tf_op jit(solution)/shard_map/ppermute | solution.py:363
  20.9 4.2 %collective-permute-start.12 = (f32[5,8,128]{2,1,0:T(8,128)S(1)}, f32[5,8,128]{2,1,0:T(8,128)S(1)}, u32[]{:S(2)}, u32[]{:S(2)}) collective-permute-start(f32[5,8,128]{2,1,0:T(8,128)S(1)} %get-tuple-element.52), channel_id=1, source_target_pairs={{0,28},{1,29},{2,30},{3,31},{4,8},{5,9},{6,10},{7,11},{8,4},{9,5},... | collective-permute-start | bytes 61448 | tf_op jit(solution)/shard_map/ppermute | solution.py:363
  21.6 3.8 %collective-permute-start.13 = (f32[5,8,128]{2,1,0:T(8,128)S(1)}, f32[5,8,128]{2,1,0:T(8,128)S(1)}, u32[]{:S(2)}, u32[]{:S(2)}) collective-permute-start(f32[5,8,128]{2,1,0:T(8,128)S(1)} %get-tuple-element.53), channel_id=1, source_target_pairs={{0,1},{1,0},{2,3},{3,2},{4,5},{5,4},{6,7},{7,6},{8,9},{9,8},{10,11... | collective-permute-start | bytes 61448 | tf_op jit(solution)/shard_map/ppermute | solution.py:363
  23.5 1.9 %collective-permute-start.14 = (f32[5,8,128]{2,1,0:T(8,128)S(1)}, f32[5,8,128]{2,1,0:T(8,128)S(1)}, u32[]{:S(2)}, u32[]{:S(2)}) collective-permute-start(f32[5,8,128]{2,1,0:T(8,128)S(1)} %get-tuple-element.54), channel_id=1, source_target_pairs={{0,4},{1,2},{2,1},{3,7},{4,0},{5,6},{6,5},{7,3},{8,12},{9,10},{10,... | collective-permute-start | bytes 61448 | tf_op jit(solution)/shard_map/ppermute | solution.py:363
  23.5 1.9 %collective-permute-start.15 = (f32[5,8,128]{2,1,0:T(8,128)S(1)}, f32[5,8,128]{2,1,0:T(8,128)S(1)}, u32[]{:S(2)}, u32[]{:S(2)}) collective-permute-start(f32[5,8,128]{2,1,0:T(8,128)S(1)} %get-tuple-element.55), channel_id=1, source_target_pairs={{0,4},{1,5},{2,6},{3,7},{4,0},{5,1},{6,2},{7,3},{8,12},{9,13},{10,... | collective-permute-start | bytes 61448 | tf_op jit(solution)/shard_map/ppermute | solution.py:363
  26.3 1.2 %collective-permute-start.16 = (f32[32,128]{1,0:T(8,128)S(1)}, f32[32,128]{1,0:T(8,128)S(1)}, u32[]{:S(2)}, u32[]{:S(2)}) collective-permute-start(f32[32,128]{1,0:T(8,128)S(1)} %get-tuple-element.56), channel_id=1, source_target_pairs={{0,4},{1,5},{2,6},{3,7},{4,0},{5,1},{6,2},{7,3},{8,12},{9,13},{10,... | collective-permute-start | bytes 49160 | tf_op jit(solution)/shard_map/ppermute | solution.py:323
  27.5 3.2 %collective-permute-start.17 = (f32[32,128]{1,0:T(8,128)S(1)}, f32[32,128]{1,0:T(8,128)S(1)}, u32[]{:S(2)}, u32[]{:S(2)}) collective-permute-start(f32[32,128]{1,0:T(8,128)S(1)} %add.15), channel_id=1, source_target_pairs={{0,12},{1,13},{2,14},{3,15},{4,8},{5,9},{6,10},{7,11},{8,4},{9,5},... | collective-permute-start | bytes 49160 | tf_op jit(solution)/shard_map/ppermute | solution.py:323
  30.7 3.2 %collective-permute-start.18 = (f32[32,128]{1,0:T(8,128)S(1)}, f32[32,128]{1,0:T(8,128)S(1)}, u32[]{:S(2)}, u32[]{:S(2)}) collective-permute-start(f32[32,128]{1,0:T(8,128)S(1)} %add.16), channel_id=1, source_target_pairs={{0,20},{1,21},{2,22},{3,23},{4,16},{5,17},{6,18},{7,19},{8,28},{9,... | collective-permute-start | bytes 49160 | tf_op jit(solution)/shard_map/ppermute | solution.py:323
  33.9 3.2 %collective-permute-start.19 = (f32[32,128]{1,0:T(8,128)S(1)}, f32[32,128]{1,0:T(8,128)S(1)}, u32[]{:S(2)}, u32[]{:S(2)}) collective-permute-start(f32[32,128]{1,0:T(8,128)S(1)} %add.17), channel_id=1, source_target_pairs={{0,5},{1,4},{2,7},{3,6},{4,1},{5,0},{6,3},{7,2},{8,13},{9,12},{10,... | collective-permute-start | bytes 49160 | tf_op jit(solution)/shard_map/ppermute | solution.py:323
  37.1 4.1 %collective-permute-start.20 = (f32[32,128]{1,0:T(8,128)S(1)}, f32[32,128]{1,0:T(8,128)S(1)}, u32[]{:S(2)}, u32[]{:S(2)}) collective-permute-start(f32[32,128]{1,0:T(8,128)S(1)} %add.18), channel_id=1, source_target_pairs={{0,6},{1,7},{2,4},{3,5},{4,2},{5,3},{6,0},{7,1},{8,14},{9,15},{10,... | collective-permute-start | bytes 49160 | tf_op jit(solution)/shard_map/ppermute | solution.py:323
